TPU v7x, 32 devices: a whole 2x2x4 slice. The times are simulated.
32 devices in a mesh: tower: 2 (over y), dp: 16 (over z, x, core).
Axes of the slice: x: 2, y: 2, z: 4, core: 2. Of those that a mesh axis runs over, the one named last changes fastest.
Arguments:
- hidden: bfloat16 [2, 16, 2, 1024, 768], P('tower', 'dp'), may hold values from -6 to 6
- lengths: int32 [2, 16, 2, 16], P('tower', 'dp'), may hold values from 0 to 1024, as said below
- pairs: int32 [2, 16, 16], P(None, 'dp'), may hold values from 0 to 15
- out_grad: bfloat16 [2, 16, 2, 1024, 768], P('tower', 'dp'), may hold values from -6 to 6
- w_query: bfloat16 [768, 768], P(('tower', 'dp')), may hold values from -0.21875 to 0.21875
- w_key: bfloat16 [768, 768], P(('tower', 'dp')), may hold values from -0.21875 to 0.21875
- w_value: bfloat16 [768, 768], P(('tower', 'dp')), may hold values from -0.21875 to 0.21875
- w_attn_out: bfloat16 [768, 768], P(('tower', 'dp')), may hold values from -1.75 to 1.75
- w_in: bfloat16 [768, 3072], P(('tower', 'dp')), may hold values from -0.21875 to 0.21875
- w_out: bfloat16 [3072, 768], P(('tower', 'dp')), may hold values from -0.109375 to 0.109375
- w_proj: bfloat16 [768, 768], P(('tower', 'dp')), may hold values from -0.21875 to 0.21875
- gain_attn: float32 [768], replicated, may hold values from 0.5 to 1.5
- gain_ffn: float32 [768], replicated, may hold values from 0.5 to 1.5
- gain_final: float32 [768], replicated, may hold values from 0.5 to 1.5
- rel_bias: float32 [32, 12], replicated, may hold values from -4 to 4
Outputs:
- block_out: bfloat16 [2, 16, 2, 1024, 768], P('tower', 'dp')
- hidden_grad: float32 [2, 16, 2, 1024, 768], P('tower', 'dp')
- loss: float32 [], replicated
- grad_w_query: float32 [768, 768], P(('tower', 'dp'))
- grad_w_key: float32 [768, 768], P(('tower', 'dp'))
- grad_w_value: float32 [768, 768], P(('tower', 'dp'))
- grad_w_attn_out: float32 [768, 768], P(('tower', 'dp'))
- grad_w_in: float32 [768, 3072], P(('tower', 'dp'))
- grad_w_out: float32 [3072, 768], P(('tower', 'dp'))
- grad_w_proj: float32 [768, 768], P(('tower', 'dp'))
- grad_gain_attn: float32 [768], replicated
- grad_gain_ffn: float32 [768], replicated
- grad_gain_final: float32 [768], replicated
- grad_rel_bias: float32 [32, 12], replicated
Inputs may be any that keep to these rules, and one draw needn't show every extreme that they name: lengths[0,r,m,s] is a query's length from 32 to 64 for every slot; lengths[1,r,m,0] is a document's length from 512 to 1024 and lengths[1,r,m,s] = 0 for s > 0; some query has 64 and some document 1024 rows in every draw.
All inputs are finite; a program needn't handle non-finite values.
Results may differ from a plain program's by a relative error of at most 0.015.
Values may be sent and summed in bfloat16 or wider, within the bound.
No kernel may reach another device: no remote copies, remote signals or barrier semaphores. Data moves between devices by JAX's collectives and lax.ppermute only.
A program may use at most 320 MiB of HBM per device.

v0:
```python
from functools import partial

import jax
import jax.numpy as jnp
from jax import lax
from jax.sharding import PartitionSpec as P

BLOCK = 512
MICRO = 2


bucket_steps = (12, 16, 23, 32, 46, 64, 91)
score_scale = 0.125
logit_scale = 64.0
negative = -1e30


def shortened(x):

    def short(part):
        return part.astype(jnp.bfloat16) if part.dtype == jnp.float32 else part

    return jax.tree.map(short, x)


def shifted(x, axis, by):
    peers = lax.axis_size(axis)
    pairs = [(i, i + by) for i in range(peers) if 0 <= i + by < peers]
    return lax.ppermute(x, axis, pairs)


def rms_norm(activation, gain_vec):
    return (
        activation
        * lax.rsqrt(jnp.mean(activation * activation, axis=-1, keepdims=True) + 1e-06)
        * gain_vec
    )


def unit_norm(vector):
    return vector * lax.rsqrt(jnp.sum(vector * vector, axis=-1, keepdims=True) + 1e-06)


def bucket_ids(offset):
    distance = jnp.abs(offset)
    far_bucket = jnp.full(offset.shape, 8, jnp.int32)
    for threshold in bucket_steps:
        far_bucket = far_bucket + (distance >= threshold).astype(jnp.int32)
    bucket = jnp.where(distance < 8, distance, far_bucket)
    return bucket + 16 * (offset > 0).astype(jnp.int32)


def layout(lengths_row, is_doc, row_count):
    slot_count = lengths_row.shape[0]
    spacing = row_count // slot_count
    positions = jnp.arange(row_count, dtype=jnp.int32)
    slot_starts = jnp.where(is_doc, 0, jnp.arange(slot_count, dtype=jnp.int32) * spacing)
    member = (positions[None, :] >= slot_starts[:, None]) & (
        positions[None, :] < (slot_starts + lengths_row)[:, None]
    )
    segment = jnp.where(is_doc, 0, positions // spacing)
    usable = jnp.any(member, axis=0)
    return (member, segment, usable)


def outer_sum(left, right):
    return jnp.einsum("ti,tj->ij", left, right, preferred_element_type=jnp.float32)


def per_device(
    hidden,
    lengths,
    pairs,
    out_grad,
    w_query,
    w_key,
    w_value,
    w_attn_out,
    w_in,
    w_out,
    w_proj,
    gain_attn,
    gain_ffn,
    gain_final,
    rel_bias,
):
    shards = (w_query, w_key, w_value, w_attn_out, w_in, w_out, w_proj)
    dp_count = lax.axis_size("dp")
    tower_count = lax.axis_size("tower")
    is_doc = lax.axis_index("tower") == 1
    query_side = jnp.where(is_doc, 0.0, 1.0).astype(jnp.float32)
    row_count = hidden.shape[3]
    model_width = hidden.shape[4]
    slot_count = lengths.shape[3]
    head_count = rel_bias.shape[1]
    head_size = model_width // head_count
    bucket_count = rel_bias.shape[0]
    block_total = row_count // BLOCK
    block_starts = jnp.arange(block_total, dtype=jnp.int32) * BLOCK
    bias_high = rel_bias.astype(jnp.bfloat16)
    bias_rest = (rel_bias - bias_high.astype(jnp.float32)).astype(jnp.bfloat16)
    bucket_range = jnp.arange(bucket_count, dtype=jnp.int32)
    positions = jnp.arange(row_count, dtype=jnp.int32)
    first_slot = (jnp.arange(slot_count) == 0)[:, None]

    def collect(parts):
        return (
            lax.all_gather(parts[0], ("tower", "dp"), axis=0, tiled=True),
            lax.all_gather(parts[1], ("tower", "dp"), axis=0, tiled=True),
            lax.all_gather(parts[2], ("tower", "dp"), axis=0, tiled=True),
            lax.all_gather(parts[3], ("tower", "dp"), axis=0, tiled=True),
            lax.all_gather(parts[4], ("tower", "dp"), axis=0, tiled=True),
            lax.all_gather(parts[5], ("tower", "dp"), axis=0, tiled=True),
            lax.all_gather(parts[6], ("tower", "dp"), axis=0, tiled=True),
        )

    def spread(parts):
        shaped = tuple(
            (
                piece.reshape(tower_count, piece.shape[0] // tower_count, piece.shape[1])
                for piece in parts
            )
        )
        within = lax.psum_scatter(shaped, "dp", scatter_dimension=1, tiled=True)
        across = jax.tree.map(
            lambda part: part.astype(jnp.float32),
            lax.psum_scatter(shortened(within), "tower", scatter_dimension=0, tiled=True),
        )
        return tuple((piece.reshape(piece.shape[1], piece.shape[2]) for piece in across))

    def one_batch(running, batch_item):
        grad_sums, smalls = running
        slab_rows, lengths_row, picked, cotangent = batch_item
        stream = slab_rows.astype(jnp.float32)
        member, segment, usable = layout(lengths_row, is_doc, row_count)
        weights = collect(shards)
        (
            query_weight,
            key_weight,
            value_weight,
            attn_weight,
            inner_weight,
            outer_weight,
            proj_weight,
        ) = weights
        normed_one, attn_norm_pull = jax.vjp(rms_norm, stream, gain_attn)
        attn_in = normed_one.astype(jnp.bfloat16)
        queries = (
            jnp.dot(attn_in, query_weight, preferred_element_type=jnp.float32)
            .astype(jnp.bfloat16)
            .reshape(row_count, head_count, head_size)
        )
        keys_all = (
            jnp.dot(attn_in, key_weight, preferred_element_type=jnp.float32)
            .astype(jnp.bfloat16)
            .reshape(row_count, head_count, head_size)
        )
        values_all = (
            jnp.dot(attn_in, value_weight, preferred_element_type=jnp.float32)
            .astype(jnp.bfloat16)
            .reshape(row_count, head_count, head_size)
        )

        def block_scores(begin_row):
            query_blk = lax.dynamic_slice_in_dim(queries, begin_row, BLOCK, 0)
            offset = positions[None, :] - (begin_row + jnp.arange(BLOCK, dtype=jnp.int32))[:, None]
            onehot = (bucket_ids(offset)[None] == bucket_range[:, None, None]).astype(jnp.bfloat16)
            pos_bias = jnp.einsum(
                "bij,bh->hij", onehot, bias_high, preferred_element_type=jnp.float32
            )
            pos_bias = pos_bias + jnp.einsum(
                "bij,bh->hij", onehot, bias_rest, preferred_element_type=jnp.float32
            )
            scores = (
                jnp.einsum("ihd,jhd->hij", query_blk, keys_all, preferred_element_type=jnp.float32)
                * score_scale
                + pos_bias
            )
            seg_rows = lax.dynamic_slice_in_dim(segment, begin_row, BLOCK, 0)
            allowed = (seg_rows[:, None] == segment[None, :]) & usable[None, :]
            return (query_blk, scores, allowed, onehot)

        def attend(begin_row):
            _, scores, allowed, _ = block_scores(begin_row)
            scores = jnp.where(allowed[None], scores, negative)
            row_max = jnp.max(scores, axis=-1, keepdims=True)
            raised = jnp.exp(scores - row_max)
            row_total = jnp.sum(raised, axis=-1, keepdims=True)
            attn_probs = (raised / row_total).astype(jnp.bfloat16)
            block_mix = jnp.einsum(
                "hij,jhd->ihd", attn_probs, values_all, preferred_element_type=jnp.float32
            ).astype(jnp.bfloat16)
            return (block_mix, (row_max + jnp.log(row_total))[:, :, 0])

        mixed_blocks, lse_blocks = lax.map(attend, block_starts)
        mixed_out = mixed_blocks.reshape(row_count, model_width)
        after_attn = stream + jnp.dot(mixed_out, attn_weight, preferred_element_type=jnp.float32)
        normed_two, ffn_norm_pull = jax.vjp(rms_norm, after_attn, gain_ffn)
        ffn_in = normed_two.astype(jnp.bfloat16)
        pre_act = jnp.dot(ffn_in, inner_weight, preferred_element_type=jnp.float32)
        gelu_value, gelu_pull = jax.vjp(partial(jax.nn.gelu, approximate=True), pre_act)
        activated = gelu_value.astype(jnp.bfloat16)
        block_value = after_attn + jnp.dot(
            activated, outer_weight, preferred_element_type=jnp.float32
        )
        normed_three, final_norm_pull = jax.vjp(rms_norm, block_value, gain_final)
        member_f = member.astype(jnp.float32)
        counts = jnp.maximum(jnp.sum(member_f, axis=1), 1.0)
        pool_weights = member_f / counts[:, None]
        pooled = jnp.dot(pool_weights, normed_three, precision=lax.Precision.HIGHEST).astype(
            jnp.bfloat16
        )
        projected = jnp.dot(pooled, proj_weight, preferred_element_type=jnp.float32)
        unit_vec, unit_pull = jax.vjp(unit_norm, projected)
        unit_low = unit_vec.astype(jnp.bfloat16)
        gathered = lax.all_gather(unit_low[0:1], ("tower", "dp"), axis=0, tiled=True)
        doc_embed = gathered[dp_count:]
        logits = jnp.dot(unit_low, doc_embed.T, preferred_element_type=jnp.float32) * logit_scale
        row_max = jnp.max(logits, axis=-1, keepdims=True)
        log_total = row_max + jnp.log(jnp.sum(jnp.exp(logits - row_max), axis=-1, keepdims=True))
        chosen_mask = jnp.arange(dp_count, dtype=jnp.int32)[None, :] == picked[:, None]
        chosen = jnp.sum(jnp.where(chosen_mask, logits, 0.0), axis=-1)
        loss_part = jnp.sum(log_total[:, 0] - chosen) * query_side
        logit_grad = (
            (jnp.exp(logits - log_total) - chosen_mask.astype(jnp.float32)) * query_side
        ).astype(jnp.bfloat16)
        unit_grad = jnp.dot(logit_grad, doc_embed, preferred_element_type=jnp.float32) * logit_scale
        docs_grad = (
            jnp.dot(logit_grad.T, unit_low, preferred_element_type=jnp.float32) * logit_scale
        )
        summed_docs = lax.psum_scatter(docs_grad, "dp", scatter_dimension=0, tiled=True)
        returned = shifted(summed_docs, "tower", 1)
        unit_grad = unit_grad + jnp.where(first_slot, returned, 0.0)
        proj_grad_in = unit_pull(unit_grad)[0].astype(jnp.bfloat16)
        grad_proj = outer_sum(pooled, proj_grad_in)
        pooled_grad = jnp.dot(proj_grad_in, proj_weight.T, preferred_element_type=jnp.float32)
        normed_grad = jnp.dot(pool_weights.T, pooled_grad, precision=lax.Precision.HIGHEST)
        block_grad, grad_final = final_norm_pull(normed_grad)
        block_grad = block_grad + cotangent.astype(jnp.float32)
        weights = collect(shards)
        (
            query_weight,
            key_weight,
            value_weight,
            attn_weight,
            inner_weight,
            outer_weight,
            proj_weight,
        ) = weights
        branch_grad = block_grad.astype(jnp.bfloat16)
        grad_outer = outer_sum(activated, branch_grad)
        act_grad = jnp.dot(branch_grad, outer_weight.T, preferred_element_type=jnp.float32)
        pre_grad = gelu_pull(act_grad)[0].astype(jnp.bfloat16)
        grad_inner = outer_sum(ffn_in, pre_grad)
        ffn_in_grad = jnp.dot(pre_grad, inner_weight.T, preferred_element_type=jnp.float32)
        after_grad, grad_ffn = ffn_norm_pull(ffn_in_grad)
        after_grad = after_grad + block_grad
        attn_branch_grad = after_grad.astype(jnp.bfloat16)
        grad_attn_out = outer_sum(mixed_out, attn_branch_grad)
        mixed_grad = jnp.dot(
            attn_branch_grad, attn_weight.T, preferred_element_type=jnp.float32
        ).astype(jnp.bfloat16)
        mixed_grad_blocks = mixed_grad.reshape(block_total, BLOCK, head_count, head_size)

        def attend_back(state_in, block_item):
            key_sum, value_sum, bias_sum = state_in
            begin_row, lse_blk, out_grad_blk = block_item
            query_blk, scores, allowed, onehot = block_scores(begin_row)
            probs_full = jnp.where(allowed[None], jnp.exp(scores - lse_blk[:, :, None]), 0.0)
            probs_low = probs_full.astype(jnp.bfloat16)
            value_sum = value_sum + jnp.einsum(
                "hij,ihd->jhd", probs_low, out_grad_blk, preferred_element_type=jnp.float32
            )
            prob_grad = jnp.einsum(
                "ihd,jhd->hij", out_grad_blk, values_all, preferred_element_type=jnp.float32
            )
            row_delta = jnp.sum(probs_full * prob_grad, axis=-1, keepdims=True)
            score_grad = jnp.where(allowed[None], probs_full * (prob_grad - row_delta), 0.0).astype(
                jnp.bfloat16
            )
            query_part = (
                jnp.einsum("hij,jhd->ihd", score_grad, keys_all, preferred_element_type=jnp.float32)
                * score_scale
            )
            key_sum = (
                key_sum
                + jnp.einsum(
                    "hij,ihd->jhd", score_grad, query_blk, preferred_element_type=jnp.float32
                )
                * score_scale
            )
            bias_sum = bias_sum + jnp.einsum(
                "hij,bij->bh", score_grad, onehot, preferred_element_type=jnp.float32
            )
            return ((key_sum, value_sum, bias_sum), query_part)

        zero_heads = jnp.zeros((row_count, head_count, head_size), jnp.float32)
        (key_sum, value_sum, bias_grad), query_parts = lax.scan(
            attend_back,
            (zero_heads, zero_heads, jnp.zeros((bucket_count, head_count), jnp.float32)),
            (block_starts, lse_blocks, mixed_grad_blocks),
        )
        query_grad = query_parts.reshape(row_count, model_width).astype(jnp.bfloat16)
        key_grad = key_sum.reshape(row_count, model_width).astype(jnp.bfloat16)
        value_grad = value_sum.reshape(row_count, model_width).astype(jnp.bfloat16)
        grad_query = outer_sum(attn_in, query_grad)
        grad_key = outer_sum(attn_in, key_grad)
        grad_value = outer_sum(attn_in, value_grad)
        attn_in_grad = jnp.dot(query_grad, query_weight.T, preferred_element_type=jnp.float32)
        attn_in_grad = attn_in_grad + jnp.dot(
            key_grad, key_weight.T, preferred_element_type=jnp.float32
        )
        attn_in_grad = attn_in_grad + jnp.dot(
            value_grad, value_weight.T, preferred_element_type=jnp.float32
        )
        stream_grad, grad_attn = attn_norm_pull(attn_in_grad)
        stream_grad = stream_grad + after_grad
        local_grads = (
            grad_query,
            grad_key,
            grad_value,
            grad_attn_out,
            grad_inner,
            grad_outer,
            grad_proj,
        )
        grad_sums = jax.tree.map(jnp.add, grad_sums, spread(local_grads))
        smalls = (
            smalls[0] + grad_attn,
            smalls[1] + grad_ffn,
            smalls[2] + grad_final,
            smalls[3] + bias_grad,
            smalls[4] + loss_part,
        )
        return ((grad_sums, smalls), (block_value.astype(jnp.bfloat16), stream_grad))

    start_sums = tuple((jnp.zeros(piece.shape, jnp.float32) for piece in shards))
    start_smalls = (
        jnp.zeros_like(gain_attn),
        jnp.zeros_like(gain_ffn),
        jnp.zeros_like(gain_final),
        jnp.zeros_like(rel_bias),
        jnp.zeros((), jnp.float32),
    )
    (grad_sums, smalls), (outputs, input_grads) = lax.scan(
        one_batch,
        (start_sums, start_smalls),
        (hidden[0, 0], lengths[0, 0], pairs[:, 0], out_grad[0, 0]),
    )
    totals = lax.psum((smalls[0], smalls[1], smalls[2], smalls[3], smalls[4]), ("tower", "dp"))
    loss_mean = totals[4] / (dp_count * slot_count * MICRO)
    return (
        outputs[None, None],
        input_grads[None, None],
        loss_mean,
        grad_sums[0],
        grad_sums[1],
        grad_sums[2],
        grad_sums[3],
        grad_sums[4],
        grad_sums[5],
        grad_sums[6],
        totals[0],
        totals[1],
        totals[2],
        totals[3],
    )


def solution(mesh):
    placed = (
        P("tower", "dp", None, None, None),
        P("tower", "dp", None, None),
        P(None, "dp", None),
        P("tower", "dp", None, None, None),
        P(("tower", "dp"), None),
        P(("tower", "dp"), None),
        P(("tower", "dp"), None),
        P(("tower", "dp"), None),
        P(("tower", "dp"), None),
        P(("tower", "dp"), None),
        P(("tower", "dp"), None),
        P(),
        P(),
        P(),
        P(),
    )
    return jax.shard_map(
        per_device,
        mesh=mesh,
        in_specs=placed,
        out_specs=(
            P("tower", "dp", None, None, None),
            P("tower", "dp", None, None, None),
            P(),
            P(("tower", "dp"), None),
            P(("tower", "dp"), None),
            P(("tower", "dp"), None),
            P(("tower", "dp"), None),
            P(("tower", "dp"), None),
            P(("tower", "dp"), None),
            P(("tower", "dp"), None),
            P(),
            P(),
            P(),
            P(),
        ),
        check_vma=False,
    )
```

profile of v0, /device:TPU:0, one launch (start us, length us, event | category | flops | bytes accessed | tf_op | source)
XLA Modules:
  0.0 3050.3 jit_solution(15536100501876975344)
XLA Ops:
  15.9 2985.2 %while.105 = (s32[]{:T(128)}, f32[24,768]{1,0:T(8,128)}, f32[24,768]{1,0:T(8,128)}, f32[24,768]{1,0:T(8,128)}, f32[24,768]{1,0:T(8,128)}, /*index=5*/f32[24,3072...) while((s32[]{:T(128)}, f32[24,768]{1,0:T(8,128)}, ...), condition=%wide.region_40.41_spmd.clone.clone, body=%wide.region_0.40_spmd.clone.clone.sunk | while | flops 52733739008 | bytes 1295849600 | solution.py:345
  28.1 48.6 %all-gather.16.cloned.1.call-done = bf16[768,768]{1,0:T(8,128)(2,1)} async-done(((bf16[24,768]{1,0:T(8,128)(2,1)}), bf16[768,768]{1,0:T(8,128)(2,1)}) %all-gather.16.cloned.1.call-update) | async-done | bytes 1179664 | tf_op jit(solution)/shard_map/while/body/eval_jaxpr/all_gather | solution.py:110
  79.8 52.6 %all-gather.14.cloned.1.call-done = bf16[768,768]{1,0:T(8,128)(2,1)} async-done(((bf16[24,768]{1,0:T(8,128)(2,1)}), bf16[768,768]{1,0:T(8,128)(2,1)}) %all-gather.14.cloned.1.call-update) | async-done | bytes 1179664 | tf_op jit(solution)/shard_map/while/body/eval_jaxpr/all_gather | solution.py:109
  136.8 51.5 %all-gather.12.cloned.1.call-done = bf16[768,768]{1,0:T(8,128)(2,1)} async-done(((bf16[24,768]{1,0:T(8,128)(2,1)}), bf16[768,768]{1,0:T(8,128)(2,1)}) %all-gather.12.cloned.1.call-update) | async-done | bytes 1179664 | tf_op jit(solution)/shard_map/while/body/eval_jaxpr/all_gather | solution.py:108
  192.7 229.7 %while.106 = (s32[]{:T(128)}, bf16[2,512,12,64]{1,3,2,0:T(8,128)(2,1)}, f32[2,12,512]{2,1,0:T(8,128)S(1)}, s32[2]{0:T(128)S(1)}, s32[1024]{0:T(1024)S(1)}, /*ind...) while((s32[]{:T(128)}, ...), condition=%wide.region_6.6_spmd, body=%wide.region_3.5_spmd.sunk | while | flops 2528504320 | bytes 217838608 | solution.py:195
  228.5 56.4 %fusion.392 = (f32[12,512]{1,0:T(8,128)S(1)}, f32[12,512,1024]{2,1,0:T(8,128)}) fusion(f32[512,1024,12]{1,2,0:T(8,128)} %fusion.390, f32[512,1024,12]{1,2,0:T(8,128)} %fusion.391, bf16[1024,12,64]{0,2,1:T(8,128)(2,1)} %get-tuple-element.1700, bf16[1024,12,64]{0,2,1:T(8,128)(2,1)} %get-tuple-element.1699, s32[]{:T(128)S(6)} %select_n.166, ...), kind=kOutput, calls=%fused_computation.228.clone.1 | convolution fusion | flops 836757504 | bytes 95182848 | tf_op jit(solution)/shard_map/while/body/eval_jaxpr/while/body/eval_jaxpr/ihd,jhd->hij/dot_general | solution.py:175
  343.3 56.2 %fusion.392 = (f32[12,512]{1,0:T(8,128)S(1)}, f32[12,512,1024]{2,1,0:T(8,128)}) fusion(f32[512,1024,12]{1,2,0:T(8,128)} %fusion.390, f32[512,1024,12]{1,2,0:T(8,128)} %fusion.391, bf16[1024,12,64]{0,2,1:T(8,128)(2,1)} %get-tuple-element.1700, bf16[1024,12,64]{0,2,1:T(8,128)(2,1)} %get-tuple-element.1699, s32[]{:T(128)S(6)} %select_n.166, ...), kind=kOutput, calls=%fused_computation.228.clone.1 | convolution fusion | flops 836757504 | bytes 95182848 | tf_op jit(solution)/shard_map/while/body/eval_jaxpr/while/body/eval_jaxpr/ihd,jhd->hij/dot_general | solution.py:175
  460.8 39.6 %all-gather.3 = bf16[32,1,768]{2,1,0:T(2,128)(2,1)S(1)} all-gather(bf16[1,1,768]{2,1,0:T(2,128)(2,1)S(1)} %slice_bitcast_fusion.2), channel_id=1, replica_groups=mesh['tower'=2,'dp'=16] {'tower','dp'}, dimensions={0}, use_global_device_ids=true | all-gather | bytes 50688 | tf_op jit(solution)/shard_map/while/body/eval_jaxpr/all_gather | solution.py:216
  501.4 57.9 %all-reduce.3 = f32[16,768]{1,0:T(8,128)S(1)} all-reduce(f32[16,768]{1,0:T(8,128)S(1)} %convolution_multiply_fusion.4), channel_id=2, replica_groups=mesh['tower'=2,'dp'=16] {'dp'}, use_global_device_ids=true, to_apply=%region_13.13.clone | all-reduce | flops 12288 | bytes 98304 | tf_op jit(solution)/shard_map/while
  620.7 367.1 %while.107 = (s32[]{:T(128)}, f32[1024,12,64]{0,2,1:T(8,128)}, f32[1024,12,64]{0,2,1:T(8,128)}, f32[32,12]{0,1:T(8,128)S(1)}, bf16[2,512,12,64]{1,3,2,0:T(8,128)...) while((s32[]{:T(128)}, f32[1024,12,64]{0,2,1:T(8,128)}, ...), condition=%wide.region_19.19_spmd.clone, body=%wide.region_17.18_spmd.clone.sunk | while | flops 6179397632 | bytes 321750240 | solution.py:298
  677.0 53.5 %fusion.418 = f32[12,512,1024]{2,1,0:T(8,128)} fusion(f32[512,1024,12]{1,2,0:T(8,128)} %fusion.416, f32[512,1024,12]{1,2,0:T(8,128)} %fusion.417, f32[12,512]{1,0:T(8,128)S(1)} %dynamic-slice_bitcast_fusion.2, pred[512,1024]{1,0:T(8,128)(4,1)S(1)} %compare_and_fusion.5, bf16[1024,12,64]{0,2,1:T(8,128)(2,1)S(1)} %copy-done.3, ...), kind=kOutput, calls=%fused_computation.56.clone.1 | convolution fusion | flops 836763648 | bytes 95182848 | tf_op jit(solution)/shard_map/while/body/eval_jaxpr/while/body/eval_jaxpr/ihd,jhd->hij/dot_general | solution.py:175
  846.1 53.3 %fusion.418 = f32[12,512,1024]{2,1,0:T(8,128)} fusion(f32[512,1024,12]{1,2,0:T(8,128)} %fusion.416, f32[512,1024,12]{1,2,0:T(8,128)} %fusion.417, f32[12,512]{1,0:T(8,128)S(1)} %dynamic-slice_bitcast_fusion.2, pred[512,1024]{1,0:T(8,128)(4,1)S(1)} %compare_and_fusion.5, bf16[1024,12,64]{0,2,1:T(8,128)(2,1)S(1)} %copy-done.3, ...), kind=kOutput, calls=%fused_computation.56.clone.1 | convolution fusion | flops 836763648 | bytes 95182848 | tf_op jit(solution)/shard_map/while/body/eval_jaxpr/while/body/eval_jaxpr/ihd,jhd->hij/dot_general | solution.py:175
  1058.2 64.1 %reduce-scatter.23.cloned.1.call-done = f32[2,24,768]{2,1,0:T(8,128)} async-done(((f32[2,384,768]{2,1,0:T(8,128)}), f32[2,24,768]{2,1,0:T(8,128)}) %reduce-scatter.23.cloned.1.call-update) | async-done | bytes 147472 | tf_op jit(solution)/shard_map/while/body/eval_jaxpr/reduce_scatter | solution.py:124
  1123.9 64.5 %reduce-scatter.19.cloned.1.call-done = f32[2,24,768]{2,1,0:T(8,128)} async-done(((f32[2,384,768]{2,1,0:T(8,128)}), f32[2,24,768]{2,1,0:T(8,128)}) %reduce-scatter.19.cloned.1.call-update) | async-done | bytes 147472 | tf_op jit(solution)/shard_map/while/body/eval_jaxpr/reduce_scatter | solution.py:124
  1229.1 97.9 %reduce-scatter.31.cloned.1.call-done = f32[2,24,3072]{2,1,0:T(8,128)} async-done(((f32[2,384,3072]{2,1,0:T(8,128)}), f32[2,24,3072]{2,1,0:T(8,128)}) %reduce-scatter.31.cloned.1.call-update) | async-done | bytes 589840 | tf_op jit(solution)/shard_map/while/body/eval_jaxpr/reduce_scatter | solution.py:124
  1363.7 115.3 %reduce-scatter.35.cloned.1.call-done = f32[2,96,768]{2,1,0:T(8,128)} async-done(((f32[2,1536,768]{2,1,0:T(8,128)}), f32[2,96,768]{2,1,0:T(8,128)}) %reduce-scatter.35.cloned.1.call-update) | async-done | bytes 589840 | tf_op jit(solution)/shard_map/while/body/eval_jaxpr/reduce_scatter | solution.py:124
  1521.3 45.9 %all-gather.16.cloned.1.call-done = bf16[768,768]{1,0:T(8,128)(2,1)} async-done(((bf16[24,768]{1,0:T(8,128)(2,1)}), bf16[768,768]{1,0:T(8,128)(2,1)}) %all-gather.16.cloned.1.call-update) | async-done | bytes 1179664 | tf_op jit(solution)/shard_map/while/body/eval_jaxpr/all_gather | solution.py:110
  1570.4 52.6 %all-gather.14.cloned.1.call-done = bf16[768,768]{1,0:T(8,128)(2,1)} async-done(((bf16[24,768]{1,0:T(8,128)(2,1)}), bf16[768,768]{1,0:T(8,128)(2,1)}) %all-gather.14.cloned.1.call-update) | async-done | bytes 1179664 | tf_op jit(solution)/shard_map/while/body/eval_jaxpr/all_gather | solution.py:109
  1627.4 51.4 %all-gather.12.cloned.1.call-done = bf16[768,768]{1,0:T(8,128)(2,1)} async-done(((bf16[24,768]{1,0:T(8,128)(2,1)}), bf16[768,768]{1,0:T(8,128)(2,1)}) %all-gather.12.cloned.1.call-update) | async-done | bytes 1179664 | tf_op jit(solution)/shard_map/while/body/eval_jaxpr/all_gather | solution.py:108
  1683.1 229.6 %while.106 = (s32[]{:T(128)}, bf16[2,512,12,64]{1,3,2,0:T(8,128)(2,1)}, f32[2,12,512]{2,1,0:T(8,128)S(1)}, s32[2]{0:T(128)S(1)}, s32[1024]{0:T(1024)S(1)}, /*ind...) while((s32[]{:T(128)}, ...), condition=%wide.region_6.6_spmd, body=%wide.region_3.5_spmd.sunk | while | flops 2528504320 | bytes 217838608 | solution.py:195
  1718.5 56.4 %fusion.392 = (f32[12,512]{1,0:T(8,128)S(1)}, f32[12,512,1024]{2,1,0:T(8,128)}) fusion(f32[512,1024,12]{1,2,0:T(8,128)} %fusion.390, f32[512,1024,12]{1,2,0:T(8,128)} %fusion.391, bf16[1024,12,64]{0,2,1:T(8,128)(2,1)} %get-tuple-element.1700, bf16[1024,12,64]{0,2,1:T(8,128)(2,1)} %get-tuple-element.1699, s32[]{:T(128)S(6)} %select_n.166, ...), kind=kOutput, calls=%fused_computation.228.clone.1 | convolution fusion | flops 836757504 | bytes 95182848 | tf_op jit(solution)/shard_map/while/body/eval_jaxpr/while/body/eval_jaxpr/ihd,jhd->hij/dot_general | solution.py:175
  1833.3 56.2 %fusion.392 = (f32[12,512]{1,0:T(8,128)S(1)}, f32[12,512,1024]{2,1,0:T(8,128)}) fusion(f32[512,1024,12]{1,2,0:T(8,128)} %fusion.390, f32[512,1024,12]{1,2,0:T(8,128)} %fusion.391, bf16[1024,12,64]{0,2,1:T(8,128)(2,1)} %get-tuple-element.1700, bf16[1024,12,64]{0,2,1:T(8,128)(2,1)} %get-tuple-element.1699, s32[]{:T(128)S(6)} %select_n.166, ...), kind=kOutput, calls=%fused_computation.228.clone.1 | convolution fusion | flops 836757504 | bytes 95182848 | tf_op jit(solution)/shard_map/while/body/eval_jaxpr/while/body/eval_jaxpr/ihd,jhd->hij/dot_general | solution.py:175
  1951.0 39.6 %all-gather.3 = bf16[32,1,768]{2,1,0:T(2,128)(2,1)S(1)} all-gather(bf16[1,1,768]{2,1,0:T(2,128)(2,1)S(1)} %slice_bitcast_fusion.2), channel_id=1, replica_groups=mesh['tower'=2,'dp'=16] {'tower','dp'}, dimensions={0}, use_global_device_ids=true | all-gather | bytes 50688 | tf_op jit(solution)/shard_map/while/body/eval_jaxpr/all_gather | solution.py:216
  1991.6 57.9 %all-reduce.3 = f32[16,768]{1,0:T(8,128)S(1)} all-reduce(f32[16,768]{1,0:T(8,128)S(1)} %convolution_multiply_fusion.4), channel_id=2, replica_groups=mesh['tower'=2,'dp'=16] {'dp'}, use_global_device_ids=true, to_apply=%region_13.13.clone | all-reduce | flops 12288 | bytes 98304 | tf_op jit(solution)/shard_map/while
  2110.6 367.0 %while.107 = (s32[]{:T(128)}, f32[1024,12,64]{0,2,1:T(8,128)}, f32[1024,12,64]{0,2,1:T(8,128)}, f32[32,12]{0,1:T(8,128)S(1)}, bf16[2,512,12,64]{1,3,2,0:T(8,128)...) while((s32[]{:T(128)}, f32[1024,12,64]{0,2,1:T(8,128)}, ...), condition=%wide.region_19.19_spmd.clone, body=%wide.region_17.18_spmd.clone.sunk | while | flops 6179397632 | bytes 321750240 | solution.py:298
  2166.9 53.5 %fusion.418 = f32[12,512,1024]{2,1,0:T(8,128)} fusion(f32[512,1024,12]{1,2,0:T(8,128)} %fusion.416, f32[512,1024,12]{1,2,0:T(8,128)} %fusion.417, f32[12,512]{1,0:T(8,128)S(1)} %dynamic-slice_bitcast_fusion.2, pred[512,1024]{1,0:T(8,128)(4,1)S(1)} %compare_and_fusion.5, bf16[1024,12,64]{0,2,1:T(8,128)(2,1)S(1)} %copy-done.3, ...), kind=kOutput, calls=%fused_computation.56.clone.1 | convolution fusion | flops 836763648 | bytes 95182848 | tf_op jit(solution)/shard_map/while/body/eval_jaxpr/while/body/eval_jaxpr/ihd,jhd->hij/dot_general | solution.py:175
  2336.0 53.3 %fusion.418 = f32[12,512,1024]{2,1,0:T(8,128)} fusion(f32[512,1024,12]{1,2,0:T(8,128)} %fusion.416, f32[512,1024,12]{1,2,0:T(8,128)} %fusion.417, f32[12,512]{1,0:T(8,128)S(1)} %dynamic-slice_bitcast_fusion.2, pred[512,1024]{1,0:T(8,128)(4,1)S(1)} %compare_and_fusion.5, bf16[1024,12,64]{0,2,1:T(8,128)(2,1)S(1)} %copy-done.3, ...), kind=kOutput, calls=%fused_computation.56.clone.1 | convolution fusion | flops 836763648 | bytes 95182848 | tf_op jit(solution)/shard_map/while/body/eval_jaxpr/while/body/eval_jaxpr/ihd,jhd->hij/dot_general | solution.py:175
  2548.0 64.2 %reduce-scatter.23.cloned.1.call-done = f32[2,24,768]{2,1,0:T(8,128)} async-done(((f32[2,384,768]{2,1,0:T(8,128)}), f32[2,24,768]{2,1,0:T(8,128)}) %reduce-scatter.23.cloned.1.call-update) | async-done | bytes 147472 | tf_op jit(solution)/shard_map/while/body/eval_jaxpr/reduce_scatter | solution.py:124
  2613.8 64.5 %reduce-scatter.19.cloned.1.call-done = f32[2,24,768]{2,1,0:T(8,128)} async-done(((f32[2,384,768]{2,1,0:T(8,128)}), f32[2,24,768]{2,1,0:T(8,128)}) %reduce-scatter.19.cloned.1.call-update) | async-done | bytes 147472 | tf_op jit(solution)/shard_map/while/body/eval_jaxpr/reduce_scatter | solution.py:124
  2719.0 98.0 %reduce-scatter.31.cloned.1.call-done = f32[2,24,3072]{2,1,0:T(8,128)} async-done(((f32[2,384,3072]{2,1,0:T(8,128)}), f32[2,24,3072]{2,1,0:T(8,128)}) %reduce-scatter.31.cloned.1.call-update) | async-done | bytes 589840 | tf_op jit(solution)/shard_map/while/body/eval_jaxpr/reduce_scatter | solution.py:124
  2853.8 115.2 %reduce-scatter.35.cloned.1.call-done = f32[2,96,768]{2,1,0:T(8,128)} async-done(((f32[2,1536,768]{2,1,0:T(8,128)}), f32[2,96,768]{2,1,0:T(8,128)}) %reduce-scatter.35.cloned.1.call-update) | async-done | bytes 589840 | tf_op jit(solution)/shard_map/while/body/eval_jaxpr/reduce_scatter | solution.py:124
  3001.1 40.7 %all-reduce.1 = (f32[]{:T(128)}, f32[768]{0:T(1024)}, f32[768]{0:T(1024)}, f32[768]{0:T(1024)}, f32[32,12]{0,1:T(8,128)}) all-reduce(f32[]{:T(128)} %get-tuple-element.647, f32[768]{0:T(1024)} %get-tuple-element.655, f32[768]{0:T(1024)} %get-tuple-element.656, ...), channel_id=1, replica_groups=mesh['tower'=2,'dp'=16] {'tower','dp'}, use_global_device_ids=true, to_apply=%region_41.42 | all-reduce | flops 2689 | bytes 21512 | tf_op jit(solution)/shard_map/psum | solution.py:350
  (712 shorter events, 1296.1 us)
Async XLA Ops:
  18.4 408.6 %all-gather.18.cloned.1.call-start = ((), (), s32[]{:S(2)}) async-start(), calls=%async_computation.17 | async-start | bytes 1216512 | tf_op jit(solution)/shard_map/while/body/eval_jaxpr/all_gather | solution.py:111
  19.0 413.5 %all-gather.22.cloned.1.call-start = ((), (), s32[]{:S(2)}) async-start(), calls=%async_computation.19 | async-start | bytes 4866048 | tf_op jit(solution)/shard_map/while/body/eval_jaxpr/all_gather | solution.py:112
  19.6 424.0 %all-gather.20.cloned.1.call-start = ((), (), s32[]{:S(2)}) async-start(), calls=%async_computation.18 | async-start | bytes 4866048 | tf_op jit(solution)/shard_map/while/body/eval_jaxpr/all_gather | solution.py:113
  20.2 438.8 %all-gather.24.cloned.1.call-start = ((), (), s32[]{:S(2)}) async-start(), calls=%async_computation.20 | async-start | bytes 1216512 | tf_op jit(solution)/shard_map/while/body/eval_jaxpr/all_gather | solution.py:114
  20.9 984.3 %reduce-scatter.39.cloned.1.call-start = ((), (), s32[]{:S(2)}) async-start(), calls=%async_computation.33 | async-start | bytes 2506752 | tf_op jit(solution)/shard_map/while/body/eval_jaxpr/reduce_scatter | solution.py:124
  567.0 439.9 %reduce-scatter.27.cloned.1.call-start = ((), (), s32[]{:S(2)}) async-start(), calls=%async_computation.27 | async-start | bytes 2506752 | tf_op jit(solution)/shard_map/while/body/eval_jaxpr/reduce_scatter | solution.py:124
  620.7 435.9 %reduce-scatter.15.cloned.1.call-start = ((), (), s32[]{:S(2)}) async-start(), calls=%async_computation.21 | async-start | bytes 2506752 | tf_op jit(solution)/shard_map/while/body/eval_jaxpr/reduce_scatter | solution.py:124
  1000.2 188.2 %reduce-scatter.19.cloned.1.call-start = ((), (), s32[]{:S(2)}) async-start(), calls=%async_computation.23 | async-start | bytes 2506752 | tf_op jit(solution)/shard_map/while/body/eval_jaxpr/reduce_scatter | solution.py:124
  1005.2 222.2 %reduce-scatter.41.cloned.1.call-start = ((), (), s32[]{:S(2)}) async-start(), calls=%async_computation.34 | async-start | bytes 110592 | tf_op jit(solution)/shard_map/while/body/eval_jaxpr/reduce_scatter | solution.py:127
  1006.8 221.4 %reduce-scatter.29.cloned.1.call-start = ((), (), s32[]{:S(2)}) async-start(), calls=%async_computation.28 | async-start | bytes 110592 | tf_op jit(solution)/shard_map/while/body/eval_jaxpr/reduce_scatter | solution.py:127
  1008.5 318.5 %reduce-scatter.31.cloned.1.call-start = ((), (), s32[]{:S(2)}) async-start(), calls=%async_computation.29 | async-start | bytes 10027008 | tf_op jit(solution)/shard_map/while/body/eval_jaxpr/reduce_scatter | solution.py:124
  1019.2 319.6 %reduce-scatter.17.cloned.1.call-start = ((), (), s32[]{:S(2)}) async-start(), calls=%async_computation.22 | async-start | bytes 110592 | tf_op jit(solution)/shard_map/while/body/eval_jaxpr/reduce_scatter | solution.py:127
  1058.1 292.8 %reduce-scatter.25.cloned.1.call-start = ((), (), s32[]{:S(2)}) async-start(), calls=%async_computation.26 | async-start | bytes 110592 | tf_op jit(solution)/shard_map/while/body/eval_jaxpr/reduce_scatter | solution.py:127
  1123.9 239.0 %reduce-scatter.21.cloned.1.call-start = ((), (), s32[]{:S(2)}) async-start(), calls=%async_computation.24 | async-start | bytes 110592 | tf_op jit(solution)/shard_map/while/body/eval_jaxpr/reduce_scatter | solution.py:127
  1189.9 289.0 %reduce-scatter.35.cloned.1.call-start = ((), (), s32[]{:S(2)}) async-start(), calls=%async_computation.31 | async-start | bytes 10027008 | tf_op jit(solution)/shard_map/while/body/eval_jaxpr/reduce_scatter | solution.py:124
  1203.7 289.2 %reduce-scatter.33.cloned.1.call-start = ((), (), s32[]{:S(2)}) async-start(), calls=%async_computation.30 | async-start | bytes 442368 | tf_op jit(solution)/shard_map/while/body/eval_jaxpr/reduce_scatter | solution.py:127
  1511.5 405.8 %all-gather.18.cloned.1.call-start = ((), (), s32[]{:S(2)}) async-start(), calls=%async_computation.17 | async-start | bytes 1216512 | tf_op jit(solution)/shard_map/while/body/eval_jaxpr/all_gather | solution.py:111
  1512.2 410.5 %all-gather.22.cloned.1.call-start = ((), (), s32[]{:S(2)}) async-start(), calls=%async_computation.19 | async-start | bytes 4866048 | tf_op jit(solution)/shard_map/while/body/eval_jaxpr/all_gather | solution.py:112
  1512.8 421.0 %all-gather.20.cloned.1.call-start = ((), (), s32[]{:S(2)}) async-start(), calls=%async_computation.18 | async-start | bytes 4866048 | tf_op jit(solution)/shard_map/while/body/eval_jaxpr/all_gather | solution.py:113
  1513.4 435.8 %all-gather.24.cloned.1.call-start = ((), (), s32[]{:S(2)}) async-start(), calls=%async_computation.20 | async-start | bytes 1216512 | tf_op jit(solution)/shard_map/while/body/eval_jaxpr/all_gather | solution.py:114
  1514.1 981.0 %reduce-scatter.39.cloned.1.call-start = ((), (), s32[]{:S(2)}) async-start(), calls=%async_computation.33 | async-start | bytes 2506752 | tf_op jit(solution)/shard_map/while/body/eval_jaxpr/reduce_scatter | solution.py:124
  2057.0 439.8 %reduce-scatter.27.cloned.1.call-start = ((), (), s32[]{:S(2)}) async-start(), calls=%async_computation.27 | async-start | bytes 2506752 | tf_op jit(solution)/shard_map/while/body/eval_jaxpr/reduce_scatter | solution.py:124
  2110.6 435.8 %reduce-scatter.15.cloned.1.call-start = ((), (), s32[]{:S(2)}) async-start(), calls=%async_computation.21 | async-start | bytes 2506752 | tf_op jit(solution)/shard_map/while/body/eval_jaxpr/reduce_scatter | solution.py:124
  2490.1 188.2 %reduce-scatter.19.cloned.1.call-start = ((), (), s32[]{:S(2)}) async-start(), calls=%async_computation.23 | async-start | bytes 2506752 | tf_op jit(solution)/shard_map/while/body/eval_jaxpr/reduce_scatter | solution.py:124
  2495.0 222.2 %reduce-scatter.41.cloned.1.call-start = ((), (), s32[]{:S(2)}) async-start(), calls=%async_computation.34 | async-start | bytes 110592 | tf_op jit(solution)/shard_map/while/body/eval_jaxpr/reduce_scatter | solution.py:127
  2496.7 221.4 %reduce-scatter.29.cloned.1.call-start = ((), (), s32[]{:S(2)}) async-start(), calls=%async_computation.28 | async-start | bytes 110592 | tf_op jit(solution)/shard_map/while/body/eval_jaxpr/reduce_scatter | solution.py:127
  2498.3 318.6 %reduce-scatter.31.cloned.1.call-start = ((), (), s32[]{:S(2)}) async-start(), calls=%async_computation.29 | async-start | bytes 10027008 | tf_op jit(solution)/shard_map/while/body/eval_jaxpr/reduce_scatter | solution.py:124
  2509.0 319.8 %reduce-scatter.17.cloned.1.call-start = ((), (), s32[]{:S(2)}) async-start(), calls=%async_computation.22 | async-start | bytes 110592 | tf_op jit(solution)/shard_map/while/body/eval_jaxpr/reduce_scatter | solution.py:127
  2547.9 293.1 %reduce-scatter.25.cloned.1.call-start = ((), (), s32[]{:S(2)}) async-start(), calls=%async_computation.26 | async-start | bytes 110592 | tf_op jit(solution)/shard_map/while/body/eval_jaxpr/reduce_scatter | solution.py:127
  2613.7 239.3 %reduce-scatter.21.cloned.1.call-start = ((), (), s32[]{:S(2)}) async-start(), calls=%async_computation.24 | async-start | bytes 110592 | tf_op jit(solution)/shard_map/while/body/eval_jaxpr/reduce_scatter | solution.py:127
  2679.9 289.2 %reduce-scatter.35.cloned.1.call-start = ((), (), s32[]{:S(2)}) async-start(), calls=%async_computation.31 | async-start | bytes 10027008 | tf_op jit(solution)/shard_map/while/body/eval_jaxpr/reduce_scatter | solution.py:124
  2693.7 289.6 %reduce-scatter.33.cloned.1.call-start = ((), (), s32[]{:S(2)}) async-start(), calls=%async_computation.30 | async-start | bytes 442368 | tf_op jit(solution)/shard_map/while/body/eval_jaxpr/reduce_scatter | solution.py:127
  (160 other events, 7686.1 us)
Sparse Core Ops, SparseCore 0:
  19.9 56.6 all-gather.15
  79.5 52.9 all-gather.13
  135.4 52.9 all-gather.11
  191.1 52.9 all-gather.17
  246.8 62.5 all-gather.21
  312.1 62.4 all-gather.19
  377.5 52.7 all-gather.23
  567.1 61.0 reduce-scatter.38
  632.4 62.0 reduce-scatter.26
  995.5 60.9 reduce-scatter.14
  1060.3 61.9 reduce-scatter.22
  1126.4 61.9 reduce-scatter.18
  1215.6 111.3 reduce-scatter.30
  1367.5 111.3 reduce-scatter.34
  1481.1 11.7 reduce-scatter.32
  1495.1 12.0 reduce-scatter.36
  1513.1 53.9 all-gather.15
  1570.0 52.9 all-gather.13
  1625.7 52.9 all-gather.11
  1681.6 52.9 all-gather.17
  1737.3 62.5 all-gather.21
  1802.6 62.4 all-gather.19
  1868.0 52.7 all-gather.23
  2057.1 61.0 reduce-scatter.38
  2122.3 62.0 reduce-scatter.26
  2485.4 60.9 reduce-scatter.14
  2550.1 61.9 reduce-scatter.22
  2616.2 62.0 reduce-scatter.18
  2705.6 111.3 reduce-scatter.30
  2857.7 111.3 reduce-scatter.34
  2971.3 11.8 reduce-scatter.32
  2985.5 12.0 reduce-scatter.36
  (10 shorter events, 96.1 us)
where the time goes:
time: 3060 us; the launch traced here: 3050 us
  matrix products  1290 us (42%)
  waiting for transfers between devices  1190 us (39%)
  blocking collectives  236 us (8%)
  other arithmetic  134 us (4%)
  local copies, waits for them, and re-layouts  101 us (3%)
  loops' own time  77.8 us (3%)
    reduce_scatter x14, waiting for transfers between devices, spread(): within = lax.psum_scatter(shaped, 'dp', scatter_dimension=1, tiled=True)  758 us
    dot_general x8, matrix products, block_scores(): jnp.einsum('ihd,jhd->hij', query_blk, keys_all, preferred_element_type=jn...  439 us
    dot_general x8, matrix products, block_scores(): jnp.einsum('bij,bh->hij', onehot, bias_high, preferred_element_type=jnp.f...  118 us
    dot_general x8, matrix products, block_scores(): jnp.einsum('bij,bh->hij', onehot, bias_rest, preferred_element_type=jnp.f...  118 us
    while x2, blocking collectives  116 us
    reduce_scatter x14, waiting for transfers between devices, spread(): lax.psum_scatter(shortened(within), 'tower', scatter_dimension=0, tiled=T...  113 us
    sub x4, matrix products, attend_back(): prob_grad - row_delta  105 us
    all_gather x2, waiting for transfers between devices, collect(): lax.all_gather(parts[1], ('tower', 'dp'), axis=0, tiled=True)  105 us
  transfers between devices with their start and end apart: 44, of which 28 were waited for; matrix products, arithmetic and copies ran while one was open for 48% of the time, Pallas kernels for 0%

commit v1 on v0

v1 whole, which is shorter than its diff:
```python
import jax
import jax.numpy as jnp
from jax import lax
from jax.experimental import pallas as pl
from jax.experimental.pallas import tpu as pltpu
from jax.sharding import Mesh, PartitionSpec as P

bucket_steps = (12, 16, 23, 32, 46, 64, 91)
score_scale = 0.125
logit_scale = 64.0
negative = -1e30
MICRO = 2
TILE = 128
WIDE = 256
GROUP = 64

BF = jnp.bfloat16
F32 = jnp.float32
NN = (((1,), (0,)), ((), ()))
NT = (((1,), (1,)), ((), ()))
TN = (((0,), (0,)), ((), ()))
GELU_A = 0.7978845608028654
GELU_B = 0.044715


def mm(a, b, dims=NN):
    return lax.dot_general(a, b, dims, preferred_element_type=F32)


def params(megabytes):
    return pltpu.CompilerParams(vmem_limit_bytes=megabytes << 20)


def fixed(shape):
    zeros = (0,) * len(shape)
    return pl.BlockSpec(shape, lambda *_: zeros, pipeline_mode=pl.Buffered(1))


def cost(flops, data):
    return pl.CostEstimate(flops=int(flops), bytes_accessed=int(data), transcendentals=0)


def unit_norm(vector):
    return vector * lax.rsqrt(jnp.sum(vector * vector, axis=-1, keepdims=True) + 1e-06)


def bucket_ids(offset):
    distance = jnp.abs(offset)
    far_bucket = jnp.full(offset.shape, 8, jnp.int32)
    for threshold in bucket_steps:
        far_bucket = far_bucket + (distance >= threshold).astype(jnp.int32)
    bucket = jnp.where(distance < 8, distance, far_bucket)
    return bucket + 16 * (offset > 0).astype(jnp.int32)


def qkv_kernel(x_ref, gain_ref, w_ref, a1_ref, qkv_ref):
    x = x_ref[...].astype(F32)
    r = lax.rsqrt(jnp.mean(x * x, axis=-1, keepdims=True) + 1e-06)
    a1 = (x * r * gain_ref[...]).astype(BF)
    a1_ref[...] = a1
    width = a1.shape[1]
    for part in range(3):
        out = mm(a1, w_ref[:, part * width : (part + 1) * width]).astype(BF)
        if part == 0:
            out = out * BF(score_scale)
        qkv_ref[:, part * width : (part + 1) * width] = out


def project_qkv(x, gain, w):
    rows, width = x.shape
    block = 256
    return pl.pallas_call(
        qkv_kernel,
        grid=(rows // block,),
        in_specs=[
            pl.BlockSpec((block, width), lambda i: (i, 0)),
            fixed((1, width)),
            fixed(w.shape),
        ],
        out_specs=[
            pl.BlockSpec((block, width), lambda i: (i, 0)),
            pl.BlockSpec((block, 3 * width), lambda i: (i, 0)),
        ],
        out_shape=[
            jax.ShapeDtypeStruct((rows, width), BF),
            jax.ShapeDtypeStruct((rows, 3 * width), BF),
        ],
        compiler_params=params(40),
        cost_estimate=cost(6 * rows * width * width, rows * width * 10),
        name="norm_qkv",
    )(x, gain, w)


def lane_half(shape, head):
    lane = lax.broadcasted_iota(jnp.int32, shape, 1)
    return (lane // GROUP) == head


def key_extras(rows, length):
    row = lax.broadcasted_iota(jnp.int32, (rows, TILE), 0)
    col = lax.broadcasted_iota(jnp.int32, (rows, TILE), 1)
    block = row // TILE
    hit = (col - 1 == block) | (col - 1 - rows // TILE == block)
    ones = jnp.where(hit & (col > 0), 1.0, 0.0)
    return jnp.where(col == 0, jnp.where(row < length, 0.0, negative), ones).astype(BF)


def query_mask(info_ref, tile):
    row = lax.broadcasted_iota(jnp.int32, (TILE, TILE), 0)
    col = lax.broadcasted_iota(jnp.int32, (TILE, TILE), 1)
    per = TILE // GROUP
    good = jnp.zeros((TILE, TILE), jnp.bool_)
    for s in range(per):
        low = s * GROUP
        inside = (row >= low) & (row < low + info_ref[2 + tile * per + s])
        good = good | (inside & (col >= low) & (col < low + GROUP))
    return good


def attn_fwd_kernel(
    info_ref, q_ref, k_ref, v_ref, eq_ref, t_ref, o_ref, p_ref, linv_ref, s_scr, ot_scr
):
    rows = q_ref.shape[0]
    tiles = rows // TILE
    vt = v_ref[...].T

    def ones_below(head):
        return jnp.concatenate(
            [vt[head * GROUP : (head + 1) * GROUP, :], jnp.ones((16, rows), BF)], axis=0
        )

    @pl.when(info_ref[0] == 1)
    def _():
        keys = jnp.concatenate([k_ref[...], key_extras(rows, info_ref[1])], axis=1)
        for head in range(2):
            va = ones_below(head)
            masked = jnp.where(lane_half((rows, TILE), head), q_ref[...], BF(0))
            for wide in range(rows // WIDE):
                cols = slice(wide * WIDE, (wide + 1) * WIDE)
                tags = [
                    jnp.broadcast_to(eq_ref[head, qb : qb + 1, :], (TILE, TILE))
                    for qb in range(wide * WIDE // TILE, (wide + 1) * WIDE // TILE)
                ]
                qa = jnp.concatenate([masked[cols, :], jnp.concatenate(tags, axis=0)], axis=1)
                slot = (head * (rows // WIDE) + wide) % 2
                s_scr[slot] = mm(keys, qa, NT)
                for kb in range(tiles):
                    for sub in range(WIDE // TILE):
                        delta = kb - (wide * WIDE // TILE + sub)
                        if abs(delta) <= 1:
                            at = (
                                slot,
                                slice(kb * TILE, (kb + 1) * TILE),
                                slice(sub * TILE, (sub + 1) * TILE),
                            )
                            s_scr[at] = s_scr[at] + t_ref[head, delta + 1]
                top = s_scr[slot, 0:TILE, :]
                for kb in range(1, tiles):
                    top = jnp.maximum(top, s_scr[slot, kb * TILE : (kb + 1) * TILE, :])
                top = jnp.max(top, axis=0, keepdims=True)
                for kb in range(tiles):
                    at = slice(kb * TILE, (kb + 1) * TILE)
                    p_ref[head, at, cols] = jnp.exp(s_scr[slot, at, :] - top).astype(BF)
                out = mm(va, p_ref[head, :, cols])
                inv = 1.0 / out[GROUP : GROUP + 1, :]
                ot_scr[head * GROUP : (head + 1) * GROUP, cols] = out[:GROUP, :] * inv
                linv_ref[0, head : head + 1, cols] = inv

    @pl.when(info_ref[0] == 0)
    def _():
        for tile in range(tiles):
            at = slice(tile * TILE, (tile + 1) * TILE)
            good = query_mask(info_ref, tile)
            for head in range(2):
                va = ones_below(head)[:, at]
                masked = jnp.where(lane_half((TILE, TILE), head), q_ref[at, :], BF(0))
                s = mm(k_ref[at, :], masked, NT) + t_ref[head, 1]
                s = jnp.where(good, s, negative)
                top = jnp.max(s, axis=0, keepdims=True)
                p = jnp.exp(s - top).astype(BF)
                p_ref[head, at, at] = p
                out = mm(va, p)
                inv = 1.0 / out[GROUP : GROUP + 1, :]
                ot_scr[head * GROUP : (head + 1) * GROUP, at] = out[:GROUP, :] * inv
                linv_ref[0, head : head + 1, at] = inv

    o_ref[...] = ot_scr[...].T.astype(BF)


def attention(info, qkv, tags, near, heads):
    rows = qkv.shape[0]
    width = qkv.shape[1] // 3
    pairs = heads // 2
    return pl.pallas_call(
        attn_fwd_kernel,
        grid_spec=pltpu.PrefetchScalarGridSpec(
            num_scalar_prefetch=1,
            grid=(pairs,),
            in_specs=[
                pl.BlockSpec((rows, TILE), lambda i, _: (0, i)),
                pl.BlockSpec((rows, TILE), lambda i, _: (0, pairs + i)),
                pl.BlockSpec((rows, TILE), lambda i, _: (0, 2 * pairs + i)),
                pl.BlockSpec((2,) + tags.shape[1:], lambda i, _: (i, 0, 0)),
                pl.BlockSpec((2,) + near.shape[1:], lambda i, _: (i, 0, 0, 0)),
            ],
            out_specs=[
                pl.BlockSpec((rows, TILE), lambda i, _: (0, i)),
                pl.BlockSpec((2, rows, rows), lambda i, _: (i, 0, 0)),
                pl.BlockSpec((1, 2, rows), lambda i, _: (i, 0, 0)),
            ],
            scratch_shapes=[pltpu.VMEM((2, rows, WIDE), F32), pltpu.VMEM((TILE, rows), F32)],
        ),
        out_shape=[
            jax.ShapeDtypeStruct((rows, width), BF),
            jax.ShapeDtypeStruct((heads, rows, rows), BF),
            jax.ShapeDtypeStruct((pairs, 2, rows), F32),
        ],
        compiler_params=params(48),
        cost_estimate=cost(heads * rows * rows * 512, heads * rows * rows * 2),
        name="attention_forward",
    )(info, qkv, qkv, qkv, tags, near)


def attn_bwd_kernel(
    info_ref,
    q_ref,
    k_ref,
    v_ref,
    o_ref,
    do_ref,
    p_ref,
    linv_ref,
    dqkv_ref,
    near_ref,
    far_ref,
    ds_scr,
    dqt_scr,
):
    rows = q_ref.shape[0]
    tiles = rows // TILE
    col = lax.broadcasted_iota(jnp.int32, (rows, TILE), 1)
    kt = k_ref[...].T
    scale = jnp.concatenate([linv_ref[0], jnp.zeros((6, rows), F32)], axis=0).T
    d_out = do_ref[...].astype(F32)
    prod = d_out * o_ref[...].astype(F32)
    values = jnp.concatenate([v_ref[...], jnp.where(col < 2, 1.0, 0.0).astype(BF)], axis=1)

    def prepare(head):
        mine = lane_half((rows, TILE), head)
        inv = scale[:, head : head + 1]
        scaled = jnp.where(mine, d_out * inv, 0.0).astype(BF)
        shift = -jnp.sum(jnp.where(mine, prod, 0.0), axis=1, keepdims=True) * inv
        high = shift.astype(BF)
        rest = (shift - high.astype(F32)).astype(BF)
        extra = jnp.where(col == 0, high, jnp.where(col == 1, rest, BF(0)))
        masked = jnp.where(mine, q_ref[...], BF(0))
        return scaled, jnp.concatenate([scaled, extra], axis=1), masked

    @pl.when(info_ref[0] == 1)
    def _():
        block = lax.broadcasted_iota(jnp.int32, (16, rows), 1) // TILE
        place = lax.broadcasted_iota(jnp.int32, (16, rows), 0)
        marks = jnp.where(block == place, 1.0, 0.0).astype(BF)
        dk = jnp.zeros((rows, TILE), F32)
        dv = jnp.zeros((rows, TILE), F32)
        for head in range(2):
            scaled, outer, masked = prepare(head)
            ka = jnp.concatenate([kt[head * GROUP : (head + 1) * GROUP, :], marks], axis=0)
            for wide in range(rows // WIDE):
                cols = slice(wide * WIDE, (wide + 1) * WIDE)
                dp = mm(values, outer[cols, :], NT)
                ds = (p_ref[head, :, cols].astype(F32) * dp).astype(BF)
                ds_scr[head, :, cols] = ds
                out = mm(ka, ds)
                dqt_scr[head * GROUP : (head + 1) * GROUP, cols] = out[:GROUP, :] * score_scale
                far_ref[0, head, :, cols] = out[GROUP : GROUP + tiles, :]
            dv = dv + mm(p_ref[head], scaled)
            dk = dk + mm(ds_scr[head], masked)
            for delta in (-1, 0, 1):
                total = None
                for qb in range(tiles):
                    kb = qb + delta
                    if 0 <= kb < tiles:
                        part = ds_scr[
                            head, kb * TILE : (kb + 1) * TILE, qb * TILE : (qb + 1) * TILE
                        ].astype(F32)
                        total = part if total is None else total + part
                near_ref[head, delta + 1] = total
        dqkv_ref[1] = dk.astype(BF)
        dqkv_ref[2] = dv.astype(BF)

    @pl.when(info_ref[0] == 0)
    def _():
        far_ref[...] = jnp.zeros(far_ref.shape, F32)
        near_ref[...] = jnp.zeros(near_ref.shape, F32)
        for head in range(2):
            scaled, outer, masked = prepare(head)
            total = None
            for tile in range(tiles):
                at = slice(tile * TILE, (tile + 1) * TILE)
                p = p_ref[head, at, at]
                dp = mm(values[at, :], outer[at, :], NT)
                part = p.astype(F32) * dp
                ds = part.astype(BF)
                total = part if total is None else total + part
                out = mm(kt[head * GROUP : (head + 1) * GROUP, at], ds)
                dqt_scr[head * GROUP : (head + 1) * GROUP, at] = out * score_scale
                dk = mm(ds, masked[at, :])
                dv = mm(p, scaled[at, :])
                if head == 0:
                    ds_scr[0, at, 0:TILE] = dk.astype(BF)
                    ds_scr[1, at, 0:TILE] = dv.astype(BF)
                else:
                    dqkv_ref[1, at, :] = ds_scr[0, at, 0:TILE] + dk.astype(BF)
                    dqkv_ref[2, at, :] = ds_scr[1, at, 0:TILE] + dv.astype(BF)
            near_ref[head, 1] = total

    dqkv_ref[0] = dqt_scr[...].T.astype(BF)


def attention_back(info, qkv, mixed, d_mixed, probs, linv):
    rows = qkv.shape[0]
    width = qkv.shape[1] // 3
    pairs = linv.shape[0]
    heads = 2 * pairs
    tiles = rows // TILE
    return pl.pallas_call(
        attn_bwd_kernel,
        grid_spec=pltpu.PrefetchScalarGridSpec(
            num_scalar_prefetch=1,
            grid=(pairs,),
            in_specs=[
                pl.BlockSpec((rows, TILE), lambda i, _: (0, i)),
                pl.BlockSpec((rows, TILE), lambda i, _: (0, pairs + i)),
                pl.BlockSpec((rows, TILE), lambda i, _: (0, 2 * pairs + i)),
                pl.BlockSpec((rows, TILE), lambda i, _: (0, i)),
                pl.BlockSpec((rows, TILE), lambda i, _: (0, i)),
                pl.BlockSpec((2, rows, rows), lambda i, _: (i, 0, 0)),
                pl.BlockSpec((1, 2, rows), lambda i, _: (i, 0, 0)),
            ],
            out_specs=[
                pl.BlockSpec((3, rows, TILE), lambda i, _: (0, 0, i)),
                pl.BlockSpec((2, 3, TILE, TILE), lambda i, _: (i, 0, 0, 0)),
                pl.BlockSpec((1, 2, tiles, rows), lambda i, _: (i, 0, 0, 0)),
            ],
            scratch_shapes=[pltpu.VMEM((2, rows, rows), BF), pltpu.VMEM((TILE, rows), F32)],
        ),
        out_shape=[
            jax.ShapeDtypeStruct((3, rows, width), BF),
            jax.ShapeDtypeStruct((heads, 3, TILE, TILE), F32),
            jax.ShapeDtypeStruct((pairs, 2, tiles, rows), F32),
        ],
        compiler_params=params(56),
        cost_estimate=cost(heads * rows * rows * 1024, heads * rows * rows * 2),
        name="attention_backward",
    )(info, qkv, qkv, qkv, mixed, d_mixed, probs, linv)


def usable_rows(glen_ref, first, rows):
    row = lax.broadcasted_iota(jnp.int32, (rows, 1), 0)
    good = jnp.zeros((rows, 1), jnp.bool_)
    for g in range(rows // GROUP):
        low = g * GROUP
        good = good | ((row >= low) & (row < low + glen_ref[first + g]))
    return good


def ffn_fwd_kernel(
    glen_ref,
    x_ref,
    mixed_ref,
    w_ref,
    gain2_ref,
    gain3_ref,
    x1_ref,
    a2_ref,
    act_ref,
    slope_ref,
    x2_ref,
    out_ref,
    pool_ref,
):
    rows, width = x_ref.shape
    last = w_ref.shape[1] - 2 * width
    x1 = x_ref[...].astype(F32) + mm(mixed_ref[...], w_ref[:, last : last + width])
    x1_ref[...] = x1
    r = lax.rsqrt(jnp.mean(x1 * x1, axis=-1, keepdims=True) + 1e-06)
    a2 = (x1 * r * gain2_ref[...]).astype(BF)
    a2_ref[...] = a2
    total = x1
    for c in range(last // (2 * width)):
        at = slice(c * width, (c + 1) * width)
        into = 2 * c * width
        pre = mm(a2, w_ref[:, into : into + width])
        sq = pre * pre
        tanh = jnp.tanh(pre * (sq * (GELU_A * GELU_B) + GELU_A))
        half = 0.5 * tanh + 0.5
        act = pre * half
        slope = half + 2.0 * act * (1.0 - half) * (sq * (3 * GELU_A * GELU_B) + GELU_A)
        act = act.astype(BF)
        act_ref[:, at] = act
        slope_ref[:, at] = slope.astype(BF)
        total = total + mm(act, w_ref[:, into + width : into + 2 * width])
    x2_ref[...] = total
    out_ref[...] = total.astype(BF)
    r3 = lax.rsqrt(jnp.mean(total * total, axis=-1, keepdims=True) + 1e-06)
    a3 = total * r3 * gain3_ref[...]
    a3 = jnp.where(usable_rows(glen_ref, pl.program_id(0) * (rows // GROUP), rows), a3, 0.0)
    for g in range(rows // GROUP):
        pool_ref[0, g : g + 1, :] = jnp.sum(
            a3[g * GROUP : (g + 1) * GROUP, :], axis=0, keepdims=True
        )


def ffn_forward(glen, x, mixed, w_all, gain2, gain3):
    rows, width = x.shape
    ff = w_all.shape[1] // 2 - width
    block = 256
    groups = block // GROUP
    spec = pl.BlockSpec((block, width), lambda i, _: (i, 0))
    wide = pl.BlockSpec((block, ff), lambda i, _: (i, 0))
    out = pl.pallas_call(
        ffn_fwd_kernel,
        grid_spec=pltpu.PrefetchScalarGridSpec(
            num_scalar_prefetch=1,
            grid=(rows // block,),
            in_specs=[
                spec,
                spec,
                fixed(w_all.shape),
                fixed((1, width)),
                fixed((1, width)),
            ],
            out_specs=[
                spec,
                spec,
                wide,
                wide,
                spec,
                spec,
                pl.BlockSpec((1, groups, width), lambda i, _: (i, 0, 0)),
            ],
        ),
        out_shape=[
            jax.ShapeDtypeStruct((rows, width), F32),
            jax.ShapeDtypeStruct((rows, width), BF),
            jax.ShapeDtypeStruct((rows, ff), BF),
            jax.ShapeDtypeStruct((rows, ff), BF),
            jax.ShapeDtypeStruct((rows, width), F32),
            jax.ShapeDtypeStruct((rows, width), BF),
            jax.ShapeDtypeStruct((rows // block, groups, width), F32),
        ],
        compiler_params=params(56),
        cost_estimate=cost(2 * rows * width * (width + 2 * ff), rows * width * 40),
        name="ffn_forward",
    )(glen, x, mixed, w_all, gain2, gain3)
    return *out[:6], out[6].reshape(rows // GROUP, width)


def norm_back(x, gain, grad):
    r = lax.rsqrt(jnp.mean(x * x, axis=-1, keepdims=True) + 1e-06)
    hat = x * r
    d_gain = jnp.sum(grad * hat, axis=0, keepdims=True)
    d_hat = grad * gain
    dx = r * (d_hat - hat * jnp.mean(d_hat * hat, axis=-1, keepdims=True))
    return dx, d_gain


def ffn_bwd_kernel(second):
    def kernel(*refs):
        (
            glen_ref,
            x2_ref,
            cot_ref,
            dpool_ref,
            x1_ref,
            a2_ref,
            mixed_ref,
            act_ref,
            slope_ref,
            w_ref,
            gain2_ref,
            gain3_ref,
        ) = refs[:12]
        rest = refs[12:]
        if second:
            before_ref, gproj_ref = rest[:2]
            rest = rest[2:]
        (
            g_ref,
            dx1_ref,
            dmixed_ref,
            ggain_ref,
            dx2_scr,
            dy2_scr,
            da2_scr,
            dpre_scr,
        ) = rest
        rows, width = x2_ref.shape
        step = pl.program_id(0)
        last = pl.num_programs(0) - 1
        block = 256
        left, right = slice(0, width), slice(width, 2 * width)

        def put(side, value):
            if second:
                value = value + before_ref[:, side]
            g_ref[:, side] = value.astype(g_ref.dtype)

        @pl.when(step == 0)
        def _():
            gain = jnp.zeros((1, width), F32)
            for b in range(rows // block):
                at = slice(b * block, (b + 1) * block)
                per = block // GROUP
                grad = jnp.concatenate(
                    [
                        jnp.broadcast_to(dpool_ref[b * per + g : b * per + g + 1, :], (GROUP, width))
                        for g in range(per)
                    ],
                    axis=0,
                )
                grad = jnp.where(usable_rows(glen_ref, b * per, block), grad, 0.0)
                dx, d_gain = norm_back(x2_ref[at, :], gain3_ref[...], grad)
                gain = gain + d_gain
                dx = dx + cot_ref[at, :].astype(F32)
                dx2_scr[at, :] = dx
                dy2_scr[at, :] = dx.astype(BF)
            ggain_ref[1:2, :] = gain
            da2_scr[...] = jnp.zeros_like(da2_scr)

        @pl.when(step < last)
        def _():
            dact = mm(dy2_scr[...], w_ref[:, right], NT)
            dpre_scr[...] = (dact * slope_ref[...].astype(F32)).astype(BF)
            put(right, mm(act_ref[...], dy2_scr[...], TN))
            put(left, mm(a2_ref[...], dpre_scr[...], TN))
            da2_scr[...] = da2_scr[...] + mm(dpre_scr[...], w_ref[:, left], NT)

        @pl.when(step == last)
        def _():
            gain = jnp.zeros((1, width), F32)
            for b in range(rows // block):
                at = slice(b * block, (b + 1) * block)
                dx, d_gain = norm_back(x1_ref[at, :], gain2_ref[...], da2_scr[at, :])
                gain = gain + d_gain
                dx = dx + dx2_scr[at, :]
                dx1_ref[at, :] = dx
                dy2_scr[at, :] = dx.astype(BF)
            ggain_ref[0:1, :] = gain
            put(left, mm(mixed_ref[...], dy2_scr[...], TN))
            if second:
                g_ref[:, right] = gproj_ref[...]
            dmixed_ref[...] = mm(dy2_scr[...], w_ref[:, left], NT).astype(BF)

    return kernel


def ffn_backward(
    glen, x2, cot, dpool, x1, a2, mixed, act, slope, w_all, gain2, gain3, before, gproj
):
    rows, width = x2.shape
    chunks = w_all.shape[1] // (2 * width) - 1
    ff = chunks * width
    second = before is not None
    side = pl.BlockSpec((rows, width), lambda i, _: (0, jnp.minimum(i, chunks - 1)))
    part = pl.BlockSpec((width, 2 * width), lambda i, _: (0, i))
    in_specs = [
        fixed((rows, width)),
        fixed((rows, width)),
        fixed(dpool.shape),
        fixed((rows, width)),
        fixed((rows, width)),
        fixed((rows, width)),
        side,
        side,
        part,
        fixed((1, width)),
        fixed((1, width)),
    ]
    operands = [x2, cot, dpool, x1, a2, mixed, act, slope, w_all, gain2, gain3]
    if second:
        in_specs += [part, fixed((width, width))]
        operands += [before, gproj]
    return pl.pallas_call(
        ffn_bwd_kernel(second),
        grid_spec=pltpu.PrefetchScalarGridSpec(
            num_scalar_prefetch=1,
            grid=(chunks + 1,),
            in_specs=in_specs,
            out_specs=[
                part,
                fixed((rows, width)),
                fixed((rows, width)),
                fixed((2, width)),
            ],
            scratch_shapes=[
                pltpu.VMEM((rows, width), F32),
                pltpu.VMEM((rows, width), BF),
                pltpu.VMEM((rows, width), F32),
                pltpu.VMEM((rows, width), BF),
            ],
        ),
        out_shape=[
            jax.ShapeDtypeStruct(w_all.shape, BF if second else F32),
            jax.ShapeDtypeStruct((rows, width), F32),
            jax.ShapeDtypeStruct((rows, width), BF),
            jax.ShapeDtypeStruct((2, width), F32),
        ],
        compiler_params=params(60),
        cost_estimate=cost(4 * rows * width * (width + 2 * ff), rows * width * 60),
        name="ffn_backward",
    )(glen, *operands)


def qkv_weight_kernel(a1_ref, d0_ref, d1_ref, w_ref, g_ref, gain_ref):
    rows, width = d0_ref.shape[1:]
    total = mm(a1_ref[0:rows, :], d0_ref[0], TN) + mm(a1_ref[rows:, :], d1_ref[0], TN)
    g_ref[...] = total.astype(BF)
    prod = total * w_ref[...].astype(F32)
    part = prod[:, 0:TILE]
    for lane in range(1, width // TILE):
        part = part + prod[:, lane * TILE : (lane + 1) * TILE]

    @pl.when(pl.program_id(0) == 0)
    def _():
        gain_ref[...] = part

    @pl.when(pl.program_id(0) > 0)
    def _():
        gain_ref[...] = gain_ref[...] + part


def qkv_weight_grads(a1, d0, d1, w):
    rows, width = a1.shape
    one = pl.BlockSpec((1, rows // 2, width), lambda i: (i, 0, 0))
    col = pl.BlockSpec((width, width), lambda i: (0, i))
    return pl.pallas_call(
        qkv_weight_kernel,
        grid=(3,),
        in_specs=[fixed((rows, width)), one, one, col],
        out_specs=[col, fixed((width, TILE))],
        out_shape=[
            jax.ShapeDtypeStruct((width, 3 * width), BF),
            jax.ShapeDtypeStruct((width, TILE), F32),
        ],
        compiler_params=params(48),
        cost_estimate=cost(6 * rows * width * width, rows * width * 10),
        name="qkv_weight_grads",
    )(a1, d0, d1, w)


def qkv_input_kernel(x_ref, gain_ref, w_ref, d_ref, dx1_ref, out_ref):
    width = x_ref.shape[1]
    grad = mm(d_ref[0], w_ref[:, 0:width], NT)
    grad = grad + mm(d_ref[1], w_ref[:, width : 2 * width], NT)
    grad = grad + mm(d_ref[2], w_ref[:, 2 * width : 3 * width], NT)
    x = x_ref[...].astype(F32)
    r = lax.rsqrt(jnp.mean(x * x, axis=-1, keepdims=True) + 1e-06)
    hat = x * r
    d_hat = grad * gain_ref[...]
    dx = r * (d_hat - hat * jnp.mean(d_hat * hat, axis=-1, keepdims=True))
    out_ref[0] = dx + dx1_ref[...]


def qkv_input_grad(x, gain, w, d, dx1, slab, before):
    slabs, rows, width = x.shape
    block = 256
    spec = pl.BlockSpec((block, width), lambda i: (i, 0))
    in_specs = [
        pl.BlockSpec((None, block, width), lambda i: (slab, i, 0)),
        fixed((1, width)),
        fixed(w.shape),
        pl.BlockSpec((3, block, width), lambda i: (0, i, 0)),
        spec,
    ]
    operands = [x, gain, w, d, dx1]
    kernel, aliases = qkv_input_kernel, {}
    if before is not None:
        in_specs.append(pl.BlockSpec(memory_space=pl.ANY))
        operands.append(before)
        aliases = {5: 0}

        def kernel(*refs):
            qkv_input_kernel(*refs[:5], refs[6])

    return pl.pallas_call(
        kernel,
        grid=(rows // block,),
        in_specs=in_specs,
        out_specs=pl.BlockSpec((1, block, width), lambda i: (slab, i, 0)),
        out_shape=jax.ShapeDtypeStruct((slabs, rows, width), F32),
        input_output_aliases=aliases,
        compiler_params=params(40),
        cost_estimate=cost(6 * rows * width * width, rows * width * 16),
        name="qkv_input_grad",
    )(*operands)


def near_offsets():
    key = jnp.arange(TILE, dtype=jnp.int32)[None, :, None]
    query = jnp.arange(TILE, dtype=jnp.int32)[None, None, :]
    delta = jnp.arange(-1, 2, dtype=jnp.int32)[:, None, None]
    return delta * TILE + key - query


def bias_tables(rel_bias, tiles):
    buckets, heads = rel_bias.shape
    onehot = (
        bucket_ids(near_offsets()).reshape(1, -1) == jnp.arange(buckets, dtype=jnp.int32)[:, None]
    )
    near = jnp.einsum(
        "bh,bn->hn", rel_bias, onehot.astype(F32), precision=lax.Precision.HIGHEST
    ).reshape(heads, 3, TILE, TILE)
    qb = jnp.arange(tiles)[:, None]
    kb = jnp.arange(tiles)[None, :]
    left = rel_bias[buckets // 2 - 1][:, None, None]
    right = rel_bias[buckets - 1][:, None, None]
    far = jnp.where(kb >= qb + 2, right, jnp.where(kb <= qb - 2, left, 0.0))
    high = far.astype(BF)
    rest = (far - high.astype(F32)).astype(BF)
    tags = jnp.concatenate(
        [
            jnp.ones((heads, tiles, 1), BF),
            high,
            rest,
            jnp.zeros((heads, tiles, TILE - 1 - 2 * tiles), BF),
        ],
        axis=2,
    )
    return near, tags


def bias_grad(near, far, buckets):
    heads = near.shape[0]
    tiles = far.shape[2]
    onehot = (
        bucket_ids(near_offsets()).reshape(-1, 1) == jnp.arange(buckets, dtype=jnp.int32)[None, :]
    )
    grad = jnp.einsum(
        "hn,nb->bh", near.reshape(heads, -1), onehot.astype(F32), precision=lax.Precision.HIGHEST
    )
    sums = jnp.sum(far.reshape(heads, tiles, tiles, TILE), axis=3)
    kb = jnp.arange(tiles)[:, None]
    qb = jnp.arange(tiles)[None, :]
    left = jnp.sum(jnp.where(kb <= qb - 2, sums, 0.0), axis=(1, 2))
    right = jnp.sum(jnp.where(kb >= qb + 2, sums, 0.0), axis=(1, 2))
    row = jnp.arange(buckets)[:, None]
    grad = grad + jnp.where(row == buckets // 2 - 1, left[None, :], 0.0)
    return grad + jnp.where(row == buckets - 1, right[None, :], 0.0)


def swap(x, axis):
    return lax.ppermute(x, axis, [(0, 1), (1, 0)])


def both_halves(x, axis):
    first = lax.axis_index(axis) == 0
    other = swap(x, axis)
    return jnp.stack([jnp.where(first, x, other), jnp.where(first, other, x)])


def ring_gather(x, axis):
    count = lax.axis_size(axis)
    if count > 4:
        return lax.all_gather(x, axis)
    me = lax.axis_index(axis)
    out = jnp.zeros((count,) + x.shape, x.dtype)
    out = lax.dynamic_update_index_in_dim(out, x, me, 0)
    for k in range(1, count):
        part = lax.ppermute(x, axis, [(j, (j + k) % count) for j in range(count)])
        out = lax.dynamic_update_index_in_dim(out, part, (me - k) % count, 0)
    return out


def quick_gather(x):
    rows, columns = x.shape
    half = columns // 2
    cut = half // 2 // TILE * TILE
    low = lax.axis_index("core") == 0
    pair = both_halves(x, "core")
    mine = jnp.where(low, pair[..., :half], pair[..., half:])
    line = ring_gather(mine, "z")
    one = both_halves(both_halves(line[..., :cut], "x"), "tower")
    two = both_halves(both_halves(line[..., cut:], "tower"), "x")
    full = jnp.concatenate([one, jnp.swapaxes(two, 0, 1)], axis=-1)
    full = both_halves(full, "core")
    full = jnp.concatenate([full[0], full[1]], axis=-1)
    return jnp.swapaxes(full, 1, 2).reshape(-1, columns)


def give_half(x, axis, dim):
    me = lax.axis_index(axis)
    keep = lax.dynamic_index_in_dim(x, me, dim, keepdims=False)
    got = swap(lax.dynamic_index_in_dim(x, 1 - me, dim, keepdims=False), axis)
    return (keep.astype(F32) + got.astype(F32)).astype(BF)


def ring_scatter(x, axis):
    count = lax.axis_size(axis)
    if count > 4:
        return lax.psum_scatter(x, axis, scatter_dimension=0, tiled=False).astype(F32)
    me = lax.axis_index(axis)
    total = lax.dynamic_index_in_dim(x, me, 0, keepdims=False).astype(F32)
    for k in range(1, count):
        part = lax.dynamic_index_in_dim(x, (me + k) % count, 0, keepdims=False)
        part = lax.ppermute(part, axis, [(j, (j + k) % count) for j in range(count)])
        total = total + part.astype(F32)
    return total


def by_device(x):
    sizes = tuple(lax.axis_size(a) for a in ("tower", "z", "x", "core"))
    return x.reshape(sizes + (-1, x.shape[-1]))


def quick_scatter(x):
    half = x.shape[-1] // 2
    x = give_half(by_device(x), "core", 3)
    one = give_half(give_half(x[..., :half], "tower", 0), "x", 1)
    two = give_half(give_half(x[..., half:], "x", 2), "tower", 0)
    return ring_scatter(jnp.concatenate([one, two], axis=-1), "z")


def big_scatter(x):
    x = give_half(by_device(x), "core", 3)
    columns = x.shape[-1]
    x = jnp.swapaxes(x, 1, 2).reshape(-1, columns)
    x = lax.psum_scatter(x, ("tower", "x"), scatter_dimension=0, tiled=True)
    return lax.psum_scatter(x, "z", scatter_dimension=0, tiled=True).astype(F32)


def sum_everywhere(x):
    for axis in ("core", "x", "tower", "z"):
        count, step = lax.axis_size(axis), 1
        while step < count:
            x = x + lax.ppermute(x, axis, [(j, j ^ step) for j in range(count)])
            step *= 2
    return x


AXES = ("tower", "z", "x", "core")


def per_device(
    hidden,
    lengths,
    pairs,
    out_grad,
    w_query,
    w_key,
    w_value,
    w_attn_out,
    w_in,
    w_out,
    w_proj,
    gain_attn,
    gain_ffn,
    gain_final,
    rel_bias,
):
    devices = lax.axis_size(AXES)
    dp_count = devices // lax.axis_size("tower")
    is_doc = lax.axis_index("tower") == 1
    query_side = jnp.where(is_doc, 0.0, 1.0).astype(F32)
    rows, width = hidden.shape[3:]
    slots = lengths.shape[3]
    buckets, heads = rel_bias.shape
    shard, ff = w_in.shape
    chunks = ff // width
    first_slot = (jnp.arange(slots) == 0)[:, None]
    gain1, gain2, gain3 = gain_attn[None], gain_ffn[None], gain_final[None]
    x_all = hidden[0, 0].reshape(MICRO * rows, width)

    w_in = w_in.reshape(shard, devices, chunks, shard).swapaxes(1, 2).reshape(shard, ff)
    pieces = []
    for c in range(chunks):
        pieces.append(w_in[:, c * width : (c + 1) * width])
        pieces.append(w_out[c * shard : (c + 1) * shard])
    wqkv = quick_gather(jnp.concatenate([w_query, w_key, w_value], axis=1))
    w_all = lax.all_gather(
        jnp.concatenate(pieces + [w_attn_out, w_proj], axis=1), AXES, axis=0, tiled=True
    )
    w_proj_all = w_all[:, -width:]

    near_bias, tags = bias_tables(rel_bias, rows // TILE)
    a1, qkv = project_qkv(x_all, gain1, wqkv)

    slabs = []
    for m in range(MICRO):
        at = slice(m * rows, (m + 1) * rows)
        lens = lengths[0, 0, m]
        per_group = jnp.clip(lens[0] - GROUP * jnp.arange(rows // GROUP), 0, GROUP)
        glen = jnp.where(is_doc, per_group, lens).astype(jnp.int32)
        info = jnp.concatenate([jnp.stack([is_doc.astype(jnp.int32), lens[0]]), glen])
        mixed, probs, linv = attention(info, qkv[at], tags, near_bias, heads)
        x1, a2, act, slope, x2, out, pool = ffn_forward(
            glen, hidden[0, 0, m], mixed, w_all, gain2, gain3
        )
        slabs.append((glen, info, lens, mixed, probs, linv, x1, a2, act, slope, x2, out, pool))

    pool = jnp.stack([slab[-1] for slab in slabs])
    counts = jnp.maximum(lengths[0, 0].astype(F32), 1.0)[..., None]
    doc_pool = jnp.where(first_slot, jnp.sum(pool, axis=1, keepdims=True), 0.0)
    pooled = (jnp.where(is_doc, doc_pool, pool) / counts).astype(BF)
    projected = jnp.dot(
        pooled.reshape(MICRO * slots, width), w_proj_all, preferred_element_type=F32
    ).reshape(MICRO, slots, width)
    unit_vec, unit_pull = jax.vjp(unit_norm, projected)
    unit_low = unit_vec.astype(BF)
    sent = jnp.broadcast_to(unit_low[None, :, 0], (devices, MICRO, width))
    docs = lax.all_to_all(sent, AXES, 0, 0, tiled=True)[dp_count:]
    logits = (
        jnp.einsum("msd,bmd->msb", unit_low, docs, preferred_element_type=F32) * logit_scale
    )
    row_max = jnp.max(logits, axis=-1, keepdims=True)
    log_total = row_max + jnp.log(jnp.sum(jnp.exp(logits - row_max), axis=-1, keepdims=True))
    chosen_mask = jnp.arange(dp_count, dtype=jnp.int32) == pairs[:, 0, :, None]
    chosen = jnp.sum(jnp.where(chosen_mask, logits, 0.0), axis=-1)
    loss_part = jnp.sum(log_total[..., 0] - chosen) * query_side
    logit_grad = (
        (jnp.exp(logits - log_total) - chosen_mask.astype(F32)) * query_side
    ).astype(BF)
    unit_grad = (
        jnp.einsum("msb,bmd->msd", logit_grad, docs, preferred_element_type=F32) * logit_scale
    )
    docs_grad = (
        jnp.einsum("msb,msd->bmd", logit_grad, unit_low, preferred_element_type=F32) * logit_scale
    )
    back = jnp.concatenate([jnp.zeros_like(docs_grad), docs_grad], axis=0)
    returned = jnp.sum(lax.all_to_all(back, AXES, 0, 0, tiled=True)[:dp_count], axis=0)
    unit_grad = unit_grad + jnp.where(first_slot & is_doc, returned[:, None], 0.0)
    proj_grad_in = unit_pull(unit_grad)[0].astype(BF)
    flat = proj_grad_in.reshape(MICRO * slots, width)
    grad_proj = mm(pooled.reshape(MICRO * slots, width), flat, TN).astype(BF)
    dpooled = jnp.dot(flat, w_proj_all.T, preferred_element_type=F32)
    dpooled = dpooled.reshape(MICRO, slots, width) / counts
    dpool = jnp.where(is_doc, jnp.broadcast_to(dpooled[:, 0:1], dpooled.shape), dpooled)

    grads, ggains, backs = None, 0.0, []
    for m in range(MICRO):
        glen, info, lens, mixed, probs, linv, x1, a2, act, slope, x2, out, _ = slabs[m]
        grads, dx1, d_mixed, ggain = ffn_backward(
            glen,
            x2,
            out_grad[0, 0, m],
            dpool[m],
            x1,
            a2,
            mixed,
            act,
            slope,
            w_all,
            gain2,
            gain3,
            grads,
            grad_proj,
        )
        backs.append((dx1, d_mixed))
        ggains = ggains + ggain
    grad_all = big_scatter(grads)
    grad_in = jnp.concatenate(
        [grad_all[:, 2 * c * width : (2 * c + 1) * width] for c in range(chunks)], axis=1
    )
    grad_in = grad_in.reshape(shard, chunks, devices, shard).swapaxes(1, 2).reshape(shard, ff)
    grad_out = jnp.concatenate(
        [grad_all[:, (2 * c + 1) * width : (2 * c + 2) * width] for c in range(chunks)], axis=0
    )
    grad_wo = grad_all[:, 2 * ff : 2 * ff + width]
    grad_proj = grad_all[:, 2 * ff + width :]

    dqkvs, near_sum, far_sum = [], 0.0, 0.0
    for m in range(MICRO):
        glen, info, lens, mixed, probs, linv = slabs[m][:6]
        at = slice(m * rows, (m + 1) * rows)
        dqkv, near, far = attention_back(info, qkv[at], mixed, backs[m][1], probs, linv)
        dqkvs.append(dqkv)
        near_sum = near_sum + near
        far_sum = far_sum + far
    grad_bias = bias_grad(near_sum, far_sum, buckets)

    grad_qkv, gain_part = qkv_weight_grads(a1, *dqkvs, wqkv)
    grad_qkv = quick_scatter(grad_qkv)
    ggain1 = jnp.sum(gain_part, axis=1) / gain_attn
    smalls = jnp.concatenate(
        [ggain1, ggains[0], ggains[1], grad_bias.reshape(-1), loss_part[None]]
    )
    pad = -smalls.shape[0] % (8 * TILE)
    totals = sum_everywhere(jnp.pad(smalls, (0, pad)).reshape(-1, TILE)).reshape(-1)
    input_grads = None
    for m in range(MICRO):
        input_grads = qkv_input_grad(
            hidden[0, 0], gain1, wqkv, dqkvs[m], backs[m][0], m, input_grads
        )

    outputs = jnp.stack([slab[-2] for slab in slabs])
    return (
        outputs[None, None],
        input_grads[None, None],
        totals[3 * width + buckets * heads] / (dp_count * slots * MICRO),
        grad_qkv[:, :width],
        grad_qkv[:, width : 2 * width],
        grad_qkv[:, 2 * width :],
        grad_wo,
        grad_in,
        grad_out,
        grad_proj,
        totals[:width],
        totals[width : 2 * width],
        totals[2 * width : 3 * width],
        totals[3 * width : 3 * width + buckets * heads].reshape(buckets, heads),
    )


def solution(mesh):
    towers, per_tower = mesh.devices.shape
    fine = Mesh(mesh.devices.reshape(towers, per_tower // 4, 2, 2), AXES)
    dp = AXES[1:]
    rows = P(AXES, None)
    slabs = P("tower", dp, None, None, None)
    return jax.shard_map(
        per_device,
        mesh=fine,
        in_specs=(slabs, P("tower", dp, None, None), P(None, dp, None), slabs)
        + (rows,) * 7
        + (P(),) * 4,
        out_specs=(slabs, slabs, P()) + (rows,) * 7 + (P(),) * 4,
        check_vma=False,
    )
```

time: 3060 us -> 564 us (0.18)
  matrix products: 1290 us -> 12 us
  waiting for transfers between devices: 1190 us -> 83 us
  Pallas kernels: 0 us -> 256 us
  blocking collectives: 236 us -> 0 us
  other arithmetic: 134 us -> 30.1 us
  starting transfers between devices: 8.15 us -> 91.8 us
  loops' own time: 77.8 us -> 0 us
  local copies, waits for them, and re-layouts: 101 us -> 67.1 us
    dot_general x96 -> x8, matrix products: 1190 us -> 12 us  [the longest x1 3.33 us: bias_grad(): jnp.einsum('hn,nb->bh', near.reshape(heads, -1), onehot.astype(F32), prec...]
    reduce_scatter x28 -> x2, waiting for transfers between devices: 872 us -> 0.01 us  [the longest x1 0.01 us: big_scatter(): x = lax.psum_scatter(x, ('tower', 'x'), scatter_dimension=0, tiled=True)]
    all_gather x14 -> x1, waiting for transfers between devices: 303 us -> 0.01 us  [per_device(): lax.all_gather(jnp.concatenate(pieces + [w_attn_out, w_proj], axis=1), AX...]
    pallas_call x0 -> x12, Pallas kernels: none -> 256 us  [the longest x2 75.6 us: ffn_backward(): pl.pallas_call(ffn_bwd_kernel(second), grid_spec=pltpu.PrefetchScalarGrid...]
    while x2 -> x0, blocking collectives: 116 us -> none
    sub x4 -> x0, matrix products: 105 us -> none  [attend_back(): prob_grad - row_delta]
    all_gather x2 -> x0, blocking collectives: 79.2 us -> none  [one_batch(): lax.all_gather(unit_low[0:1], ('tower', 'dp'), axis=0, tiled=True)]
    another operation x5 -> x0, loops' own time: 77.8 us -> none  [the longest x2 62.2 us: one_batch(): lax.scan(attend_back, (zero_heads, zero_heads, jnp.zeros((bucket_count, h...]
  transfers between devices with their start and end apart: 44 -> 28, of which waited for: 28 -> 17; matrix products, arithmetic and copies ran while one was open for 48% -> 10% of each run, Pallas kernels for 0% -> 24%
where the time goes in v1:
time: 564 us; the launch traced here: 558 us
  Pallas kernels  256 us (45%)
  starting transfers between devices  91.8 us (16%)
  waiting for transfers between devices  83 us (15%)
  local copies, waits for them, and re-layouts  67.1 us (12%)
  other arithmetic  30.1 us (5%)
  between operations  17.9 us (3%)
  matrix products  12 us (2%)
    pallas_call x2, Pallas kernels, ffn_backward(): pl.pallas_call(ffn_bwd_kernel(second), grid_spec=pltpu.PrefetchScalarGrid...  75.6 us
    pallas_call x2, Pallas kernels, attention(): pl.pallas_call(attn_fwd_kernel, grid_spec=pltpu.PrefetchScalarGridSpec(nu...  52.3 us
    pallas_call x2, Pallas kernels, ffn_forward(): pl.pallas_call(ffn_fwd_kernel, grid_spec=pltpu.PrefetchScalarGridSpec(num...  47.1 us
    pallas_call x2, Pallas kernels, attention_back(): pl.pallas_call(attn_bwd_kernel, grid_spec=pltpu.PrefetchScalarGridSpec(nu...  45.5 us
    ppermute x5, starting transfers between devices, sum_everywhere(): x = x + lax.ppermute(x, axis, [(j, j ^ step) for j in range(count)])  44.6 us
    ppermute x12, waiting for transfers between devices, swap(): return lax.ppermute(x, axis, [(0, 1), (1, 0)])  40.5 us
    all_to_all x1, starting transfers between devices, per_device(): docs = lax.all_to_all(sent, AXES, 0, 0, tiled=True)[dp_count:]  23 us
    unnamed x131, local copies, waits for them, and re-layouts  18.2 us
  transfers between devices with their start and end apart: 28, of which 17 were waited for; matrix products, arithmetic and copies ran while one was open for 10% of the time, Pallas kernels for 24%

profile of v1, /device:TPU:0, one launch (start us, length us, event | category | flops | bytes accessed | tf_op | source)
XLA Modules:
  0.0 558.3 jit_solution(132196851978428774)
XLA Ops:
  25.4 5.8 %collective-permute-done.2 = bf16[2,24,1152]{2,1,0:T(8,128)(2,1)S(1)} collective-permute-done((bf16[2,24,1152]{2,1,0:T(8,128)(2,1)S(1)}, bf16[2,24,1152]{2,1,0:T(8,128)(2,1)S(1)}, u32[]{:S(2)}, u32[]{:S(2)}) %collective-permute-start.2) | collective-permute-done | bytes 110624 | tf_op jit(solution)/shard_map/ppermute | solution.py:771
  56.5 7.6 %collective-permute-done.7 = bf16[2,4,2,24,640]{4,3,2,1,0:T(8,128)(2,1)} collective-permute-done((bf16[2,4,2,24,640]{4,3,2,1,0:T(8,128)(2,1)}, bf16[2,4,2,24,640]{4,3,2,1,0:T(8,128)(2,1)}, u32[]{:S(2)}, u32[]{:S(2)}) %collective-permute-start.7) | collective-permute-done | bytes 491552 | tf_op jit(solution)/shard_map/ppermute | solution.py:754
  71.2 10.5 %norm_qkv.1 = (bf16[2048,768]{1,0:T(8,128)(2,1)S(1)}, bf16[2048,2304]{1,0:T(8,128)(2,1)}) custom-call(bf16[2048,768]{1,0:T(8,128)(2,1)S(1)} %bitcast.175, f32[1,768]{1,0:T(1,128)S(1)} %broadcast_in_dim.189.gain_ref.refs_1_, bf16[768,2304]{1,0:T(8,128)(2,1)S(1)} %bitcast.171), custom_call_target="tpu_custom_call" | custom-call | flops 7247757312 | bytes 15728640 | tf_op jit(solution)/shard_map/norm_qkv/pallas_call | solution.py:72
  83.3 8.1 %fusion.53 = (bf16[1024,2304]{1,0:T(8,128)(2,1)}, bf16[1024,2304]{1,0:T(8,128)(2,1)}) fusion(bf16[2048,2304]{1,0:T(8,128)(2,1)} %get-tuple-element.52), kind=kLoop, calls=%fused_computation.187 | loop fusion | bytes 18874368 | tf_op jit(solution)/shard_map/slice | solution.py:896
  91.5 26.0 %attention_forward.3 = (bf16[1024,768]{1,0:T(8,128)(2,1)S(1)}, bf16[12,1024,1024]{2,1,0:T(8,128)(2,1)}, f32[6,2,1024]{2,1,0:T(2,128)S(1)}) custom-call(s32[18]{0:T(128)S(1)} %get-tuple-element.204.info_ref, bf16[1024,2304]{1,0:T(8,128)(2,1)} %get-tuple-element.145.q_ref.k_ref.v_ref, bf16[1024,2304]{1,0:T(8,128)(2,1)} %get-tuple-element.145.q_ref.k_ref.v_ref, ...), custom_call_target="tpu_custom_call" | custom-call | flops 6442450944 | bytes 25165824 | tf_op jit(solution)/shard_map/attention_forward/pallas_call | solution.py:194
  119.4 26.3 %attention_forward.2 = (bf16[1024,768]{1,0:T(8,128)(2,1)S(1)}, bf16[12,1024,1024]{2,1,0:T(8,128)(2,1)}, f32[6,2,1024]{2,1,0:T(2,128)S(1)}) custom-call(s32[18]{0:T(128)S(1)} %get-tuple-element.203.info_ref, bf16[1024,2304]{1,0:T(8,128)(2,1)} %get-tuple-element.144.q_ref.k_ref.v_ref, bf16[1024,2304]{1,0:T(8,128)(2,1)} %get-tuple-element.144.q_ref.k_ref.v_ref, ...), custom_call_target="tpu_custom_call" | custom-call | flops 6442450944 | bytes 25165824 | tf_op jit(solution)/shard_map/attention_forward/pallas_call | solution.py:194
  147.4 23.6 %ffn_forward.2 = (f32[1024,768]{1,0:T(8,128)}, bf16[1024,768]{1,0:T(8,128)(2,1)}, bf16[1024,3072]{1,0:T(8,128)(2,1)}, bf16[1024,3072]{1,0:T(8,128)(2,1)}, f32[10...) custom-call(s32[16]{0:T(128)} %copy-done.51, bf16[1024,768]{1,0:T(8,128)(2,1)} %get-tuple-element.152.x_ref, ...), custom_call_target="tpu_custom_call" | custom-call | flops 10871635968 | bytes 31457280 | tf_op jit(solution)/shard_map/ffn_forward/pallas_call | solution.py:422
  171.8 23.6 %ffn_forward.3 = (f32[1024,768]{1,0:T(8,128)}, bf16[1024,768]{1,0:T(8,128)(2,1)}, bf16[1024,3072]{1,0:T(8,128)(2,1)}, bf16[1024,3072]{1,0:T(8,128)(2,1)}, f32[10...) custom-call(s32[16]{0:T(128)} %copy-done.50, bf16[1024,768]{1,0:T(8,128)(2,1)} %get-tuple-element.153.x_ref, ...), custom_call_target="tpu_custom_call" | custom-call | flops 10871635968 | bytes 31457280 | tf_op jit(solution)/shard_map/ffn_forward/pallas_call | solution.py:422
  199.0 23.0 %all-to-all-start = ((bf16[32,2,768]{2,1,0:T(2,128)(2,1)}), bf16[32,2,768]{2,1,0:T(2,128)(2,1)S(1)}, u32[]{:S(2)}, u32[]{:S(2)}) async-start(bf16[32,2,768]{2,1,0:T(2,128)(2,1)} %broadcast_in_dim.211), calls=%async_computation | async-start | bytes 196608 | tf_op jit(solution)/shard_map/all_to_all | solution.py:912
  222.1 7.8 %all-to-all-done = bf16[32,2,768]{2,1,0:T(2,128)(2,1)S(1)} async-done(((bf16[32,2,768]{2,1,0:T(2,128)(2,1)}), bf16[32,2,768]{2,1,0:T(2,128)(2,1)S(1)}, u32[]{:S(2)}, u32[]{:S(2)}) %all-to-all-start) | async-done | bytes 98336 | tf_op jit(solution)/shard_map/all_to_all | solution.py:912
  236.3 6.9 %all-to-all-done.1 = f32[32,2,768]{2,1,0:T(2,128)S(1)} async-done(((f32[32,2,768]{2,1,0:T(2,128)}), f32[32,2,768]{2,1,0:T(2,128)S(1)}, u32[]{:S(2)}, u32[]{:S(2)}) %all-to-all-start.1) | async-done | bytes 196640 | tf_op jit(solution)/shard_map/all_to_all | solution.py:931
  248.7 37.3 %ffn_backward.2 = (f32[768,7680]{1,0:T(8,128)}, f32[1024,768]{1,0:T(8,128)}, bf16[1024,768]{1,0:T(8,128)(2,1)}, f32[2,768]{1,0:T(2,128)}) custom-call(s32[16]{0:T(128)} %copy-done.51, f32[1024,768]{1,0:T(8,128)} %get-tuple-element.64.refs_1_, bf16[1024,768]{1,0:T(8,128)(2,1)} %get-tuple-element.150.refs_2_, f32[16,768]{1,0:T(8,128)} %get-tuple-element.182.refs_3_, ...), custom_call_target="tpu_custom_call" | custom-call | flops 21743271936 | bytes 47185920 | tf_op jit(solution)/shard_map/ffn_backward/pallas_call | solution.py:585
  286.0 38.3 %ffn_backward.3 = (bf16[768,7680]{1,0:T(8,128)(2,1)}, f32[1024,768]{1,0:T(8,128)}, bf16[1024,768]{1,0:T(8,128)(2,1)}, f32[2,768]{1,0:T(2,128)}) custom-call(s32[16]{0:T(128)} %copy-done.50, f32[1024,768]{1,0:T(8,128)} %get-tuple-element.57.refs_1_, bf16[1024,768]{1,0:T(8,128)(2,1)} %get-tuple-element.151.refs_2_, f32[16,768]{1,0:T(8,128)} %get-tuple-element.183.refs_3_, ...), custom_call_target="tpu_custom_call" | custom-call | flops 21743271936 | bytes 47185920 | tf_op jit(solution)/shard_map/ffn_backward/pallas_call | solution.py:585
  324.3 5.6 %dynamic-slice_bitcast_fusion = bf16[2,4,2,24,7680]{4,3,2,1,0:T(8,128)(2,1)} fusion(bf16[2,4,2,2,24,7680]{5,4,3,2,1,0:T(8,128)(2,1)} %bitcast.187, s32[]{:T(128)S(6)} %select_n.286), kind=kLoop, calls=%fused_computation.8 | loop fusion | bytes 11796484 | tf_op jit(solution)/shard_map/jit(dynamic_index_in_dim)/squeeze | solution.py:795
  330.5 9.6 %collective-permute-done.22 = bf16[2,4,2,24,7680]{4,3,2,1,0:T(8,128)(2,1)} collective-permute-done((bf16[2,4,2,24,7680]{4,3,2,1,0:T(8,128)(2,1)}, bf16[2,4,2,24,7680]{4,3,2,1,0:T(8,128)(2,1)}, u32[]{:S(2)}, u32[]{:S(2)}) %collective-permute-start.22) | collective-permute-done | bytes 5898272 | tf_op jit(solution)/shard_map/ppermute | solution.py:754
  340.1 6.2 %fusion.4 = bf16[2,2,4,24,7680]{4,3,1,2,0:T(8,128)(2,1)S(1)} fusion(bf16[2,4,2,24,7680]{4,3,2,1,0:T(8,128)(2,1)} %collective-permute-done.22, bf16[2,4,2,2,24,7680]{5,4,3,2,1,0:T(8,128)(2,1)} %bitcast.188, s32[]{:T(128)S(6)} %select_n.285), kind=kLoop, calls=%fused_computation.7 | loop fusion | flops 11796480 | bytes 17694724 | tf_op jit(solution)/shard_map/transpose | solution.py:828
  346.3 3.0 copy.73
  350.0 22.7 %attention_backward.2 = (bf16[3,1024,768]{2,1,0:T(8,128)(2,1)}, f32[12,3,128,128]{3,2,1,0:T(8,128)}, f32[6,2,8,1024]{3,2,1,0:T(8,128)}) custom-call(s32[18]{0:T(128)} %copy-done.8, bf16[1024,2304]{1,0:T(8,128)(2,1)} %get-tuple-element.145.q_ref.k_ref.v_ref, bf16[1024,2304]{1,0:T(8,128)(2,1)} %get-tuple-element.145.q_ref.k_ref.v_ref, ...), custom_call_target="tpu_custom_call" | custom-call | flops 12884901888 | bytes 25165824 | tf_op jit(solution)/shard_map/attention_backward/pallas_call | solution.py:327
  372.7 22.8 %attention_backward.3 = (bf16[3,1024,768]{2,1,0:T(8,128)(2,1)}, f32[12,3,128,128]{3,2,1,0:T(8,128)}, f32[6,2,8,1024]{3,2,1,0:T(8,128)}) custom-call(s32[18]{0:T(128)} %copy-done.7, bf16[1024,2304]{1,0:T(8,128)(2,1)} %get-tuple-element.144.q_ref.k_ref.v_ref, bf16[1024,2304]{1,0:T(8,128)(2,1)} %get-tuple-element.144.q_ref.k_ref.v_ref, ...), custom_call_target="tpu_custom_call" | custom-call | flops 12884901888 | bytes 25165824 | tf_op jit(solution)/shard_map/attention_backward/pallas_call | solution.py:327
  395.5 11.8 %qkv_weight_grads.1 = (bf16[768,2304]{1,0:T(8,128)(2,1)}, f32[768,128]{1,0:T(8,128)S(1)}) custom-call(bf16[2048,768]{1,0:T(8,128)(2,1)S(1)} %copy-done.12, bf16[3,1024,768]{2,1,0:T(8,128)(2,1)} %get-tuple-element.78.d_ref.d0_ref, bf16[3,1024,768]{2,1,0:T(8,128)(2,1)} %get-tuple-element.73.refs_3_.d1_ref, bf16[768,2304]{1,0:T(8,128)(2,1)} %bitcast.172), custom_call_target="tpu_custom_call" | custom-call | flops 7247757312 | bytes 15728640 | tf_op jit(solution)/shard_map/qkv_weight_grads/pallas_call | solution.py:638
  414.1 3.3 fusion.15
  417.6 3.7 constant_dynamic-slice_fusion.1
  423.3 3.0 collective-permute-done.9
  430.0 41.9 %collective-permute-start.11 = (f32[24,128]{1,0:T(8,128)S(1)}, f32[24,128]{1,0:T(8,128)S(1)}, u32[]{:S(2)}, u32[]{:S(2)}) collective-permute-start(f32[24,128]{1,0:T(8,128)S(1)} %fusion.67), channel_id=1, source_target_pairs={{0,16},{16,0},{1,17},{17,1},{2,18},{18,2},{3,19},{19,3},{4,20},{20... | collective-permute-start | bytes 36872 | tf_op jit(solution)/shard_map/ppermute | solution.py:837
  471.9 4.0 maximum_bitcast_fusion
  480.7 6.8 %qkv_input_grad.2.refs_5_ = f32[2,1024,768]{2,1,0:T(8,128)} custom-call(bf16[2,1024,768]{2,1,0:T(8,128)(2,1)S(1)} %bitcast.176, f32[1,768]{1,0:T(1,128)S(1)} %broadcast_in_dim.189.gain_ref.refs_1_, bf16[768,2304]{1,0:T(8,128)(2,1)S(1)} %bitcast.173, bf16[3,1024,768]{2,1,0:T(8,128)(2,1)S(1)} %copy-done.4, f32[1024,768]{1,0:T(8,128)S(1)} %copy-done.6), custom_call_target="tpu_custom_call" | custom-call | flops 3623878656 | bytes 12582912 | tf_op jit(solution)/shard_map/qkv_input_grad/pallas_call | solution.py:687
  492.5 6.8 %qkv_input_grad.3 = f32[2,1024,768]{2,1,0:T(8,128)} custom-call(bf16[2,1024,768]{2,1,0:T(8,128)(2,1)S(1)} %bitcast.177, f32[1,768]{1,0:T(1,128)S(1)} %broadcast_in_dim.189.gain_ref.refs_1_, bf16[768,2304]{1,0:T(8,128)(2,1)S(1)} %bitcast.174, bf16[3,1024,768]{2,1,0:T(8,128)(2,1)S(1)} %bitcast.179, ...), custom_call_target="tpu_custom_call", output_to_operand_aliasing={{}: (5, {})} | custom-call | flops 3623878656 | bytes 12582912 | tf_op jit(solution)/shard_map/qkv_input_grad/pallas_call | solution.py:687
  501.7 10.3 %collective-permute-done.17 = bf16[2,4,24,1152]{3,2,1,0:T(8,128)(2,1)S(1)} collective-permute-done((bf16[2,4,24,1152]{3,2,1,0:T(8,128)(2,1)S(1)}, bf16[2,4,24,1152]{3,2,1,0:T(8,128)(2,1)S(1)}, u32[]{:S(2)}, u32[]{:S(2)}) %collective-permute-start.17) | collective-permute-done | bytes 442400 | tf_op jit(solution)/shard_map/ppermute | solution.py:754
  514.5 3.7 collective-permute-done.18
  518.3 3.4 collective-permute-start.21
  525.6 4.1 collective-permute-done.21
  529.7 12.3 %collective-permute-done.20 = bf16[24,2304]{1,0:T(8,128)(2,1)S(1)} collective-permute-done((bf16[24,2304]{1,0:T(8,128)(2,1)S(1)}, bf16[24,2304]{1,0:T(8,128)(2,1)S(1)}, u32[]{:S(2)}, u32[]{:S(2)}) %collective-permute-start.20) | collective-permute-done | bytes 110624 | tf_op jit(solution)/shard_map/ppermute | solution.py:807
  (294 shorter events, 110.6 us)
Async XLA Ops:
  7.2 140.2 %all-gather.2.cloned.1.call-start = ((), (), s32[]{:S(2)}) async-start(), calls=%async_computation.4 | async-start | bytes 12165120 | tf_op jit(solution)/shard_map/all_gather | solution.py:881
  11.9 1.5 collective-permute-start
  14.3 9.6 %collective-permute-start.1 = (bf16[2,24,1152]{2,1,0:T(8,128)(2,1)S(1)}, bf16[2,24,1152]{2,1,0:T(8,128)(2,1)}, u32[]{:S(2)}, u32[]{:S(2)}) collective-permute-start(bf16[2,24,1152]{2,1,0:T(8,128)(2,1)S(1)} %get-tuple-element.143), channel_id=1, source_target_pairs={{0,4},{4,8},{8,12},{12,0},{1,5},{5,9},{9,13},{13,1},{2,6},{6,10},{... | collective-permute-start | bytes 331784 | tf_op jit(solution)/shard_map/ppermute | solution.py:771
  19.4 11.8 %collective-permute-start.2 = (bf16[2,24,1152]{2,1,0:T(8,128)(2,1)S(1)}, bf16[2,24,1152]{2,1,0:T(8,128)(2,1)S(1)}, u32[]{:S(2)}, u32[]{:S(2)}) collective-permute-start(bf16[2,24,1152]{2,1,0:T(8,128)(2,1)S(1)} %get-tuple-element.143), channel_id=1, source_target_pairs={{0,8},{4,12},{8,0},{12,4},{1,9},{5,13},{9,1},{13,5},{2,10},{6,14},... | collective-permute-start | bytes 331784 | tf_op jit(solution)/shard_map/ppermute | solution.py:771
  22.0 9.8 %collective-permute-start.3 = (bf16[2,24,1152]{2,1,0:T(8,128)(2,1)S(1)}, bf16[2,24,1152]{2,1,0:T(8,128)(2,1)S(1)}, u32[]{:S(2)}, u32[]{:S(2)}) collective-permute-start(bf16[2,24,1152]{2,1,0:T(8,128)(2,1)S(1)} %get-tuple-element.143), channel_id=1, source_target_pairs={{0,12},{4,0},{8,4},{12,8},{1,13},{5,1},{9,5},{13,9},{2,14},{6,2},{... | collective-permute-start | bytes 331784 | tf_op jit(solution)/shard_map/ppermute | solution.py:771
  33.5 5.7 %collective-permute-start.4 = (bf16[4,2,24,512]{3,2,1,0:T(8,128)(2,1)S(1)}, bf16[4,2,24,512]{3,2,1,0:T(8,128)(2,1)S(1)}, u32[]{:S(2)}, u32[]{:S(2)}) collective-permute-start(bf16[4,2,24,512]{3,2,1,0:T(8,128)(2,1)S(1)} %slice.241), channel_id=1, source_target_pairs={{0,2},{2,0},{1,3},{3,1},{4,6},{6,4},{5,7},{7,5},{8,10},{10,8},{9,1... | collective-permute-start | bytes 589832 | tf_op jit(solution)/shard_map/ppermute | solution.py:754
  36.5 8.9 %collective-permute-start.6 = (bf16[4,2,24,640]{3,2,1,0:T(8,128)(2,1)S(1)}, bf16[4,2,24,640]{3,2,1,0:T(8,128)(2,1)S(1)}, u32[]{:S(2)}, u32[]{:S(2)}) collective-permute-start(bf16[4,2,24,640]{3,2,1,0:T(8,128)(2,1)S(1)} %slice.242), channel_id=1, source_target_pairs={{0,16},{16,0},{1,17},{17,1},{2,18},{18,2},{3,19},{19,3},{4,20},{20... | collective-permute-start | bytes 737288 | tf_op jit(solution)/shard_map/ppermute | solution.py:754
  41.0 14.4 %collective-permute-start.5 = (bf16[2,4,2,24,512]{4,3,2,1,0:T(8,128)(2,1)}, bf16[2,4,2,24,512]{4,3,2,1,0:T(8,128)(2,1)}, u32[]{:S(2)}, u32[]{:S(2)}) collective-permute-start(bf16[2,4,2,24,512]{4,3,2,1,0:T(8,128)(2,1)} %pad_maximum_fusion.4), channel_id=1, source_target_pairs={{0,16},{16,0},{1,17},{17,1},{2,18},{18,2},{3,19},{19,3},{4,20},{20... | collective-permute-start | bytes 1179656 | tf_op jit(solution)/shard_map/ppermute | solution.py:754
  48.0 16.2 %collective-permute-start.7 = (bf16[2,4,2,24,640]{4,3,2,1,0:T(8,128)(2,1)}, bf16[2,4,2,24,640]{4,3,2,1,0:T(8,128)(2,1)}, u32[]{:S(2)}, u32[]{:S(2)}) collective-permute-start(bf16[2,4,2,24,640]{4,3,2,1,0:T(8,128)(2,1)} %pad_maximum_fusion.3), channel_id=1, source_target_pairs={{0,2},{2,0},{1,3},{3,1},{4,6},{6,4},{5,7},{7,5},{8,10},{10,8},{9,1... | collective-permute-start | bytes 1474568 | tf_op jit(solution)/shard_map/ppermute | solution.py:754
  65.6 4.6 collective-permute-start.8
  67.2 52.1 %copy-start.7 = (s32[18]{0:T(128)}, s32[18]{0:T(128)S(1)}, u32[]{:S(2)}) copy-start(s32[18]{0:T(128)S(1)} %get-tuple-element.203.info_ref) | copy-start | bytes 220
  171.8 58.2 %copy-start.43 = (s32[2,1,16]{2,1,0:T(1,128)S(1)}, s32[2,1,16]{2,1,0:T(1,128)}, u32[]{:S(2)}) copy-start(s32[2,1,16]{2,1,0:T(1,128)} %param.17) | copy-start | bytes 388
  195.4 38.9 %copy-start.19 = (bf16[1,1,2,1024,768]{4,3,2,1,0:T(8,128)(2,1)S(1)}, bf16[1,1,2,1024,768]{4,3,2,1,0:T(8,128)(2,1)}, u32[]{:S(2)}) copy-start(bf16[1,1,2,1024,768]{4,3,2,1,0:T(8,128)(2,1)} %param.18) | copy-start | bytes 9437188
  199.0 30.8 %all-to-all-start = ((bf16[32,2,768]{2,1,0:T(2,128)(2,1)}), bf16[32,2,768]{2,1,0:T(2,128)(2,1)S(1)}, u32[]{:S(2)}, u32[]{:S(2)}) async-start(bf16[32,2,768]{2,1,0:T(2,128)(2,1)} %broadcast_in_dim.211), calls=%async_computation | async-start | bytes 196608 | tf_op jit(solution)/shard_map/all_to_all | solution.py:912
  231.7 11.5 %all-to-all-start.1 = ((f32[32,2,768]{2,1,0:T(2,128)}), f32[32,2,768]{2,1,0:T(2,128)S(1)}, u32[]{:S(2)}, u32[]{:S(2)}) async-start(f32[32,2,768]{2,1,0:T(2,128)} %concatenate.43.clone), calls=%async_computation.1 | async-start | bytes 393216 | tf_op jit(solution)/shard_map/all_to_all | solution.py:931
  234.3 267.4 %reduce-scatter.3.cloned.1.call-start = ((), (), s32[]{:S(2)}) async-start(), calls=%async_computation.5 | async-start | bytes 7372800 | tf_op jit(solution)/shard_map/reduce_scatter | solution.py:829
  329.9 10.2 %collective-permute-start.22 = (bf16[2,4,2,24,7680]{4,3,2,1,0:T(8,128)(2,1)}, bf16[2,4,2,24,7680]{4,3,2,1,0:T(8,128)(2,1)}, u32[]{:S(2)}, u32[]{:S(2)}) collective-permute-start(bf16[2,4,2,24,7680]{4,3,2,1,0:T(8,128)(2,1)} %dynamic-slice_bitcast_fusion), channel_id=1, source_target_pairs={{0,1},{1,0},{2,3},{3,2},{4,5},{5,4},{6,7},{7,6},{8,9},{9,8},{10,11... | collective-permute-start | bytes 17694728 | tf_op jit(solution)/shard_map/ppermute | solution.py:754
  349.3 193.4 %reduce-scatter.5.cloned.1.call-start = ((), (), s32[]{:S(2)}) async-start(), calls=%async_computation.6 | async-start | bytes 1843200 | tf_op jit(solution)/shard_map/reduce_scatter | solution.py:830
  417.6 58.9 %copy-start.3 = (bf16[1,1,2,1024,768]{4,3,2,1,0:T(8,128)(2,1)S(1)}, bf16[1,1,2,1024,768]{4,3,2,1,0:T(8,128)(2,1)}, u32[]{:S(2)}) copy-start(bf16[1,1,2,1024,768]{4,3,2,1,0:T(8,128)(2,1)} %param.15) | copy-start | bytes 9437188
  422.6 65.4 %collective-permute-start.14 = (bf16[2,4,2,24,2304]{4,3,1,0,2:T(8,128)(2,1)}, bf16[2,4,2,24,2304]{4,3,1,0,2:T(8,128)(2,1)}, u32[]{:S(2)}, u32[]{:S(2)}) collective-permute-start(bf16[2,4,2,24,2304]{4,3,1,0,2:T(8,128)(2,1)} %bitcast.168), channel_id=1, source_target_pairs={{0,1},{1,0},{2,3},{3,2},{4,5},{5,4},{6,7},{7,6},{8,9},{9,8},{10,11... | collective-permute-start | bytes 5308424 | tf_op jit(solution)/shard_map/ppermute | solution.py:754
  422.9 3.4 collective-permute-start.9
  426.3 3.7 collective-permute-start.10
  430.0 45.9 %collective-permute-start.11 = (f32[24,128]{1,0:T(8,128)S(1)}, f32[24,128]{1,0:T(8,128)S(1)}, u32[]{:S(2)}, u32[]{:S(2)}) collective-permute-start(f32[24,128]{1,0:T(8,128)S(1)} %fusion.67), channel_id=1, source_target_pairs={{0,16},{16,0},{1,17},{17,1},{2,18},{18,2},{3,19},{19,3},{4,20},{20... | collective-permute-start | bytes 36872 | tf_op jit(solution)/shard_map/ppermute | solution.py:837
  475.9 11.6 %collective-permute-start.12 = (f32[24,128]{1,0:T(8,128)S(1)}, f32[24,128]{1,0:T(8,128)S(1)}, u32[]{:S(2)}, u32[]{:S(2)}) collective-permute-start(f32[24,128]{1,0:T(8,128)S(1)} %add.375), channel_id=1, source_target_pairs={{0,4},{4,0},{8,12},{12,8},{1,5},{5,1},{9,13},{13,9},{2,6},{6,2},{1... | collective-permute-start | bytes 36872 | tf_op jit(solution)/shard_map/ppermute | solution.py:837
  487.5 11.8 %collective-permute-start.13 = (f32[24,128]{1,0:T(8,128)S(1)}, f32[24,128]{1,0:T(8,128)S(1)}, u32[]{:S(2)}, u32[]{:S(2)}) collective-permute-start(f32[24,128]{1,0:T(8,128)S(1)} %add.376), channel_id=1, source_target_pairs={{0,8},{4,12},{8,0},{12,4},{1,9},{5,13},{9,1},{13,5},{2,10},{6,14},... | collective-permute-start | bytes 36872 | tf_op jit(solution)/shard_map/ppermute | solution.py:837
  490.4 10.3 %collective-permute-start.15 = (bf16[4,2,24,1152]{3,2,0,1:T(8,128)(2,1)S(1)}, bf16[4,2,24,1152]{3,2,0,1:T(8,128)(2,1)S(1)}, u32[]{:S(2)}, u32[]{:S(2)}) collective-permute-start(bf16[4,2,24,1152]{3,2,0,1:T(8,128)(2,1)S(1)} %dynamic-slice_bitcast_fusion.2), channel_id=1, source_target_pairs={{0,16},{16,0},{1,17},{17,1},{2,18},{18,2},{3,19},{19,3},{4,20},{20... | collective-permute-start | bytes 1327112 | tf_op jit(solution)/shard_map/ppermute | solution.py:754
  499.4 12.7 %collective-permute-start.17 = (bf16[2,4,24,1152]{3,2,1,0:T(8,128)(2,1)S(1)}, bf16[2,4,24,1152]{3,2,1,0:T(8,128)(2,1)S(1)}, u32[]{:S(2)}, u32[]{:S(2)}) collective-permute-start(bf16[2,4,24,1152]{3,2,1,0:T(8,128)(2,1)S(1)} %dynamic-slice_bitcast_fusion.1), channel_id=1, source_target_pairs={{0,2},{2,0},{1,3},{3,1},{4,6},{6,4},{5,7},{7,5},{8,10},{10,8},{9,1... | collective-permute-start | bytes 1327112 | tf_op jit(solution)/shard_map/ppermute | solution.py:754
  500.8 13.6 %collective-permute-start.16 = (bf16[4,24,1152]{2,1,0:T(8,128)(2,1)S(1)}, bf16[4,24,1152]{2,1,0:T(8,128)(2,1)S(1)}, u32[]{:S(2)}, u32[]{:S(2)}) collective-permute-start(bf16[4,24,1152]{2,1,0:T(8,128)(2,1)S(1)} %dynamic-slice_bitcast_fusion.4), channel_id=1, source_target_pairs={{0,2},{2,0},{1,3},{3,1},{4,6},{6,4},{5,7},{7,5},{8,10},{10,8},{9,1... | collective-permute-start | bytes 663560 | tf_op jit(solution)/shard_map/ppermute | solution.py:754
  512.2 6.0 %collective-permute-start.18 = (bf16[4,24,1152]{2,1,0:T(8,128)(2,1)S(1)}, bf16[4,24,1152]{2,1,0:T(8,128)(2,1)S(1)}, u32[]{:S(2)}, u32[]{:S(2)}) collective-permute-start(bf16[4,24,1152]{2,1,0:T(8,128)(2,1)S(1)} %dynamic-slice_bitcast_fusion.3), channel_id=1, source_target_pairs={{0,16},{16,0},{1,17},{17,1},{2,18},{18,2},{3,19},{19,3},{4,20},{20... | collective-permute-start | bytes 663560 | tf_op jit(solution)/shard_map/ppermute | solution.py:754
  518.3 11.4 %collective-permute-start.21 = (bf16[24,2304]{1,0:T(8,128)(2,1)S(1)}, bf16[24,2304]{1,0:T(8,128)(2,1)S(1)}, u32[]{:S(2)}, u32[]{:S(2)}) collective-permute-start(bf16[24,2304]{1,0:T(8,128)(2,1)S(1)} %get-tuple-element.166), channel_id=1, source_target_pairs={{0,12},{4,0},{8,4},{12,8},{1,13},{5,1},{9,5},{13,9},{2,14},{6,2},{... | collective-permute-start | bytes 331784 | tf_op jit(solution)/shard_map/ppermute | solution.py:807
  521.7 20.3 %collective-permute-start.20 = (bf16[24,2304]{1,0:T(8,128)(2,1)S(1)}, bf16[24,2304]{1,0:T(8,128)(2,1)S(1)}, u32[]{:S(2)}, u32[]{:S(2)}) collective-permute-start(bf16[24,2304]{1,0:T(8,128)(2,1)S(1)} %get-tuple-element.165), channel_id=1, source_target_pairs={{0,8},{4,12},{8,0},{12,4},{1,9},{5,13},{9,1},{13,5},{2,10},{6,14},... | collective-permute-start | bytes 331784 | tf_op jit(solution)/shard_map/ppermute | solution.py:807
  521.7 20.3 %collective-permute-start.19 = (bf16[24,2304]{1,0:T(8,128)(2,1)S(1)}, bf16[24,2304]{1,0:T(8,128)(2,1)S(1)}, u32[]{:S(2)}, u32[]{:S(2)}) collective-permute-start(bf16[24,2304]{1,0:T(8,128)(2,1)S(1)} %get-tuple-element.164), channel_id=1, source_target_pairs={{0,4},{4,8},{8,12},{12,0},{1,5},{5,9},{9,13},{13,1},{2,6},{6,10},{... | collective-permute-start | bytes 331784 | tf_op jit(solution)/shard_map/ppermute | solution.py:807
  (50 other events, 297.9 us)
Sparse Core Ops, SparseCore 0:
  11.9 104.0 all-gather.1
  349.5 64.5 reduce-scatter.2
  501.8 40.6 reduce-scatter.4

commit v2 on v1

--- a/solution.py
+++ b/solution.py
@@ -53,17 +53,24 @@
     return bucket + 16 * (offset > 0).astype(jnp.int32)
 
 
-def qkv_kernel(x_ref, gain_ref, w_ref, a1_ref, qkv_ref):
+def qkv_kernel(x_ref, gain_ref, w_ref, a1_ref, qkv_ref, norm_ref):
     x = x_ref[...].astype(F32)
     r = lax.rsqrt(jnp.mean(x * x, axis=-1, keepdims=True) + 1e-06)
     a1 = (x * r * gain_ref[...]).astype(BF)
     a1_ref[...] = a1
     width = a1.shape[1]
+    row = lax.broadcasted_iota(jnp.int32, (width, TILE), 0)
+    col = lax.broadcasted_iota(jnp.int32, (width, TILE), 1)
+    of_head = jnp.where(row // GROUP == col, 1.0, 0.0).astype(BF)
+    norm_ref[...] = jnp.zeros(norm_ref.shape, F32)
     for part in range(3):
         out = mm(a1, w_ref[:, part * width : (part + 1) * width]).astype(BF)
         if part == 0:
             out = out * BF(score_scale)
         qkv_ref[:, part * width : (part + 1) * width] = out
+        if part < 2:
+            square = mm(out * out, of_head)
+            norm_ref[0, part : part + 1, :] = jnp.max(square, axis=0, keepdims=True)
 
 
 def project_qkv(x, gain, w):
@@ -80,10 +87,12 @@
         out_specs=[
             pl.BlockSpec((block, width), lambda i: (i, 0)),
             pl.BlockSpec((block, 3 * width), lambda i: (i, 0)),
+            pl.BlockSpec((1, 8, TILE), lambda i: (i, 0, 0)),
         ],
         out_shape=[
             jax.ShapeDtypeStruct((rows, width), BF),
             jax.ShapeDtypeStruct((rows, 3 * width), BF),
+            jax.ShapeDtypeStruct((rows // block, 8, TILE), F32),
         ],
         compiler_params=params(40),
         cost_estimate=cost(6 * rows * width * width, rows * width * 10),
@@ -105,14 +114,14 @@
     return jnp.where(col == 0, jnp.where(row < length, 0.0, negative), ones).astype(BF)
 
 
-def query_mask(info_ref, tile):
+def query_mask(info_ref, slab, tile):
     row = lax.broadcasted_iota(jnp.int32, (TILE, TILE), 0)
     col = lax.broadcasted_iota(jnp.int32, (TILE, TILE), 1)
     per = TILE // GROUP
     good = jnp.zeros((TILE, TILE), jnp.bool_)
     for s in range(per):
         low = s * GROUP
-        inside = (row >= low) & (row < low + info_ref[2 + tile * per + s])
+        inside = (row >= low) & (row < low + info_ref[slab, 3 + tile * per + s])
         good = good | (inside & (col >= low) & (col < low + GROUP))
     return good
 
@@ -122,101 +131,142 @@
 ):
     rows = q_ref.shape[0]
     tiles = rows // TILE
+    per = WIDE // TILE
     vt = v_ref[...].T
-
-    def ones_below(head):
-        return jnp.concatenate(
-            [vt[head * GROUP : (head + 1) * GROUP, :], jnp.ones((16, rows), BF)], axis=0
-        )
-
-    @pl.when(info_ref[0] == 1)
+    below = [
+        jnp.concatenate([vt[h * GROUP : (h + 1) * GROUP, :], jnp.ones((16, rows), BF)], axis=0)
+        for h in range(2)
+    ]
+    work = [(head, wide) for head in range(2) for wide in range(rows // WIDE)]
+
+    def near(s, head, kb, qb):
+        return s + t_ref[head, kb - qb + 1] if abs(kb - qb) <= 1 else s
+
+    def tagged(n):
+        head, wide = work[n]
+        tags = [
+            jnp.broadcast_to(eq_ref[head, qb : qb + 1, :], (TILE, TILE))
+            for qb in range(wide * per, (wide + 1) * per)
+        ]
+        cols = slice(wide * WIDE, (wide + 1) * WIDE)
+        masked = jnp.where(lane_half((WIDE, TILE), head), q_ref[cols, :], BF(0))
+        return jnp.concatenate([masked, jnp.concatenate(tags, axis=0)], axis=1)
+
+    def mix(n):
+        head, wide = work[n]
+        cols = slice(wide * WIDE, (wide + 1) * WIDE)
+        out = mm(below[head], p_ref[head, :, cols])
+        inv = 1.0 / out[GROUP : GROUP + 1, :]
+        ot_scr[head * GROUP : (head + 1) * GROUP, cols] = out[:GROUP, :] * inv
+        linv_ref[0, head : head + 1, cols] = inv
+
+    slab = pl.program_id(0)
+    is_doc = info_ref[slab, 0] == 1
+    small = info_ref[slab, 2] == 1
+
+    @pl.when(is_doc & small)
     def _():
-        keys = jnp.concatenate([k_ref[...], key_extras(rows, info_ref[1])], axis=1)
-        for head in range(2):
-            va = ones_below(head)
-            masked = jnp.where(lane_half((rows, TILE), head), q_ref[...], BF(0))
-            for wide in range(rows // WIDE):
-                cols = slice(wide * WIDE, (wide + 1) * WIDE)
-                tags = [
-                    jnp.broadcast_to(eq_ref[head, qb : qb + 1, :], (TILE, TILE))
-                    for qb in range(wide * WIDE // TILE, (wide + 1) * WIDE // TILE)
-                ]
-                qa = jnp.concatenate([masked[cols, :], jnp.concatenate(tags, axis=0)], axis=1)
-                slot = (head * (rows // WIDE) + wide) % 2
-                s_scr[slot] = mm(keys, qa, NT)
-                for kb in range(tiles):
-                    for sub in range(WIDE // TILE):
-                        delta = kb - (wide * WIDE // TILE + sub)
-                        if abs(delta) <= 1:
-                            at = (
-                                slot,
-                                slice(kb * TILE, (kb + 1) * TILE),
-                                slice(sub * TILE, (sub + 1) * TILE),
-                            )
-                            s_scr[at] = s_scr[at] + t_ref[head, delta + 1]
-                top = s_scr[slot, 0:TILE, :]
-                for kb in range(1, tiles):
-                    top = jnp.maximum(top, s_scr[slot, kb * TILE : (kb + 1) * TILE, :])
-                top = jnp.max(top, axis=0, keepdims=True)
-                for kb in range(tiles):
-                    at = slice(kb * TILE, (kb + 1) * TILE)
-                    p_ref[head, at, cols] = jnp.exp(s_scr[slot, at, :] - top).astype(BF)
-                out = mm(va, p_ref[head, :, cols])
-                inv = 1.0 / out[GROUP : GROUP + 1, :]
-                ot_scr[head * GROUP : (head + 1) * GROUP, cols] = out[:GROUP, :] * inv
-                linv_ref[0, head : head + 1, cols] = inv
-
-    @pl.when(info_ref[0] == 0)
+        keys = jnp.concatenate([k_ref[...], key_extras(rows, info_ref[slab, 1])], axis=1)
+
+        def weigh(n):
+            head, wide = work[n]
+            qa = tagged(n)
+            for first in range(0, rows, WIDE):
+                part = mm(keys[first : first + WIDE, :], qa, NT)
+                for low in range(0, WIDE, TILE):
+                    for sub in range(per):
+                        kb, qb = (first + low) // TILE, wide * per + sub
+                        s = part[low : low + TILE, sub * TILE : (sub + 1) * TILE]
+                        p_ref[
+                            head, kb * TILE : (kb + 1) * TILE, qb * TILE : (qb + 1) * TILE
+                        ] = jnp.exp(near(s, head, kb, qb)).astype(BF)
+
+        for n in range(len(work)):
+            weigh(n)
+            if n > 0:
+                mix(n - 1)
+        mix(len(work) - 1)
+
+    @pl.when(is_doc & jnp.logical_not(small))
     def _():
-        for tile in range(tiles):
-            at = slice(tile * TILE, (tile + 1) * TILE)
-            good = query_mask(info_ref, tile)
+        keys = jnp.concatenate([k_ref[...], key_extras(rows, info_ref[slab, 1])], axis=1)
+        for n in range(len(work)):
+            head, wide = work[n]
+            part = mm(keys, tagged(n), NT)
+            tops = [None] * per
+            for kb in range(tiles):
+                for sub in range(per):
+                    at = (slice(kb * TILE, (kb + 1) * TILE), slice(sub * TILE, (sub + 1) * TILE))
+                    s = near(part[at], head, kb, wide * per + sub)
+                    s_scr[at] = s
+                    tops[sub] = s if tops[sub] is None else jnp.maximum(tops[sub], s)
+            top = jnp.concatenate([jnp.max(t, axis=0, keepdims=True) for t in tops], axis=1)
+            for kb in range(tiles):
+                at = slice(kb * TILE, (kb + 1) * TILE)
+                p_ref[head, at, wide * WIDE : (wide + 1) * WIDE] = jnp.exp(
+                    s_scr[at, :] - top
+                ).astype(BF)
+            mix(n)
+
+    @pl.when(jnp.logical_not(is_doc))
+    def _():
+        spans = [slice(tile * TILE, (tile + 1) * TILE) for tile in range(tiles)]
+        vo = jnp.concatenate([vt, jnp.ones((16, rows), BF)], axis=0)
+        bias = jnp.concatenate([t_ref[0, 1], t_ref[1, 1]], axis=1)
+        for at in spans:
+            q = q_ref[at, :]
+            both = [jnp.where(lane_half((TILE, TILE), head), q, BF(0)) for head in range(2)]
+            s_scr[at, :] = mm(k_ref[at, :], jnp.concatenate(both, axis=0), NT)
+        for tile, at in enumerate(spans):
+            good = query_mask(info_ref, slab, tile)
+            s = s_scr[at, :] + bias
+            s = jnp.where(jnp.concatenate([good, good], axis=1), s, negative)
+            p = jnp.exp(s - jnp.max(s, axis=0, keepdims=True)).astype(BF)
+            p_ref[0, at, at] = p[:, :TILE]
+            p_ref[1, at, at] = p[:, TILE:]
+        for at in spans:
+            out = mm(vo[:, at], jnp.concatenate([p_ref[0, at, at], p_ref[1, at, at]], axis=1))
+            inv = 1.0 / out[TILE : TILE + 1, :]
             for head in range(2):
-                va = ones_below(head)[:, at]
-                masked = jnp.where(lane_half((TILE, TILE), head), q_ref[at, :], BF(0))
-                s = mm(k_ref[at, :], masked, NT) + t_ref[head, 1]
-                s = jnp.where(good, s, negative)
-                top = jnp.max(s, axis=0, keepdims=True)
-                p = jnp.exp(s - top).astype(BF)
-                p_ref[head, at, at] = p
-                out = mm(va, p)
-                inv = 1.0 / out[GROUP : GROUP + 1, :]
-                ot_scr[head * GROUP : (head + 1) * GROUP, at] = out[:GROUP, :] * inv
-                linv_ref[0, head : head + 1, at] = inv
+                lanes = slice(head * TILE, (head + 1) * TILE)
+                mine = slice(head * GROUP, (head + 1) * GROUP)
+                ot_scr[mine, at] = out[mine, lanes] * inv[:, lanes]
+                linv_ref[0, head : head + 1, at] = inv[:, lanes]
 
     o_ref[...] = ot_scr[...].T.astype(BF)
 
 
 def attention(info, qkv, tags, near, heads):
-    rows = qkv.shape[0]
+    slabs = info.shape[0]
+    rows = qkv.shape[0] // slabs
     width = qkv.shape[1] // 3
     pairs = heads // 2
     return pl.pallas_call(
         attn_fwd_kernel,
         grid_spec=pltpu.PrefetchScalarGridSpec(
             num_scalar_prefetch=1,
-            grid=(pairs,),
+            grid=(slabs, pairs),
             in_specs=[
-                pl.BlockSpec((rows, TILE), lambda i, _: (0, i)),
-                pl.BlockSpec((rows, TILE), lambda i, _: (0, pairs + i)),
-                pl.BlockSpec((rows, TILE), lambda i, _: (0, 2 * pairs + i)),
-                pl.BlockSpec((2,) + tags.shape[1:], lambda i, _: (i, 0, 0)),
-                pl.BlockSpec((2,) + near.shape[1:], lambda i, _: (i, 0, 0, 0)),
+                pl.BlockSpec((rows, TILE), lambda s, i, _: (s, i)),
+                pl.BlockSpec((rows, TILE), lambda s, i, _: (s, pairs + i)),
+                pl.BlockSpec((rows, TILE), lambda s, i, _: (s, 2 * pairs + i)),
+                pl.BlockSpec((2,) + tags.shape[1:], lambda s, i, _: (i, 0, 0)),
+                pl.BlockSpec((2,) + near.shape[1:], lambda s, i, _: (i, 0, 0, 0)),
             ],
             out_specs=[
-                pl.BlockSpec((rows, TILE), lambda i, _: (0, i)),
-                pl.BlockSpec((2, rows, rows), lambda i, _: (i, 0, 0)),
-                pl.BlockSpec((1, 2, rows), lambda i, _: (i, 0, 0)),
+                pl.BlockSpec((rows, TILE), lambda s, i, _: (s, i)),
+                pl.BlockSpec((2, rows, rows), lambda s, i, _: (s * pairs + i, 0, 0)),
+                pl.BlockSpec((1, 2, rows), lambda s, i, _: (s * pairs + i, 0, 0)),
             ],
-            scratch_shapes=[pltpu.VMEM((2, rows, WIDE), F32), pltpu.VMEM((TILE, rows), F32)],
+            scratch_shapes=[pltpu.VMEM((rows, WIDE), F32), pltpu.VMEM((TILE, rows), F32)],
         ),
         out_shape=[
-            jax.ShapeDtypeStruct((rows, width), BF),
-            jax.ShapeDtypeStruct((heads, rows, rows), BF),
-            jax.ShapeDtypeStruct((pairs, 2, rows), F32),
+            jax.ShapeDtypeStruct((slabs * rows, width), BF),
+            jax.ShapeDtypeStruct((slabs * heads, rows, rows), BF),
+            jax.ShapeDtypeStruct((slabs * pairs, 2, rows), F32),
         ],
         compiler_params=params(48),
-        cost_estimate=cost(heads * rows * rows * 512, heads * rows * rows * 2),
+        cost_estimate=cost(slabs * heads * rows * rows * 512, slabs * heads * rows * rows * 2),
         name="attention_forward",
     )(info, qkv, qkv, qkv, tags, near)
 
@@ -231,13 +281,25 @@
     p_ref,
     linv_ref,
     dqkv_ref,
-    near_ref,
-    far_ref,
+    sums_ref,
     ds_scr,
     dqt_scr,
+    far_scr,
 ):
     rows = q_ref.shape[0]
     tiles = rows // TILE
+    square = (TILE, TILE)
+    mirror = lax.broadcasted_iota(jnp.int32, square, 0) + lax.broadcasted_iota(jnp.int32, square, 1)
+    mirror = jnp.where(mirror == TILE - 1, 1.0, 0.0)
+    sums_ref[...] = jnp.zeros(sums_ref.shape, F32)
+
+    def diagonals(x):
+        x = lax.dot_general(
+            x, mirror, NN, precision=lax.Precision.HIGHEST, preferred_element_type=F32
+        )
+        x = jnp.concatenate([x, jnp.zeros(square, F32)], axis=1)
+        return jnp.sum(pltpu.roll(x, 0, 1, stride=1, stride_axis=0), axis=0, keepdims=True)
+
     col = lax.broadcasted_iota(jnp.int32, (rows, TILE), 1)
     kt = k_ref[...].T
     scale = jnp.concatenate([linv_ref[0], jnp.zeros((6, rows), F32)], axis=0).T
@@ -256,26 +318,41 @@
         masked = jnp.where(mine, q_ref[...], BF(0))
         return scaled, jnp.concatenate([scaled, extra], axis=1), masked
 
-    @pl.when(info_ref[0] == 1)
+    @pl.when(info_ref[0, 0] == 1)
     def _():
         block = lax.broadcasted_iota(jnp.int32, (16, rows), 1) // TILE
         place = lax.broadcasted_iota(jnp.int32, (16, rows), 0)
         marks = jnp.where(block == place, 1.0, 0.0).astype(BF)
-        dk = jnp.zeros((rows, TILE), F32)
-        dv = jnp.zeros((rows, TILE), F32)
+        ready = [prepare(head) for head in range(2)]
+        ka = [
+            jnp.concatenate([kt[head * GROUP : (head + 1) * GROUP, :], marks], axis=0)
+            for head in range(2)
+        ]
+        work = [(head, wide) for head in range(2) for wide in range(rows // WIDE)]
+
+        def slope(n):
+            head, wide = work[n]
+            cols = slice(wide * WIDE, (wide + 1) * WIDE)
+            for first in range(0, rows, WIDE):
+                at = slice(first, first + WIDE)
+                dp = mm(values[at, :], ready[head][1][cols, :], NT)
+                ds_scr[head, at, cols] = (p_ref[head, at, cols].astype(F32) * dp).astype(BF)
+
+        def back(n):
+            head, wide = work[n]
+            cols = slice(wide * WIDE, (wide + 1) * WIDE)
+            out = mm(ka[head], ds_scr[head, :, cols])
+            dqt_scr[head * GROUP : (head + 1) * GROUP, cols] = out[:GROUP, :] * score_scale
+            far_scr[head, :, cols] = out[GROUP : GROUP + tiles, :]
+
+        for n in range(len(work)):
+            slope(n)
+            if n > 0:
+                back(n - 1)
+        back(len(work) - 1)
+        dk = mm(ds_scr[0], ready[0][2]) + mm(ds_scr[1], ready[1][2])
+        dv = mm(p_ref[0], ready[0][0]) + mm(p_ref[1], ready[1][0])
         for head in range(2):
-            scaled, outer, masked = prepare(head)
-            ka = jnp.concatenate([kt[head * GROUP : (head + 1) * GROUP, :], marks], axis=0)
-            for wide in range(rows // WIDE):
-                cols = slice(wide * WIDE, (wide + 1) * WIDE)
-                dp = mm(values, outer[cols, :], NT)
-                ds = (p_ref[head, :, cols].astype(F32) * dp).astype(BF)
-                ds_scr[head, :, cols] = ds
-                out = mm(ka, ds)
-                dqt_scr[head * GROUP : (head + 1) * GROUP, cols] = out[:GROUP, :] * score_scale
-                far_ref[0, head, :, cols] = out[GROUP : GROUP + tiles, :]
-            dv = dv + mm(p_ref[head], scaled)
-            dk = dk + mm(ds_scr[head], masked)
             for delta in (-1, 0, 1):
                 total = None
                 for qb in range(tiles):
@@ -285,14 +362,19 @@
                             head, kb * TILE : (kb + 1) * TILE, qb * TILE : (qb + 1) * TILE
                         ].astype(F32)
                         total = part if total is None else total + part
-                near_ref[head, delta + 1] = total
+                sums_ref[head, delta + 1 : delta + 2, :] = diagonals(total)
+            kb = lax.broadcasted_iota(jnp.int32, (tiles, rows), 0)
+            qb = lax.broadcasted_iota(jnp.int32, (tiles, rows), 1) // TILE
+            for at, side in ((3, kb <= qb - 2), (4, kb >= qb + 2)):
+                some = jnp.sum(jnp.where(side, far_scr[head], 0.0), axis=0, keepdims=True)
+                sums_ref[head, at : at + 1, 0:TILE] = sum(
+                    some[:, t * TILE : (t + 1) * TILE] for t in range(tiles)
+                )
         dqkv_ref[1] = dk.astype(BF)
         dqkv_ref[2] = dv.astype(BF)
 
-    @pl.when(info_ref[0] == 0)
+    @pl.when(info_ref[0, 0] == 0)
     def _():
-        far_ref[...] = jnp.zeros(far_ref.shape, F32)
-        near_ref[...] = jnp.zeros(near_ref.shape, F32)
         for head in range(2):
             scaled, outer, masked = prepare(head)
             total = None
@@ -313,42 +395,47 @@
                 else:
                     dqkv_ref[1, at, :] = ds_scr[0, at, 0:TILE] + dk.astype(BF)
                     dqkv_ref[2, at, :] = ds_scr[1, at, 0:TILE] + dv.astype(BF)
-            near_ref[head, 1] = total
+            sums_ref[head, 1:2, :] = diagonals(total)
 
     dqkv_ref[0] = dqt_scr[...].T.astype(BF)
 
 
-def attention_back(info, qkv, mixed, d_mixed, probs, linv):
-    rows = qkv.shape[0]
+def attention_back(info, qkv, mixed, d_mixed, probs, linv, slab, part, parts):
+    slabs = info.shape[0]
+    rows = qkv.shape[0] // slabs
     width = qkv.shape[1] // 3
-    pairs = linv.shape[0]
-    heads = 2 * pairs
+    pairs = linv.shape[0] // slabs
     tiles = rows // TILE
+    count = pairs // parts
+    base = part * count
+    heads = 2 * count
     return pl.pallas_call(
         attn_bwd_kernel,
         grid_spec=pltpu.PrefetchScalarGridSpec(
             num_scalar_prefetch=1,
-            grid=(pairs,),
+            grid=(count,),
             in_specs=[
-                pl.BlockSpec((rows, TILE), lambda i, _: (0, i)),
-                pl.BlockSpec((rows, TILE), lambda i, _: (0, pairs + i)),
-                pl.BlockSpec((rows, TILE), lambda i, _: (0, 2 * pairs + i)),
-                pl.BlockSpec((rows, TILE), lambda i, _: (0, i)),
-                pl.BlockSpec((rows, TILE), lambda i, _: (0, i)),
-                pl.BlockSpec((2, rows, rows), lambda i, _: (i, 0, 0)),
-                pl.BlockSpec((1, 2, rows), lambda i, _: (i, 0, 0)),
+                pl.BlockSpec((rows, TILE), lambda i, _: (slab, base + i)),
+                pl.BlockSpec((rows, TILE), lambda i, _: (slab, pairs + base + i)),
+                pl.BlockSpec((rows, TILE), lambda i, _: (slab, 2 * pairs + base + i)),
+                pl.BlockSpec((rows, TILE), lambda i, _: (slab, base + i)),
+                pl.BlockSpec((rows, TILE), lambda i, _: (0, base + i)),
+                pl.BlockSpec((2, rows, rows), lambda i, _: (slab * pairs + base + i, 0, 0)),
+                pl.BlockSpec((1, 2, rows), lambda i, _: (slab * pairs + base + i, 0, 0)),
             ],
             out_specs=[
                 pl.BlockSpec((3, rows, TILE), lambda i, _: (0, 0, i)),
-                pl.BlockSpec((2, 3, TILE, TILE), lambda i, _: (i, 0, 0, 0)),
-                pl.BlockSpec((1, 2, tiles, rows), lambda i, _: (i, 0, 0, 0)),
+                pl.BlockSpec((2, 8, 2 * TILE), lambda i, _: (i, 0, 0)),
             ],
-            scratch_shapes=[pltpu.VMEM((2, rows, rows), BF), pltpu.VMEM((TILE, rows), F32)],
+            scratch_shapes=[
+                pltpu.VMEM((2, rows, rows), BF),
+                pltpu.VMEM((TILE, rows), F32),
+                pltpu.VMEM((2, tiles, rows), F32),
+            ],
         ),
         out_shape=[
-            jax.ShapeDtypeStruct((3, rows, width), BF),
-            jax.ShapeDtypeStruct((heads, 3, TILE, TILE), F32),
-            jax.ShapeDtypeStruct((pairs, 2, tiles, rows), F32),
+            jax.ShapeDtypeStruct((3, rows, count * TILE), BF),
+            jax.ShapeDtypeStruct((heads, 8, 2 * TILE), F32),
         ],
         compiler_params=params(56),
         cost_estimate=cost(heads * rows * rows * 1024, heads * rows * rows * 2),
@@ -415,7 +502,7 @@
 def ffn_forward(glen, x, mixed, w_all, gain2, gain3):
     rows, width = x.shape
     ff = w_all.shape[1] // 2 - width
-    block = 256
+    block = 512
     groups = block // GROUP
     spec = pl.BlockSpec((block, width), lambda i, _: (i, 0))
     wide = pl.BlockSpec((block, ff), lambda i, _: (i, 0))
@@ -466,7 +553,9 @@
     return dx, d_gain
 
 
-def ffn_bwd_kernel(second):
+def ffn_bwd_kernel(slab, order):
+    second = slab > 0
+
     def kernel(*refs):
         (
             glen_ref,
@@ -504,8 +593,12 @@
 
         def put(side, value):
             if second:
-                value = value + before_ref[:, side]
+                value = ordered(value + before_ref[:, side])
             g_ref[:, side] = value.astype(g_ref.dtype)
+
+        def ordered(value):
+            shard = value.shape[0] // len(order)
+            return jnp.concatenate([value[d * shard : (d + 1) * shard, :] for d in order], axis=0)
 
         @pl.when(step == 0)
         def _():
@@ -520,7 +613,7 @@
                     ],
                     axis=0,
                 )
-                grad = jnp.where(usable_rows(glen_ref, b * per, block), grad, 0.0)
+                grad = jnp.where(usable_rows(glen_ref, slab * (rows // GROUP) + b * per, block), grad, 0.0)
                 dx, d_gain = norm_back(x2_ref[at, :], gain3_ref[...], grad)
                 gain = gain + d_gain
                 dx = dx + cot_ref[at, :].astype(F32)
@@ -550,28 +643,30 @@
             ggain_ref[0:1, :] = gain
             put(left, mm(mixed_ref[...], dy2_scr[...], TN))
             if second:
-                g_ref[:, right] = gproj_ref[...]
+                g_ref[:, right] = ordered(gproj_ref[...]).astype(BF)
             dmixed_ref[...] = mm(dy2_scr[...], w_ref[:, left], NT).astype(BF)
 
     return kernel
 
 
 def ffn_backward(
-    glen, x2, cot, dpool, x1, a2, mixed, act, slope, w_all, gain2, gain3, before, gproj
+    slab, order, glen, x2, cot, dpool, x1, a2, mixed, act, slope, w_all, gain2, gain3, before, gproj
 ):
-    rows, width = x2.shape
+    rows, width = cot.shape[1:]
     chunks = w_all.shape[1] // (2 * width) - 1
     ff = chunks * width
-    second = before is not None
-    side = pl.BlockSpec((rows, width), lambda i, _: (0, jnp.minimum(i, chunks - 1)))
+    second = slab > 0
+    side = pl.BlockSpec((rows, width), lambda i, _: (slab, jnp.minimum(i, chunks - 1)))
+    once = pl.Buffered(1)
+    mine = pl.BlockSpec((rows, width), lambda i, _: (slab, 0), pipeline_mode=once)
     part = pl.BlockSpec((width, 2 * width), lambda i, _: (0, i))
     in_specs = [
-        fixed((rows, width)),
-        fixed((rows, width)),
-        fixed(dpool.shape),
-        fixed((rows, width)),
-        fixed((rows, width)),
-        fixed((rows, width)),
+        mine,
+        pl.BlockSpec((None, rows, width), lambda i, _: (slab, 0, 0), pipeline_mode=once),
+        pl.BlockSpec((None,) + dpool.shape[1:], lambda i, _: (slab, 0, 0), pipeline_mode=once),
+        mine,
+        mine,
+        mine,
         side,
         side,
         part,
@@ -583,7 +678,7 @@
         in_specs += [part, fixed((width, width))]
         operands += [before, gproj]
     return pl.pallas_call(
-        ffn_bwd_kernel(second),
+        ffn_bwd_kernel(slab, order),
         grid_spec=pltpu.PrefetchScalarGridSpec(
             num_scalar_prefetch=1,
             grid=(chunks + 1,),
@@ -614,12 +709,12 @@
 
 
 def qkv_weight_kernel(a1_ref, d0_ref, d1_ref, w_ref, g_ref, gain_ref):
-    rows, width = d0_ref.shape[1:]
+    rows, cols = d0_ref.shape[1:]
     total = mm(a1_ref[0:rows, :], d0_ref[0], TN) + mm(a1_ref[rows:, :], d1_ref[0], TN)
     g_ref[...] = total.astype(BF)
     prod = total * w_ref[...].astype(F32)
     part = prod[:, 0:TILE]
-    for lane in range(1, width // TILE):
+    for lane in range(1, cols // TILE):
         part = part + prod[:, lane * TILE : (lane + 1) * TILE]
 
     @pl.when(pl.program_id(0) == 0)
@@ -631,30 +726,40 @@
         gain_ref[...] = gain_ref[...] + part
 
 
-def qkv_weight_grads(a1, d0, d1, w):
+def qkv_weight_grads(a1, d, w, part, parts):
     rows, width = a1.shape
-    one = pl.BlockSpec((1, rows // 2, width), lambda i: (i, 0, 0))
-    col = pl.BlockSpec((width, width), lambda i: (0, i))
+    cols = width // parts
+    one = pl.BlockSpec((1, rows // 2, cols), lambda i: (i, 0, 0))
     return pl.pallas_call(
         qkv_weight_kernel,
         grid=(3,),
-        in_specs=[fixed((rows, width)), one, one, col],
-        out_specs=[col, fixed((width, TILE))],
+        in_specs=[
+            fixed((rows, width)),
+            one,
+            one,
+            pl.BlockSpec((width, cols), lambda i: (0, parts * i + part)),
+        ],
+        out_specs=[pl.BlockSpec((width, cols), lambda i: (0, i)), fixed((width, TILE))],
         out_shape=[
-            jax.ShapeDtypeStruct((width, 3 * width), BF),
+            jax.ShapeDtypeStruct((width, 3 * cols), BF),
             jax.ShapeDtypeStruct((width, TILE), F32),
         ],
         compiler_params=params(48),
-        cost_estimate=cost(6 * rows * width * width, rows * width * 10),
+        cost_estimate=cost(6 * rows * width * cols, rows * width * 10),
         name="qkv_weight_grads",
-    )(a1, d0, d1, w)
-
-
-def qkv_input_kernel(x_ref, gain_ref, w_ref, d_ref, dx1_ref, out_ref):
+    )(a1, *d, w)
+
+
+def qkv_input_kernel(x_ref, gain_ref, w_ref, dx1_ref, *refs):
+    out_ref, parts = refs[-1], refs[:-1]
     width = x_ref.shape[1]
-    grad = mm(d_ref[0], w_ref[:, 0:width], NT)
-    grad = grad + mm(d_ref[1], w_ref[:, width : 2 * width], NT)
-    grad = grad + mm(d_ref[2], w_ref[:, 2 * width : 3 * width], NT)
+    grad = None
+    for i in range(3):
+        for part, d_ref in enumerate(parts):
+            cols = d_ref.shape[2]
+            at = i * width + part * cols
+            term = mm(d_ref[i], w_ref[:, at : at + cols], NT)
+            grad = term if grad is None else grad + term
     x = x_ref[...].astype(F32)
     r = lax.rsqrt(jnp.mean(x * x, axis=-1, keepdims=True) + 1e-06)
     hat = x * r
@@ -671,18 +776,17 @@
         pl.BlockSpec((None, block, width), lambda i: (slab, i, 0)),
         fixed((1, width)),
         fixed(w.shape),
-        pl.BlockSpec((3, block, width), lambda i: (0, i, 0)),
         spec,
-    ]
-    operands = [x, gain, w, d, dx1]
+    ] + [pl.BlockSpec((3, block, part.shape[2]), lambda i: (0, i, 0)) for part in d]
+    operands = [x, gain, w, dx1, *d]
     kernel, aliases = qkv_input_kernel, {}
     if before is not None:
+        aliases = {len(operands): 0}
         in_specs.append(pl.BlockSpec(memory_space=pl.ANY))
         operands.append(before)
-        aliases = {5: 0}
 
         def kernel(*refs):
-            qkv_input_kernel(*refs[:5], refs[6])
+            qkv_input_kernel(*refs[:-2], refs[-1])
 
     return pl.pallas_call(
         kernel,
@@ -697,21 +801,27 @@
     )(*operands)
 
 
-def near_offsets():
-    key = jnp.arange(TILE, dtype=jnp.int32)[None, :, None]
-    query = jnp.arange(TILE, dtype=jnp.int32)[None, None, :]
-    delta = jnp.arange(-1, 2, dtype=jnp.int32)[:, None, None]
-    return delta * TILE + key - query
+def bias_kernel(x_ref, near_ref):
+    for delta in range(3):
+        row = jnp.broadcast_to(x_ref[0, delta : delta + 1, :], (TILE, 2 * TILE))
+        near_ref[0, delta] = pltpu.roll(row, 0, 1, stride=1, stride_axis=0)[:, :TILE]
 
 
 def bias_tables(rel_bias, tiles):
     buckets, heads = rel_bias.shape
-    onehot = (
-        bucket_ids(near_offsets()).reshape(1, -1) == jnp.arange(buckets, dtype=jnp.int32)[:, None]
-    )
-    near = jnp.einsum(
-        "bh,bn->hn", rel_bias, onehot.astype(F32), precision=lax.Precision.HIGHEST
-    ).reshape(heads, 3, TILE, TILE)
+    lane = jnp.arange(2 * TILE, dtype=jnp.int32)
+    back = jnp.where(lane < TILE, lane, lane - 2 * TILE)
+    offsets = jnp.arange(-1, 2, dtype=jnp.int32)[:, None] * TILE - back[None, :]
+    onehot = bucket_ids(offsets).reshape(1, -1) == jnp.arange(buckets, dtype=jnp.int32)[:, None]
+    rows = jnp.einsum("bh,bn->hn", rel_bias, onehot.astype(F32), precision=lax.Precision.HIGHEST)
+    near = pl.pallas_call(
+        bias_kernel,
+        grid=(heads,),
+        in_specs=[pl.BlockSpec((1, 3, 2 * TILE), lambda i: (i, 0, 0))],
+        out_specs=pl.BlockSpec((1, 3, TILE, TILE), lambda i: (i, 0, 0, 0)),
+        out_shape=jax.ShapeDtypeStruct((heads, 3, TILE, TILE), F32),
+        name="bias_tables",
+    )(rows.reshape(heads, 3, 2 * TILE))
     qb = jnp.arange(tiles)[:, None]
     kb = jnp.arange(tiles)[None, :]
     left = rel_bias[buckets // 2 - 1][:, None, None]
@@ -731,23 +841,20 @@
     return near, tags
 
 
-def bias_grad(near, far, buckets):
-    heads = near.shape[0]
-    tiles = far.shape[2]
-    onehot = (
-        bucket_ids(near_offsets()).reshape(-1, 1) == jnp.arange(buckets, dtype=jnp.int32)[None, :]
-    )
-    grad = jnp.einsum(
-        "hn,nb->bh", near.reshape(heads, -1), onehot.astype(F32), precision=lax.Precision.HIGHEST
-    )
-    sums = jnp.sum(far.reshape(heads, tiles, tiles, TILE), axis=3)
-    kb = jnp.arange(tiles)[:, None]
-    qb = jnp.arange(tiles)[None, :]
-    left = jnp.sum(jnp.where(kb <= qb - 2, sums, 0.0), axis=(1, 2))
-    right = jnp.sum(jnp.where(kb >= qb + 2, sums, 0.0), axis=(1, 2))
-    row = jnp.arange(buckets)[:, None]
-    grad = grad + jnp.where(row == buckets // 2 - 1, left[None, :], 0.0)
-    return grad + jnp.where(row == buckets - 1, right[None, :], 0.0)
+def bias_grad(sums, buckets):
+    heads = sums.shape[0]
+    lane = jnp.arange(2 * TILE, dtype=jnp.int32)
+    offsets = jnp.arange(-1, 2, dtype=jnp.int32)[:, None] * TILE + lane[None, :] - (TILE - 1)
+    left = jnp.full((1, 2 * TILE), buckets // 2 - 1, jnp.int32)
+    right = jnp.full((1, 2 * TILE), buckets - 1, jnp.int32)
+    ids = jnp.concatenate([bucket_ids(offsets), left, right]).reshape(-1, 1)
+    onehot = ids == jnp.arange(buckets, dtype=jnp.int32)[None, :]
+    return jnp.einsum(
+        "hn,nb->bh",
+        sums[:, :5].reshape(heads, -1),
+        onehot.astype(F32),
+        precision=lax.Precision.HIGHEST,
+    )
 
 
 def swap(x, axis):
@@ -789,24 +896,18 @@
     return jnp.swapaxes(full, 1, 2).reshape(-1, columns)
 
 
-def give_half(x, axis, dim):
+def after(x, *earlier):
+    return lax.optimization_barrier((x,) + earlier)[0]
+
+
+def send_half(x, axis, dim):
     me = lax.axis_index(axis)
     keep = lax.dynamic_index_in_dim(x, me, dim, keepdims=False)
-    got = swap(lax.dynamic_index_in_dim(x, 1 - me, dim, keepdims=False), axis)
+    return keep, swap(lax.dynamic_index_in_dim(x, 1 - me, dim, keepdims=False), axis)
+
+
+def join(keep, got):
     return (keep.astype(F32) + got.astype(F32)).astype(BF)
-
-
-def ring_scatter(x, axis):
-    count = lax.axis_size(axis)
-    if count > 4:
-        return lax.psum_scatter(x, axis, scatter_dimension=0, tiled=False).astype(F32)
-    me = lax.axis_index(axis)
-    total = lax.dynamic_index_in_dim(x, me, 0, keepdims=False).astype(F32)
-    for k in range(1, count):
-        part = lax.dynamic_index_in_dim(x, (me + k) % count, 0, keepdims=False)
-        part = lax.ppermute(part, axis, [(j, (j + k) % count) for j in range(count)])
-        total = total + part.astype(F32)
-    return total
 
 
 def by_device(x):
@@ -814,29 +915,51 @@
     return x.reshape(sizes + (-1, x.shape[-1]))
 
 
+def scatter_order(shard):
+    t, z, x, c = (lax.axis_size(a) for a in AXES)
+    if shard % 8:
+        return tuple(range(t * z * x * c))
+    return tuple(
+        ((i * z + j) * x + k) * c + n
+        for i in range(t)
+        for k in range(x)
+        for n in range(c)
+        for j in range(z)
+    )
+
+
 def quick_scatter(x):
-    half = x.shape[-1] // 2
-    x = give_half(by_device(x), "core", 3)
-    one = give_half(give_half(x[..., :half], "tower", 0), "x", 1)
-    two = give_half(give_half(x[..., half:], "x", 2), "tower", 0)
-    return ring_scatter(jnp.concatenate([one, two], axis=-1), "z")
-
-
-def big_scatter(x):
-    x = give_half(by_device(x), "core", 3)
-    columns = x.shape[-1]
-    x = jnp.swapaxes(x, 1, 2).reshape(-1, columns)
-    x = lax.psum_scatter(x, ("tower", "x"), scatter_dimension=0, tiled=True)
-    return lax.psum_scatter(x, "z", scatter_dimension=0, tiled=True).astype(F32)
+    half = x.shape[-1] // 2 // TILE * TILE
+    keep, got = send_half(by_device(x), "core", 3)
+    x = join(keep, after(got, *(yield keep)))
+    keep1, got1 = send_half(x[..., :half], "tower", 0)
+    keep2, got2 = send_half(x[..., half:], "x", 2)
+    earlier = yield x
+    one, two = join(keep1, after(got1, *earlier)), join(keep2, after(got2, *earlier))
+    keep1, got1 = send_half(one, "x", 1)
+    keep2, got2 = send_half(two, "tower", 0)
+    earlier = yield one, two
+    one, two = join(keep1, after(got1, *earlier)), join(keep2, after(got2, *earlier))
+    x = jnp.concatenate([one, two], axis=-1)
+    count = lax.axis_size("z")
+    if count > 4:
+        yield x
+        yield lax.psum_scatter(x, "z", scatter_dimension=0, tiled=False).astype(F32)
+    me = lax.axis_index("z")
+    total = lax.dynamic_index_in_dim(x, me, 0, keepdims=False).astype(F32)
+    parts = []
+    for k in range(1, count):
+        part = lax.dynamic_index_in_dim(x, (me + k) % count, 0, keepdims=False)
+        parts.append(lax.ppermute(part, "z", [(j, (j + k) % count) for j in range(count)]))
+    earlier = yield x
+    for part in parts:
+        total = total + after(part, *earlier).astype(F32)
+    yield total
 
 
 def sum_everywhere(x):
-    for axis in ("core", "x", "tower", "z"):
-        count, step = lax.axis_size(axis), 1
-        while step < count:
-            x = x + lax.ppermute(x, axis, [(j, j ^ step) for j in range(count)])
-            step *= 2
-    return x
+    sent = jnp.broadcast_to(x[None], (lax.axis_size(AXES),) + x.shape)
+    return jnp.sum(lax.all_to_all(sent, AXES, 0, 0, tiled=True), axis=0)
 
 
 AXES = ("tower", "z", "x", "core")
@@ -884,22 +1007,23 @@
     w_proj_all = w_all[:, -width:]
 
     near_bias, tags = bias_tables(rel_bias, rows // TILE)
-    a1, qkv = project_qkv(x_all, gain1, wqkv)
-
-    slabs = []
-    for m in range(MICRO):
-        at = slice(m * rows, (m + 1) * rows)
-        lens = lengths[0, 0, m]
-        per_group = jnp.clip(lens[0] - GROUP * jnp.arange(rows // GROUP), 0, GROUP)
-        glen = jnp.where(is_doc, per_group, lens).astype(jnp.int32)
-        info = jnp.concatenate([jnp.stack([is_doc.astype(jnp.int32), lens[0]]), glen])
-        mixed, probs, linv = attention(info, qkv[at], tags, near_bias, heads)
-        x1, a2, act, slope, x2, out, pool = ffn_forward(
-            glen, hidden[0, 0, m], mixed, w_all, gain2, gain3
-        )
-        slabs.append((glen, info, lens, mixed, probs, linv, x1, a2, act, slope, x2, out, pool))
-
-    pool = jnp.stack([slab[-1] for slab in slabs])
+    a1, qkv, norms = project_qkv(x_all, gain1, wqkv)
+
+    room = jnp.maximum(60.0 - jnp.max(jnp.abs(rel_bias)), 0.0)
+    norms = jnp.max(norms, axis=0)
+    small = jnp.all(norms[0] * norms[1] * 1.05 <= room * room).astype(jnp.int32)
+    lens = lengths[0, 0]
+    groups = jnp.arange(rows // GROUP, dtype=jnp.int32)
+    per_group = jnp.clip(lens[:, 0:1] - GROUP * groups[None], 0, GROUP)
+    glen = jnp.where(is_doc, per_group, lens).astype(jnp.int32)
+    flags = jnp.broadcast_to(jnp.stack([is_doc.astype(jnp.int32), small]), (MICRO, 2))
+    info = jnp.concatenate([flags[:, 0:1], lens[:, 0:1], flags[:, 1:2], glen], axis=1)
+    glen = glen.reshape(-1)
+    mixed, probs, linv = attention(info, qkv, tags, near_bias, heads)
+    x1, a2, act, slope, x2, out, pool = ffn_forward(
+        glen, x_all, mixed, w_all, gain2, gain3
+    )
+    pool = pool.reshape(MICRO, rows // GROUP, width)
     counts = jnp.maximum(lengths[0, 0].astype(F32), 1.0)[..., None]
     doc_pool = jnp.where(first_slot, jnp.sum(pool, axis=1, keepdims=True), 0.0)
     pooled = (jnp.where(is_doc, doc_pool, pool) / counts).astype(BF)
@@ -908,8 +1032,8 @@
     ).reshape(MICRO, slots, width)
     unit_vec, unit_pull = jax.vjp(unit_norm, projected)
     unit_low = unit_vec.astype(BF)
-    sent = jnp.broadcast_to(unit_low[None, :, 0], (devices, MICRO, width))
-    docs = lax.all_to_all(sent, AXES, 0, 0, tiled=True)[dp_count:]
+    sent = jnp.broadcast_to(unit_low[:, 0].reshape(1, -1, TILE), (devices, MICRO * width // TILE, TILE))
+    docs = lax.all_to_all(sent, AXES, 0, 0, tiled=True)[dp_count:].reshape(-1, MICRO, width)
     logits = (
         jnp.einsum("msd,bmd->msb", unit_low, docs, preferred_element_type=F32) * logit_scale
     )
@@ -932,19 +1056,21 @@
     unit_grad = unit_grad + jnp.where(first_slot & is_doc, returned[:, None], 0.0)
     proj_grad_in = unit_pull(unit_grad)[0].astype(BF)
     flat = proj_grad_in.reshape(MICRO * slots, width)
-    grad_proj = mm(pooled.reshape(MICRO * slots, width), flat, TN).astype(BF)
+    grad_proj = mm(pooled.reshape(MICRO * slots, width), flat, TN)
     dpooled = jnp.dot(flat, w_proj_all.T, preferred_element_type=F32)
     dpooled = dpooled.reshape(MICRO, slots, width) / counts
     dpool = jnp.where(is_doc, jnp.broadcast_to(dpooled[:, 0:1], dpooled.shape), dpooled)
 
+    order = scatter_order(shard)
     grads, ggains, backs = None, 0.0, []
     for m in range(MICRO):
-        glen, info, lens, mixed, probs, linv, x1, a2, act, slope, x2, out, _ = slabs[m]
         grads, dx1, d_mixed, ggain = ffn_backward(
+            m,
+            order,
             glen,
             x2,
-            out_grad[0, 0, m],
-            dpool[m],
+            out_grad[0, 0],
+            dpool,
             x1,
             a2,
             mixed,
@@ -958,7 +1084,40 @@
         )
         backs.append((dx1, d_mixed))
         ggains = ggains + ggain
-    grad_all = big_scatter(grads)
+
+    if shard % 8:
+        grad_all = lax.psum_scatter(grads, AXES, scatter_dimension=0, tiled=True).astype(F32)
+    else:
+        inner = lax.psum_scatter(grads, ("tower", "x", "core"), scatter_dimension=0, tiled=True)
+    dqkvs, bias_sums = [], []
+    for m in range(MICRO):
+        dqkv, sums = attention_back(info, qkv, mixed, backs[m][1], probs, linv, m, 0, 1)
+        dqkvs.append(dqkv)
+        bias_sums.append(sums)
+    piece, gain_part = qkv_weight_grads(a1, dqkvs, wqkv, 0, 1)
+    flow = quick_scatter(piece)
+    sent = next(flow)
+    ggain1 = jnp.sum(gain_part, axis=1) / gain_attn
+    bias_part = bias_grad(bias_sums[0] + bias_sums[1], buckets)
+    smalls = jnp.concatenate(
+        [ggain1, ggains[0], ggains[1], bias_part.reshape(-1), loss_part[None]]
+    )
+    pad = -smalls.shape[0] % (8 * TILE)
+    smalls = jnp.pad(smalls, (0, pad)).reshape(-1, TILE)
+    if shard % 8 == 0:
+        sent = after(sent, inner)
+        grad_all = lax.psum_scatter(inner, "z", scatter_dimension=0, tiled=True).astype(F32)
+    input_grads = qkv_input_grad(
+        hidden[0, 0], gain1, wqkv, dqkvs[:1], after(backs[0][0], sent), 0, None
+    )
+    sent = flow.send((input_grads,))
+    input_grads = qkv_input_grad(
+        hidden[0, 0], gain1, wqkv, dqkvs[1:], after(backs[1][0], sent), 1, input_grads
+    )
+    flow.send((input_grads,))
+    totals = sum_everywhere(smalls).reshape(-1)
+    flow.send(())
+    grad_qkv = flow.send(()).reshape(shard, 3, width)
     grad_in = jnp.concatenate(
         [grad_all[:, 2 * c * width : (2 * c + 1) * width] for c in range(chunks)], axis=1
     )
@@ -969,38 +1128,13 @@
     grad_wo = grad_all[:, 2 * ff : 2 * ff + width]
     grad_proj = grad_all[:, 2 * ff + width :]
 
-    dqkvs, near_sum, far_sum = [], 0.0, 0.0
-    for m in range(MICRO):
-        glen, info, lens, mixed, probs, linv = slabs[m][:6]
-        at = slice(m * rows, (m + 1) * rows)
-        dqkv, near, far = attention_back(info, qkv[at], mixed, backs[m][1], probs, linv)
-        dqkvs.append(dqkv)
-        near_sum = near_sum + near
-        far_sum = far_sum + far
-    grad_bias = bias_grad(near_sum, far_sum, buckets)
-
-    grad_qkv, gain_part = qkv_weight_grads(a1, *dqkvs, wqkv)
-    grad_qkv = quick_scatter(grad_qkv)
-    ggain1 = jnp.sum(gain_part, axis=1) / gain_attn
-    smalls = jnp.concatenate(
-        [ggain1, ggains[0], ggains[1], grad_bias.reshape(-1), loss_part[None]]
-    )
-    pad = -smalls.shape[0] % (8 * TILE)
-    totals = sum_everywhere(jnp.pad(smalls, (0, pad)).reshape(-1, TILE)).reshape(-1)
-    input_grads = None
-    for m in range(MICRO):
-        input_grads = qkv_input_grad(
-            hidden[0, 0], gain1, wqkv, dqkvs[m], backs[m][0], m, input_grads
-        )
-
-    outputs = jnp.stack([slab[-2] for slab in slabs])
     return (
-        outputs[None, None],
+        out.reshape(hidden.shape),
         input_grads[None, None],
         totals[3 * width + buckets * heads] / (dp_count * slots * MICRO),
-        grad_qkv[:, :width],
-        grad_qkv[:, width : 2 * width],
-        grad_qkv[:, 2 * width :],
+        grad_qkv[:, 0],
+        grad_qkv[:, 1],
+        grad_qkv[:, 2],
         grad_wo,
         grad_in,
         grad_out,

time: 564 us -> 476 us (0.84)
  starting transfers between devices: 91.8 us -> 63.2 us
  Pallas kernels: 256 us -> 233 us
  local copies, waits for them, and re-layouts: 67.1 us -> 50.4 us
  other arithmetic: 30.1 us -> 17.6 us
    ppermute x8 -> x3, starting transfers between devices: 49.3 us -> 3.74 us  [quick_scatter(): lax.ppermute(part, 'z', [(j, (j + k) % count) for j in range(count)])]
    pallas_call x2 -> x1, Pallas kernels: 52.3 us -> 22.7 us  [attention(): pl.pallas_call(attn_fwd_kernel, grid_spec=pltpu.PrefetchScalarGridSpec(nu...]
    ppermute x12 -> x11, waiting for transfers between devices: 40.5 us -> 18.5 us  [swap(): return lax.ppermute(x, axis, [(0, 1), (1, 0)])]
    all_to_all x1 -> x2, starting transfers between devices: 23 us -> 37.8 us  [the longest x1 26.9 us: sum_everywhere(): return jnp.sum(lax.all_to_all(sent, AXES, 0, 0, tiled=True), axis=0)]
    all_gather x1, waiting for transfers between devices: 0.01 us -> 12.6 us  [per_device(): lax.all_gather(jnp.concatenate(pieces + [w_attn_out, w_proj], axis=1), AX...]
    squeeze x8 -> x5, local copies, waits for them, and re-layouts: 10.2 us -> 0.22 us  [the longest x4 0.14 us: send_half(): lax.dynamic_index_in_dim(x, 1 - me, dim, keepdims=False)]
    slice x6 -> x5, local copies, waits for them, and re-layouts: 9.52 us -> 0.45 us  [the longest x1 0.15 us: per_device(): grad_qkv[:, 2]]
    pallas_call x2 -> x3, Pallas kernels: 75.6 us -> 83.3 us  [the longest x2 76.2 us: ffn_backward(): pl.pallas_call(ffn_bwd_kernel(slab, order), grid_spec=pltpu.PrefetchScala...]
  transfers between devices with their start and end apart: 28 -> 23, of which waited for: 17 -> 16; matrix products, arithmetic and copies ran while one was open for 10% -> 8% of each run, Pallas kernels for 24% -> 25%
where the time goes in v2:
time: 476 us; the launch traced here: 470 us
  Pallas kernels  233 us (49%)
  waiting for transfers between devices  78.4 us (16%)
  starting transfers between devices  63.2 us (13%)
  local copies, waits for them, and re-layouts  50.4 us (11%)
  between operations  19 us (4%)
  other arithmetic  17.6 us (4%)
  matrix products  8.9 us (2%)
    pallas_call x2, Pallas kernels, ffn_backward(): pl.pallas_call(ffn_bwd_kernel(slab, order), grid_spec=pltpu.PrefetchScala...  76.2 us
    pallas_call x2, Pallas kernels, attention_back(): pl.pallas_call(attn_bwd_kernel, grid_spec=pltpu.PrefetchScalarGridSpec(nu...  49.9 us
    pallas_call x1, Pallas kernels, ffn_forward(): pl.pallas_call(ffn_fwd_kernel, grid_spec=pltpu.PrefetchScalarGridSpec(num...  40.2 us
    all_to_all x1, starting transfers between devices, sum_everywhere(): return jnp.sum(lax.all_to_all(sent, AXES, 0, 0, tiled=True), axis=0)  26.9 us
    unnamed x98, local copies, waits for them, and re-layouts  23.5 us
    pallas_call x1, Pallas kernels, attention(): pl.pallas_call(attn_fwd_kernel, grid_spec=pltpu.PrefetchScalarGridSpec(nu...  22.7 us
    ppermute x11, waiting for transfers between devices, swap(): return lax.ppermute(x, axis, [(0, 1), (1, 0)])  18.5 us
    ppermute x3, waiting for transfers between devices, quick_scatter(): lax.ppermute(part, 'z', [(j, (j + k) % count) for j in range(count)])  18 us
  transfers between devices with their start and end apart: 23, of which 16 were waited for; matrix products, arithmetic and copies ran while one was open for 8% of the time, Pallas kernels for 25%

profile of v2, /device:TPU:0, one launch (start us, length us, event | category | flops | bytes accessed | tf_op | source)
XLA Modules:
  0.0 470.5 jit_solution(15258364930653271020)
XLA Ops:
  13.5 3.0 collective-permute-start.1
  16.5 2.6 collective-permute-start.2
  22.4 4.2 collective-permute-done.2
  30.1 3.5 collective-permute-done.4
  39.3 7.1 %bias_tables.1.t_ref = f32[12,3,128,128]{3,2,1,0:T(8,128)} custom-call(f32[12,3,256]{2,1,0:T(4,128)} %reshape.245.x_ref), custom_call_target="tpu_custom_call" | custom-call | tf_op jit(solution)/shard_map/bias_tables/pallas_call | solution.py:817
  47.6 5.2 %collective-permute-done.7 = bf16[2,4,2,24,640]{4,3,2,1,0:T(8,128)(2,1)S(1)} collective-permute-done((bf16[2,4,2,24,640]{4,3,2,1,0:T(8,128)(2,1)S(1)}, bf16[2,4,2,24,640]{4,3,2,1,0:T(8,128)(2,1)S(1)}, u32[]{:S(2)}, u32[]{:S(2)}) %collective-permute-start.7) | collective-permute-done | bytes 491552 | tf_op jit(solution)/shard_map/ppermute | solution.py:861
  54.3 2.6 collective-permute-done.8
  58.0 2.8 copy-done.3
  60.8 12.0 %norm_qkv.1 = (bf16[2048,768]{1,0:T(8,128)(2,1)S(1)}, bf16[2048,2304]{1,0:T(8,128)(2,1)}, f32[8,8,128]{2,1,0:T(8,128)S(1)}) custom-call(bf16[2048,768]{1,0:T(8,128)(2,1)S(1)} %bitcast.151, f32[1,768]{1,0:T(1,128)S(1)} %broadcast_in_dim.158.gain_ref.refs_1_, bf16[768,2304]{1,0:T(8,128)(2,1)S(1)} %bitcast.146), custom_call_target="tpu_custom_call" | custom-call | flops 7247757312 | bytes 15728640 | tf_op jit(solution)/shard_map/norm_qkv/pallas_call | solution.py:79
  74.3 2.4 copy-done.9
  76.7 22.7 %attention_forward.1 = (bf16[2048,768]{1,0:T(8,128)(2,1)S(1)}, bf16[24,1024,1024]{2,1,0:T(8,128)(2,1)}, f32[12,2,1024]{2,1,0:T(2,128)S(1)}) custom-call(s32[2,19]{1,0:T(2,128)S(1)} %pad_add_fusion.info_ref, bf16[2048,2304]{1,0:T(8,128)(2,1)} %get-tuple-element.46.q_ref.k_ref.v_ref, bf16[2048,2304]{1,0:T(8,128)(2,1)} %get-tuple-element.46.q_ref.k_ref.v_ref, ...), custom_call_target="tpu_custom_call" | custom-call | flops 12884901888 | bytes 50331648 | tf_op jit(solution)/shard_map/attention_forward/pallas_call | solution.py:244
  101.7 12.6 %all-gather.2.cloned.1.call-done.w_ref.refs_9_ = bf16[768,7680]{1,0:T(8,128)(2,1)} async-done(((bf16[24,7680]{1,0:T(8,128)(2,1)}), bf16[768,7680]{1,0:T(8,128)(2,1)}) %all-gather.2.cloned.1.call-update) | async-done | bytes 11796496 | tf_op jit(solution)/shard_map/all_gather | solution.py:1004
  114.2 40.2 %ffn_forward.1 = (f32[2048,768]{1,0:T(8,128)}, bf16[2048,768]{1,0:T(8,128)(2,1)}, bf16[2048,3072]{1,0:T(8,128)(2,1)}, bf16[2048,3072]{1,0:T(8,128)(2,1)}, f32[20...) custom-call(s32[32]{0:T(128)} %broadcast_select_fusion.4.glen_ref.refs_0_, ...), custom_call_target="tpu_custom_call" | custom-call | flops 21743271936 | bytes 62914560 | tf_op jit(solution)/shard_map/ffn_forward/pallas_call | solution.py:509
  158.9 10.9 %all-to-all-start = ((bf16[32,12,128]{2,1,0:T(8,128)(2,1)}), bf16[32,12,128]{2,1,0:T(8,128)(2,1)S(1)}, u32[]{:S(2)}, u32[]{:S(2)}) async-start(bf16[32,12,128]{2,1,0:T(8,128)(2,1)} %broadcast_in_dim.180), calls=%async_computation | async-start | bytes 262144 | tf_op jit(solution)/shard_map/all_to_all | solution.py:1036
  169.9 8.2 %all-to-all-done = bf16[32,12,128]{2,1,0:T(8,128)(2,1)S(1)} async-done(((bf16[32,12,128]{2,1,0:T(8,128)(2,1)}), bf16[32,12,128]{2,1,0:T(8,128)(2,1)S(1)}, u32[]{:S(2)}, u32[]{:S(2)}) %all-to-all-start) | async-done | bytes 98336 | tf_op jit(solution)/shard_map/all_to_all | solution.py:1036
  180.0 2.6 all-to-all-start.1
  182.6 8.9 %all-to-all-done.1 = f32[32,2,768]{2,1,0:T(2,128)S(1)} async-done(((f32[32,2,768]{2,1,0:T(2,128)}), f32[32,2,768]{2,1,0:T(2,128)S(1)}, u32[]{:S(2)}, u32[]{:S(2)}) %all-to-all-start.1) | async-done | bytes 196640 | tf_op jit(solution)/shard_map/all_to_all | solution.py:1055
  197.1 37.5 %ffn_backward.2 = (f32[768,7680]{1,0:T(8,128)}, f32[1024,768]{1,0:T(8,128)}, bf16[1024,768]{1,0:T(8,128)(2,1)}, f32[2,768]{1,0:T(2,128)}) custom-call(s32[32]{0:T(128)} %broadcast_select_fusion.4.glen_ref.refs_0_, f32[2048,768]{1,0:T(8,128)} %get-tuple-element.49.refs_1_, bf16[2,1024,768]{2,1,0:T(8,128)(2,1)} %bitcast.157, ...), custom_call_target="tpu_custom_call" | custom-call | flops 21743271936 | bytes 47185920 | tf_op jit(solution)/shard_map/ffn_backward/pallas_call | solution.py:680
  234.7 38.6 %ffn_backward.3 = (bf16[768,7680]{1,0:T(8,128)(2,1)}, f32[1024,768]{1,0:T(8,128)}, bf16[1024,768]{1,0:T(8,128)(2,1)}, f32[2,768]{1,0:T(2,128)}) custom-call(s32[32]{0:T(128)} %broadcast_select_fusion.4.glen_ref.refs_0_, f32[2048,768]{1,0:T(8,128)} %get-tuple-element.49.refs_1_, bf16[2,1024,768]{2,1,0:T(8,128)(2,1)} %bitcast.158, ...), custom_call_target="tpu_custom_call" | custom-call | flops 21743271936 | bytes 47185920 | tf_op jit(solution)/shard_map/ffn_backward/pallas_call | solution.py:680
  274.5 25.9 %attention_backward.2 = (bf16[3,1024,768]{2,1,0:T(8,128)(2,1)}, f32[12,8,256]{2,1,0:T(8,128)}) custom-call(s32[2,19]{1,0:T(2,128)} %copy-done.12, bf16[2048,2304]{1,0:T(8,128)(2,1)} %get-tuple-element.46.q_ref.k_ref.v_ref, bf16[2048,2304]{1,0:T(8,128)(2,1)} %get-tuple-element.46.q_ref.k_ref.v_ref, bf16[2048,2304]{1,0:T(8,128)(2,1)} %get-tuple-element.46.q_ref.k_ref.v_ref, ...), custom_call_target="tpu_custom_call" | custom-call | flops 12884901888 | bytes 25165824 | tf_op jit(solution)/shard_map/attention_backward/pallas_call | solution.py:412
  300.4 24.1 %attention_backward.3 = (bf16[3,1024,768]{2,1,0:T(8,128)(2,1)}, f32[12,8,256]{2,1,0:T(8,128)}) custom-call(s32[2,19]{1,0:T(2,128)} %copy-done.12, bf16[2048,2304]{1,0:T(8,128)(2,1)} %get-tuple-element.46.q_ref.k_ref.v_ref, bf16[2048,2304]{1,0:T(8,128)(2,1)} %get-tuple-element.46.q_ref.k_ref.v_ref, bf16[2048,2304]{1,0:T(8,128)(2,1)} %get-tuple-element.46.q_ref.k_ref.v_ref, ...), custom_call_target="tpu_custom_call" | custom-call | flops 12884901888 | bytes 25165824 | tf_op jit(solution)/shard_map/attention_backward/pallas_call | solution.py:412
  324.5 11.4 %qkv_weight_grads.1 = (bf16[768,2304]{1,0:T(8,128)(2,1)}, f32[768,128]{1,0:T(8,128)S(1)}) custom-call(bf16[2048,768]{1,0:T(8,128)(2,1)S(1)} %get-tuple-element.57.a1_ref, bf16[3,1024,768]{2,1,0:T(8,128)(2,1)} %get-tuple-element.61.d0_ref.refs_0_, bf16[3,1024,768]{2,1,0:T(8,128)(2,1)} %get-tuple-element.63.d1_ref.refs_4_, bf16[768,2304]{1,0:T(8,128)(2,1)} %bitcast.147), custom_call_target="tpu_custom_call" | custom-call | flops 7247757312 | bytes 15728640 | tf_op jit(solution)/shard_map/qkv_weight_grads/pallas_call | solution.py:733
  335.8 3.6 constant_dynamic-slice_fusion.1
  357.3 26.9 %all-to-all-start.2 = ((f32[32,24,128]{2,1,0:T(8,128)}), f32[32,24,128]{2,1,0:T(8,128)}, u32[]{:S(2)}, u32[]{:S(2)}) async-start(f32[32,24,128]{2,1,0:T(8,128)} %broadcast_in_dim.192), calls=%async_computation.2 | async-start | bytes 786432 | tf_op jit(solution)/shard_map/all_to_all | solution.py:962
  390.4 6.9 %qkv_input_grad.2.refs_5_ = f32[2,1024,768]{2,1,0:T(8,128)} custom-call(bf16[2,1024,768]{2,1,0:T(8,128)(2,1)S(1)} %bitcast.152, f32[1,768]{1,0:T(1,128)S(1)} %broadcast_in_dim.158.gain_ref.refs_1_, bf16[768,2304]{1,0:T(8,128)(2,1)S(1)} %bitcast.148, f32[1024,768]{1,0:T(8,128)S(1)} %copy-done.8, bf16[3,1024,768]{2,1,0:T(8,128)(2,1)S(1)} %copy-done.6), custom_call_target="tpu_custom_call" | custom-call | flops 3623878656 | bytes 12582912 | tf_op jit(solution)/shard_map/qkv_input_grad/pallas_call | solution.py:791
  405.1 6.6 %qkv_input_grad.3 = f32[2,1024,768]{2,1,0:T(8,128)} custom-call(bf16[2,1024,768]{2,1,0:T(8,128)(2,1)S(1)} %bitcast.153, f32[1,768]{1,0:T(1,128)S(1)} %broadcast_in_dim.158.gain_ref.refs_1_, bf16[768,2304]{1,0:T(8,128)(2,1)S(1)} %bitcast.149, f32[1024,768]{1,0:T(8,128)S(1)} %copy-done.7, ...), custom_call_target="tpu_custom_call", output_to_operand_aliasing={{}: (5, {})} | custom-call | flops 3623878656 | bytes 12582912 | tf_op jit(solution)/shard_map/qkv_input_grad/pallas_call | solution.py:791
  417.4 2.5 collective-permute-done.11
  422.2 2.7 collective-permute-start.16
  428.5 3.4 collective-permute-done.16
  431.9 14.6 %collective-permute-done.15 = bf16[24,2304]{1,0:T(8,128)(2,1)S(1)} collective-permute-done((bf16[24,2304]{1,0:T(8,128)(2,1)S(1)}, bf16[24,2304]{1,0:T(8,128)(2,1)S(1)}, u32[]{:S(2)}, u32[]{:S(2)}) %collective-permute-start.15) | collective-permute-done | bytes 110624 | tf_op jit(solution)/shard_map/ppermute | solution.py:953
  448.8 6.2 %reduce-scatter.5.cloned.1.call-done = bf16[24,7680]{1,0:T(8,128)(2,1)} async-done(((bf16[96,7680]{1,0:T(8,128)(2,1)}), bf16[24,7680]{1,0:T(8,128)(2,1)}) %reduce-scatter.5.cloned.1.call-update) | async-done | bytes 368656 | tf_op jit(solution)/shard_map/reduce_scatter | solution.py:1109
  459.0 2.6 reshape.256
  (252 shorter events, 86.7 us)
Async XLA Ops:
  7.3 107.0 %all-gather.2.cloned.1.call-start = ((), (), s32[]{:S(2)}) async-start(), calls=%async_computation.5 | async-start | bytes 12165120 | tf_op jit(solution)/shard_map/all_gather | solution.py:1004
  11.9 1.5 collective-permute-start
  13.3 23.6 %copy-start.20 = (f32[32,12]{0,1:T(8,128)S(1)}, f32[32,12]{0,1:T(8,128)}, u32[]{:S(2)}) copy-start(f32[32,12]{0,1:T(8,128)} %param.29) | copy-start | bytes 4612
  13.3 24.4 %copy-start.26 = (f32[768]{0:T(1024)S(1)}, f32[768]{0:T(1024)}, u32[]{:S(2)}) copy-start(f32[768]{0:T(1024)} %param.26) | copy-start | bytes 9220
  13.5 9.0 %collective-permute-start.1 = (bf16[2,24,1152]{2,1,0:T(8,128)(2,1)S(1)}, bf16[2,24,1152]{2,1,0:T(8,128)(2,1)S(1)}, u32[]{:S(2)}, u32[]{:S(2)}) collective-permute-start(bf16[2,24,1152]{2,1,0:T(8,128)(2,1)S(1)} %get-tuple-element.127), channel_id=1, source_target_pairs={{0,4},{4,8},{8,12},{12,0},{1,5},{5,9},{9,13},{13,1},{2,6},{6,10},{... | collective-permute-start | bytes 331784 | tf_op jit(solution)/shard_map/ppermute | solution.py:878
  16.5 10.2 %collective-permute-start.2 = (bf16[2,24,1152]{2,1,0:T(8,128)(2,1)S(1)}, bf16[2,24,1152]{2,1,0:T(8,128)(2,1)S(1)}, u32[]{:S(2)}, u32[]{:S(2)}) collective-permute-start(bf16[2,24,1152]{2,1,0:T(8,128)(2,1)S(1)} %get-tuple-element.127), channel_id=1, source_target_pairs={{0,8},{4,12},{8,0},{12,4},{1,9},{5,13},{9,1},{13,5},{2,10},{6,14},... | collective-permute-start | bytes 331784 | tf_op jit(solution)/shard_map/ppermute | solution.py:878
  19.1 7.7 %collective-permute-start.3 = (bf16[2,24,1152]{2,1,0:T(8,128)(2,1)S(1)}, bf16[2,24,1152]{2,1,0:T(8,128)(2,1)S(1)}, u32[]{:S(2)}, u32[]{:S(2)}) collective-permute-start(bf16[2,24,1152]{2,1,0:T(8,128)(2,1)S(1)} %get-tuple-element.127), channel_id=1, source_target_pairs={{0,12},{4,0},{8,4},{12,8},{1,13},{5,1},{9,5},{13,9},{2,14},{6,2},{... | collective-permute-start | bytes 331784 | tf_op jit(solution)/shard_map/ppermute | solution.py:878
  26.8 6.8 %collective-permute-start.4 = (bf16[4,2,24,512]{3,2,1,0:T(8,128)(2,1)S(1)}, bf16[4,2,24,512]{3,2,1,0:T(8,128)(2,1)S(1)}, u32[]{:S(2)}, u32[]{:S(2)}) collective-permute-start(bf16[4,2,24,512]{3,2,1,0:T(8,128)(2,1)S(1)} %slice.200), channel_id=1, source_target_pairs={{0,2},{2,0},{1,3},{3,1},{4,6},{6,4},{5,7},{7,5},{8,10},{10,8},{9,1... | collective-permute-start | bytes 589832 | tf_op jit(solution)/shard_map/ppermute | solution.py:861
  28.5 17.9 %copy-start.34 = (f32[768]{0:T(1024)S(1)}, f32[768]{0:T(1024)}, u32[]{:S(2)}) copy-start(f32[768]{0:T(1024)} %param.27) | copy-start | bytes 9220
  28.5 18.5 %copy-start.35 = (f32[768]{0:T(1024)S(1)}, f32[768]{0:T(1024)}, u32[]{:S(2)}) copy-start(f32[768]{0:T(1024)} %param.28) | copy-start | bytes 9220
  28.5 8.1 %collective-permute-start.6 = (bf16[4,2,24,640]{3,2,1,0:T(8,128)(2,1)S(1)}, bf16[4,2,24,640]{3,2,1,0:T(8,128)(2,1)S(1)}, u32[]{:S(2)}, u32[]{:S(2)}) collective-permute-start(bf16[4,2,24,640]{3,2,1,0:T(8,128)(2,1)S(1)} %slice.201), channel_id=1, source_target_pairs={{0,16},{16,0},{1,17},{17,1},{2,18},{18,2},{3,19},{19,3},{4,20},{20... | collective-permute-start | bytes 737288 | tf_op jit(solution)/shard_map/ppermute | solution.py:861
  33.6 13.9 %collective-permute-start.5 = (bf16[2,4,2,24,512]{4,3,2,1,0:T(8,128)(2,1)S(1)}, bf16[2,4,2,24,512]{4,3,2,1,0:T(8,128)(2,1)S(1)}, u32[]{:S(2)}, u32[]{:S(2)}) collective-permute-start(bf16[2,4,2,24,512]{4,3,2,1,0:T(8,128)(2,1)S(1)} %pad_maximum_fusion.4), channel_id=1, source_target_pairs={{0,16},{16,0},{1,17},{17,1},{2,18},{18,2},{3,19},{19,3},{4,20},{20... | collective-permute-start | bytes 1179656 | tf_op jit(solution)/shard_map/ppermute | solution.py:861
  36.7 16.1 %collective-permute-start.7 = (bf16[2,4,2,24,640]{4,3,2,1,0:T(8,128)(2,1)S(1)}, bf16[2,4,2,24,640]{4,3,2,1,0:T(8,128)(2,1)S(1)}, u32[]{:S(2)}, u32[]{:S(2)}) collective-permute-start(bf16[2,4,2,24,640]{4,3,2,1,0:T(8,128)(2,1)S(1)} %pad_maximum_fusion.3), channel_id=1, source_target_pairs={{0,2},{2,0},{1,3},{3,1},{4,6},{6,4},{5,7},{7,5},{8,10},{10,8},{9,1... | collective-permute-start | bytes 1474568 | tf_op jit(solution)/shard_map/ppermute | solution.py:861
  53.1 3.8 collective-permute-start.8
  54.0 101.4 %copy-start.32 = (f32[2,16]{1,0:T(2,128)}, f32[2,16]{1,0:T(2,128)S(1)}, u32[]{:S(2)}) copy-start(f32[2,16]{1,0:T(2,128)S(1)} %convert_maximum_fusion) | copy-start | bytes 388
  74.3 25.1 %copy-start.12 = (s32[2,19]{1,0:T(2,128)}, s32[2,19]{1,0:T(2,128)S(1)}, u32[]{:S(2)}) copy-start(s32[2,19]{1,0:T(2,128)S(1)} %pad_add_fusion.info_ref) | copy-start | bytes 460
  114.2 64.1 %copy-start.30 = (s32[2,1,16]{2,1,0:T(1,128)S(1)}, s32[2,1,16]{2,1,0:T(1,128)}, u32[]{:S(2)}) copy-start(s32[2,1,16]{2,1,0:T(1,128)} %param.17) | copy-start | bytes 388
  158.9 19.2 %all-to-all-start = ((bf16[32,12,128]{2,1,0:T(8,128)(2,1)}), bf16[32,12,128]{2,1,0:T(8,128)(2,1)S(1)}, u32[]{:S(2)}, u32[]{:S(2)}) async-start(bf16[32,12,128]{2,1,0:T(8,128)(2,1)} %broadcast_in_dim.180), calls=%async_computation | async-start | bytes 262144 | tf_op jit(solution)/shard_map/all_to_all | solution.py:1036
  179.1 15.5 %copy-start.33 = (f32[2,16]{1,0:T(2,128)S(1)}, f32[2,16]{1,0:T(2,128)}, u32[]{:S(2)}) copy-start(f32[2,16]{1,0:T(2,128)} %copy-done.32) | copy-start | bytes 388
  180.0 11.5 %all-to-all-start.1 = ((f32[32,2,768]{2,1,0:T(2,128)}), f32[32,2,768]{2,1,0:T(2,128)S(1)}, u32[]{:S(2)}, u32[]{:S(2)}) async-start(f32[32,2,768]{2,1,0:T(2,128)} %concatenate.42.clone), calls=%async_computation.1 | async-start | bytes 393216 | tf_op jit(solution)/shard_map/all_to_all | solution.py:1055
  182.6 231.6 %reduce-scatter.3.cloned.1.call-start = ((), (), s32[]{:S(2)}) async-start(), calls=%async_computation.6 | async-start | bytes 13271040 | tf_op jit(solution)/shard_map/reduce_scatter | solution.py:1091
  339.4 44.8 %copy-start.1 = (bf16[2,2,4,2,24,2304]{5,4,3,1,2,0:T(8,128)(2,1)S(1)}, bf16[2,2,4,2,24,2304]{5,4,3,1,2,0:T(8,128)(2,1)}, u32[]{:S(2)}) copy-start(bf16[2,2,4,2,24,2304]{5,4,3,1,2,0:T(8,128)(2,1)} %copy-done) | copy-start | bytes 10616836
  340.8 56.5 %collective-permute-start.9 = (bf16[2,4,2,24,2304]{4,3,1,0,2:T(8,128)(2,1)}, bf16[2,4,2,24,2304]{4,3,1,0,2:T(8,128)(2,1)}, u32[]{:S(2)}, u32[]{:S(2)}) collective-permute-start(bf16[2,4,2,24,2304]{4,3,1,0,2:T(8,128)(2,1)} %bitcast.140), channel_id=1, source_target_pairs={{0,1},{1,0},{2,3},{3,2},{4,5},{5,4},{6,7},{7,6},{8,9},{9,8},{10,11... | collective-permute-start | bytes 5308424 | tf_op jit(solution)/shard_map/ppermute | solution.py:861
  357.3 59.1 %all-to-all-start.2 = ((f32[32,24,128]{2,1,0:T(8,128)}), f32[32,24,128]{2,1,0:T(8,128)}, u32[]{:S(2)}, u32[]{:S(2)}) async-start(f32[32,24,128]{2,1,0:T(8,128)} %broadcast_in_dim.192), calls=%async_computation.2 | async-start | bytes 786432 | tf_op jit(solution)/shard_map/all_to_all | solution.py:962
  384.2 70.7 %reduce-scatter.5.cloned.1.call-start = ((), (), s32[]{:S(2)}) async-start(), calls=%async_computation.7 | async-start | bytes 1843200 | tf_op jit(solution)/shard_map/reduce_scatter | solution.py:1109
  399.4 13.0 %collective-permute-start.10 = (bf16[4,2,24,1152]{3,2,0,1:T(8,128)(2,1)S(1)}, bf16[4,2,24,1152]{3,2,0,1:T(8,128)(2,1)S(1)}, u32[]{:S(2)}, u32[]{:S(2)}) collective-permute-start(bf16[4,2,24,1152]{3,2,0,1:T(8,128)(2,1)S(1)} %dynamic-slice_bitcast_fusion.1), channel_id=1, source_target_pairs={{0,16},{16,0},{1,17},{17,1},{2,18},{18,2},{3,19},{19,3},{4,20},{20... | collective-permute-start | bytes 1327112 | tf_op jit(solution)/shard_map/ppermute | solution.py:861
  401.8 12.4 %collective-permute-start.12 = (bf16[2,4,24,1152]{3,2,1,0:T(8,128)(2,1)S(1)}, bf16[2,4,24,1152]{3,2,1,0:T(8,128)(2,1)}, u32[]{:S(2)}, u32[]{:S(2)}) collective-permute-start(bf16[2,4,24,1152]{3,2,1,0:T(8,128)(2,1)S(1)} %dynamic-slice_bitcast_fusion), channel_id=1, source_target_pairs={{0,2},{2,0},{1,3},{3,1},{4,6},{6,4},{5,7},{7,5},{8,10},{10,8},{9,1... | collective-permute-start | bytes 1327112 | tf_op jit(solution)/shard_map/ppermute | solution.py:861
  412.6 7.3 %collective-permute-start.11 = (bf16[4,24,1152]{2,1,0:T(8,128)(2,1)S(1)}, bf16[4,24,1152]{2,1,0:T(8,128)(2,1)S(1)}, u32[]{:S(2)}, u32[]{:S(2)}) collective-permute-start(bf16[4,24,1152]{2,1,0:T(8,128)(2,1)S(1)} %dynamic-slice_bitcast_fusion.3), channel_id=1, source_target_pairs={{0,2},{2,0},{1,3},{3,1},{4,6},{6,4},{5,7},{7,5},{8,10},{10,8},{9,1... | collective-permute-start | bytes 663560 | tf_op jit(solution)/shard_map/ppermute | solution.py:861
  415.3 6.7 %collective-permute-start.13 = (bf16[4,24,1152]{2,1,0:T(8,128)(2,1)S(1)}, bf16[4,24,1152]{2,1,0:T(8,128)(2,1)S(1)}, u32[]{:S(2)}, u32[]{:S(2)}) collective-permute-start(bf16[4,24,1152]{2,1,0:T(8,128)(2,1)S(1)} %dynamic-slice_bitcast_fusion.2), channel_id=1, source_target_pairs={{0,16},{16,0},{1,17},{17,1},{2,18},{18,2},{3,19},{19,3},{4,20},{20... | collective-permute-start | bytes 663560 | tf_op jit(solution)/shard_map/ppermute | solution.py:861
  422.2 9.7 %collective-permute-start.16 = (bf16[24,2304]{1,0:T(8,128)(2,1)S(1)}, bf16[24,2304]{1,0:T(8,128)(2,1)S(1)}, u32[]{:S(2)}, u32[]{:S(2)}) collective-permute-start(bf16[24,2304]{1,0:T(8,128)(2,1)S(1)} %get-tuple-element.144), channel_id=1, source_target_pairs={{0,12},{4,0},{8,4},{12,8},{1,13},{5,1},{9,5},{13,9},{2,14},{6,2},{... | collective-permute-start | bytes 331784 | tf_op jit(solution)/shard_map/ppermute | solution.py:953
  424.9 21.6 %collective-permute-start.15 = (bf16[24,2304]{1,0:T(8,128)(2,1)S(1)}, bf16[24,2304]{1,0:T(8,128)(2,1)S(1)}, u32[]{:S(2)}, u32[]{:S(2)}) collective-permute-start(bf16[24,2304]{1,0:T(8,128)(2,1)S(1)} %get-tuple-element.143), channel_id=1, source_target_pairs={{0,8},{4,12},{8,0},{12,4},{1,9},{5,13},{9,1},{13,5},{2,10},{6,14},... | collective-permute-start | bytes 331784 | tf_op jit(solution)/shard_map/ppermute | solution.py:953
  424.9 21.6 %collective-permute-start.14 = (bf16[24,2304]{1,0:T(8,128)(2,1)S(1)}, bf16[24,2304]{1,0:T(8,128)(2,1)S(1)}, u32[]{:S(2)}, u32[]{:S(2)}) collective-permute-start(bf16[24,2304]{1,0:T(8,128)(2,1)S(1)} %get-tuple-element.142), channel_id=1, source_target_pairs={{0,4},{4,8},{8,12},{12,0},{1,5},{5,9},{9,13},{13,1},{2,6},{6,10},{... | collective-permute-start | bytes 331784 | tf_op jit(solution)/shard_map/ppermute | solution.py:953
  (29 other events, 106.6 us)
Sparse Core Ops, SparseCore 0:
  11.9 102.2 all-gather.1
  273.5 86.0 reduce-scatter.2
  414.3 40.6 reduce-scatter.4

commit v3 on v2

--- a/solution.py
+++ b/solution.py
@@ -53,7 +53,7 @@
     return bucket + 16 * (offset > 0).astype(jnp.int32)
 
 
-def qkv_kernel(x_ref, gain_ref, w_ref, a1_ref, qkv_ref, norm_ref):
+def qkv_kernel(room_ref, x_ref, gain_ref, w_ref, a1_ref, qkv_ref, small_ref, norm_scr):
     x = x_ref[...].astype(F32)
     r = lax.rsqrt(jnp.mean(x * x, axis=-1, keepdims=True) + 1e-06)
     a1 = (x * r * gain_ref[...]).astype(BF)
@@ -62,7 +62,11 @@
     row = lax.broadcasted_iota(jnp.int32, (width, TILE), 0)
     col = lax.broadcasted_iota(jnp.int32, (width, TILE), 1)
     of_head = jnp.where(row // GROUP == col, 1.0, 0.0).astype(BF)
-    norm_ref[...] = jnp.zeros(norm_ref.shape, F32)
+
+    @pl.when(pl.program_id(0) == 0)
+    def _():
+        norm_scr[...] = jnp.zeros(norm_scr.shape, F32)
+
     for part in range(3):
         out = mm(a1, w_ref[:, part * width : (part + 1) * width]).astype(BF)
         if part == 0:
@@ -70,16 +74,26 @@
         qkv_ref[:, part * width : (part + 1) * width] = out
         if part < 2:
             square = mm(out * out, of_head)
-            norm_ref[0, part : part + 1, :] = jnp.max(square, axis=0, keepdims=True)
-
-
-def project_qkv(x, gain, w):
+            at = slice(part, part + 1)
+            norm_scr[at, :] = jnp.maximum(
+                norm_scr[at, :], jnp.max(square, axis=0, keepdims=True)
+            )
+
+    @pl.when(pl.program_id(0) == pl.num_programs(0) - 1)
+    def _():
+        reach = jnp.max(norm_scr[0:1, :] * norm_scr[1:2, :]) * 1.05
+        room = room_ref[0, 0]
+        small_ref[0, 0] = (reach <= room * room).astype(jnp.int32)
+
+
+def project_qkv(room, x, gain, w):
     rows, width = x.shape
-    block = 256
+    block = 512
     return pl.pallas_call(
         qkv_kernel,
         grid=(rows // block,),
         in_specs=[
+            pl.BlockSpec((1, 1), lambda i: (0, 0), memory_space=pltpu.SMEM),
             pl.BlockSpec((block, width), lambda i: (i, 0)),
             fixed((1, width)),
             fixed(w.shape),
@@ -87,17 +101,18 @@
         out_specs=[
             pl.BlockSpec((block, width), lambda i: (i, 0)),
             pl.BlockSpec((block, 3 * width), lambda i: (i, 0)),
-            pl.BlockSpec((1, 8, TILE), lambda i: (i, 0, 0)),
+            pl.BlockSpec((1, 1), lambda i: (0, 0), memory_space=pltpu.SMEM),
         ],
         out_shape=[
             jax.ShapeDtypeStruct((rows, width), BF),
             jax.ShapeDtypeStruct((rows, 3 * width), BF),
-            jax.ShapeDtypeStruct((rows // block, 8, TILE), F32),
+            jax.ShapeDtypeStruct((1, 1), jnp.int32),
         ],
-        compiler_params=params(40),
+        scratch_shapes=[pltpu.VMEM((8, TILE), F32)],
+        compiler_params=params(60),
         cost_estimate=cost(6 * rows * width * width, rows * width * 10),
         name="norm_qkv",
-    )(x, gain, w)
+    )(room, x, gain, w)
 
 
 def lane_half(shape, head):
@@ -121,13 +136,13 @@
     good = jnp.zeros((TILE, TILE), jnp.bool_)
     for s in range(per):
         low = s * GROUP
-        inside = (row >= low) & (row < low + info_ref[slab, 3 + tile * per + s])
+        inside = (row >= low) & (row < low + info_ref[slab, 2 + tile * per + s])
         good = good | (inside & (col >= low) & (col < low + GROUP))
     return good
 
 
 def attn_fwd_kernel(
-    info_ref, q_ref, k_ref, v_ref, eq_ref, t_ref, o_ref, p_ref, linv_ref, s_scr, ot_scr
+    info_ref, small_ref, q_ref, k_ref, v_ref, eq_ref, t_ref, o_ref, p_ref, linv_ref, s_scr, ot_scr
 ):
     rows = q_ref.shape[0]
     tiles = rows // TILE
@@ -162,7 +177,7 @@
 
     slab = pl.program_id(0)
     is_doc = info_ref[slab, 0] == 1
-    small = info_ref[slab, 2] == 1
+    small = small_ref[0, 0] == 1
 
     @pl.when(is_doc & small)
     def _():
@@ -236,7 +251,7 @@
     o_ref[...] = ot_scr[...].T.astype(BF)
 
 
-def attention(info, qkv, tags, near, heads):
+def attention(info, small, qkv, tags, near, heads):
     slabs = info.shape[0]
     rows = qkv.shape[0] // slabs
     width = qkv.shape[1] // 3
@@ -244,19 +259,19 @@
     return pl.pallas_call(
         attn_fwd_kernel,
         grid_spec=pltpu.PrefetchScalarGridSpec(
-            num_scalar_prefetch=1,
+            num_scalar_prefetch=2,
             grid=(slabs, pairs),
             in_specs=[
-                pl.BlockSpec((rows, TILE), lambda s, i, _: (s, i)),
-                pl.BlockSpec((rows, TILE), lambda s, i, _: (s, pairs + i)),
-                pl.BlockSpec((rows, TILE), lambda s, i, _: (s, 2 * pairs + i)),
-                pl.BlockSpec((2,) + tags.shape[1:], lambda s, i, _: (i, 0, 0)),
-                pl.BlockSpec((2,) + near.shape[1:], lambda s, i, _: (i, 0, 0, 0)),
+                pl.BlockSpec((rows, TILE), lambda s, i, *_: (s, i)),
+                pl.BlockSpec((rows, TILE), lambda s, i, *_: (s, pairs + i)),
+                pl.BlockSpec((rows, TILE), lambda s, i, *_: (s, 2 * pairs + i)),
+                pl.BlockSpec((2,) + tags.shape[1:], lambda s, i, *_: (i, 0, 0)),
+                pl.BlockSpec((2,) + near.shape[1:], lambda s, i, *_: (i, 0, 0, 0)),
             ],
             out_specs=[
-                pl.BlockSpec((rows, TILE), lambda s, i, _: (s, i)),
-                pl.BlockSpec((2, rows, rows), lambda s, i, _: (s * pairs + i, 0, 0)),
-                pl.BlockSpec((1, 2, rows), lambda s, i, _: (s * pairs + i, 0, 0)),
+                pl.BlockSpec((rows, TILE), lambda s, i, *_: (s, i)),
+                pl.BlockSpec((2, rows, rows), lambda s, i, *_: (s * pairs + i, 0, 0)),
+                pl.BlockSpec((1, 2, rows), lambda s, i, *_: (s * pairs + i, 0, 0)),
             ],
             scratch_shapes=[pltpu.VMEM((rows, WIDE), F32), pltpu.VMEM((TILE, rows), F32)],
         ),
@@ -265,10 +280,10 @@
             jax.ShapeDtypeStruct((slabs * heads, rows, rows), BF),
             jax.ShapeDtypeStruct((slabs * pairs, 2, rows), F32),
         ],
-        compiler_params=params(48),
+        compiler_params=params(60),
         cost_estimate=cost(slabs * heads * rows * rows * 512, slabs * heads * rows * rows * 2),
         name="attention_forward",
-    )(info, qkv, qkv, qkv, tags, near)
+    )(info, small, qkv, qkv, qkv, tags, near)
 
 
 def attn_bwd_kernel(
@@ -437,7 +452,7 @@
             jax.ShapeDtypeStruct((3, rows, count * TILE), BF),
             jax.ShapeDtypeStruct((heads, 8, 2 * TILE), F32),
         ],
-        compiler_params=params(56),
+        compiler_params=params(60),
         cost_estimate=cost(heads * rows * rows * 1024, heads * rows * rows * 2),
         name="attention_backward",
     )(info, qkv, qkv, qkv, mixed, d_mixed, probs, linv)
@@ -537,7 +552,7 @@
             jax.ShapeDtypeStruct((rows, width), BF),
             jax.ShapeDtypeStruct((rows // block, groups, width), F32),
         ],
-        compiler_params=params(56),
+        compiler_params=params(60),
         cost_estimate=cost(2 * rows * width * (width + 2 * ff), rows * width * 40),
         name="ffn_forward",
     )(glen, x, mixed, w_all, gain2, gain3)
@@ -584,8 +599,19 @@
             dy2_scr,
             da2_scr,
             dpre_scr,
+            x1_scr,
+            a2_scr,
+            mixed_scr,
+            sems,
         ) = rest
         rows, width = x2_ref.shape
+        mine = pl.ds(slab * rows, rows)
+        later = [
+            pltpu.make_async_copy(hbm.at[mine], scr, sems.at[n])
+            for n, (hbm, scr) in enumerate(
+                ((a2_ref, a2_scr), (x1_ref, x1_scr), (mixed_ref, mixed_scr))
+            )
+        ]
         step = pl.program_id(0)
         last = pl.num_programs(0) - 1
         block = 256
@@ -602,6 +628,8 @@
 
         @pl.when(step == 0)
         def _():
+            for copy in later:
+                copy.start()
             gain = jnp.zeros((1, width), F32)
             for b in range(rows // block):
                 at = slice(b * block, (b + 1) * block)
@@ -621,27 +649,30 @@
                 dy2_scr[at, :] = dx.astype(BF)
             ggain_ref[1:2, :] = gain
             da2_scr[...] = jnp.zeros_like(da2_scr)
+            later[0].wait()
 
         @pl.when(step < last)
         def _():
             dact = mm(dy2_scr[...], w_ref[:, right], NT)
             dpre_scr[...] = (dact * slope_ref[...].astype(F32)).astype(BF)
             put(right, mm(act_ref[...], dy2_scr[...], TN))
-            put(left, mm(a2_ref[...], dpre_scr[...], TN))
+            put(left, mm(a2_scr[...], dpre_scr[...], TN))
             da2_scr[...] = da2_scr[...] + mm(dpre_scr[...], w_ref[:, left], NT)
 
         @pl.when(step == last)
         def _():
+            later[1].wait()
+            later[2].wait()
             gain = jnp.zeros((1, width), F32)
             for b in range(rows // block):
                 at = slice(b * block, (b + 1) * block)
-                dx, d_gain = norm_back(x1_ref[at, :], gain2_ref[...], da2_scr[at, :])
+                dx, d_gain = norm_back(x1_scr[at, :], gain2_ref[...], da2_scr[at, :])
                 gain = gain + d_gain
                 dx = dx + dx2_scr[at, :]
                 dx1_ref[at, :] = dx
                 dy2_scr[at, :] = dx.astype(BF)
             ggain_ref[0:1, :] = gain
-            put(left, mm(mixed_ref[...], dy2_scr[...], TN))
+            put(left, mm(mixed_scr[...], dy2_scr[...], TN))
             if second:
                 g_ref[:, right] = ordered(gproj_ref[...]).astype(BF)
             dmixed_ref[...] = mm(dy2_scr[...], w_ref[:, left], NT).astype(BF)
@@ -664,9 +695,9 @@
         mine,
         pl.BlockSpec((None, rows, width), lambda i, _: (slab, 0, 0), pipeline_mode=once),
         pl.BlockSpec((None,) + dpool.shape[1:], lambda i, _: (slab, 0, 0), pipeline_mode=once),
-        mine,
-        mine,
-        mine,
+        pl.BlockSpec(memory_space=pl.ANY),
+        pl.BlockSpec(memory_space=pl.ANY),
+        pl.BlockSpec(memory_space=pl.ANY),
         side,
         side,
         part,
@@ -694,6 +725,10 @@
                 pltpu.VMEM((rows, width), BF),
                 pltpu.VMEM((rows, width), F32),
                 pltpu.VMEM((rows, width), BF),
+                pltpu.VMEM((rows, width), F32),
+                pltpu.VMEM((rows, width), BF),
+                pltpu.VMEM((rows, width), BF),
+                pltpu.SemaphoreType.DMA((3,)),
             ],
         ),
         out_shape=[
@@ -744,7 +779,7 @@
             jax.ShapeDtypeStruct((width, 3 * cols), BF),
             jax.ShapeDtypeStruct((width, TILE), F32),
         ],
-        compiler_params=params(48),
+        compiler_params=params(60),
         cost_estimate=cost(6 * rows * width * cols, rows * width * 10),
         name="qkv_weight_grads",
     )(a1, *d, w)
@@ -795,16 +830,17 @@
         out_specs=pl.BlockSpec((1, block, width), lambda i: (slab, i, 0)),
         out_shape=jax.ShapeDtypeStruct((slabs, rows, width), F32),
         input_output_aliases=aliases,
-        compiler_params=params(40),
+        compiler_params=params(60),
         cost_estimate=cost(6 * rows * width * width, rows * width * 16),
         name="qkv_input_grad",
     )(*operands)
 
 
 def bias_kernel(x_ref, near_ref):
-    for delta in range(3):
-        row = jnp.broadcast_to(x_ref[0, delta : delta + 1, :], (TILE, 2 * TILE))
-        near_ref[0, delta] = pltpu.roll(row, 0, 1, stride=1, stride_axis=0)[:, :TILE]
+    for head in range(x_ref.shape[0]):
+        for delta in range(3):
+            row = jnp.broadcast_to(x_ref[head, delta : delta + 1, :], (TILE, 2 * TILE))
+            near_ref[head, delta] = pltpu.roll(row, 0, 1, stride=1, stride_axis=0)[:, :TILE]
 
 
 def bias_tables(rel_bias, tiles):
@@ -816,9 +852,9 @@
     rows = jnp.einsum("bh,bn->hn", rel_bias, onehot.astype(F32), precision=lax.Precision.HIGHEST)
     near = pl.pallas_call(
         bias_kernel,
-        grid=(heads,),
-        in_specs=[pl.BlockSpec((1, 3, 2 * TILE), lambda i: (i, 0, 0))],
-        out_specs=pl.BlockSpec((1, 3, TILE, TILE), lambda i: (i, 0, 0, 0)),
+        grid=(2,),
+        in_specs=[pl.BlockSpec((heads // 2, 3, 2 * TILE), lambda i: (i, 0, 0))],
+        out_specs=pl.BlockSpec((heads // 2, 3, TILE, TILE), lambda i: (i, 0, 0, 0)),
         out_shape=jax.ShapeDtypeStruct((heads, 3, TILE, TILE), F32),
         name="bias_tables",
     )(rows.reshape(heads, 3, 2 * TILE))
@@ -881,19 +917,14 @@
 
 
 def quick_gather(x):
-    rows, columns = x.shape
-    half = columns // 2
-    cut = half // 2 // TILE * TILE
-    low = lax.axis_index("core") == 0
-    pair = both_halves(x, "core")
-    mine = jnp.where(low, pair[..., :half], pair[..., half:])
-    line = ring_gather(mine, "z")
+    columns = x.shape[-1]
+    cut = columns // 2 // TILE * TILE
+    line = ring_gather(x, "z")
     one = both_halves(both_halves(line[..., :cut], "x"), "tower")
     two = both_halves(both_halves(line[..., cut:], "tower"), "x")
     full = jnp.concatenate([one, jnp.swapaxes(two, 0, 1)], axis=-1)
     full = both_halves(full, "core")
-    full = jnp.concatenate([full[0], full[1]], axis=-1)
-    return jnp.swapaxes(full, 1, 2).reshape(-1, columns)
+    return jnp.transpose(full, (1, 3, 2, 0, 4, 5)).reshape(-1, columns)
 
 
 def after(x, *earlier):
@@ -957,9 +988,9 @@
     yield total
 
 
-def sum_everywhere(x):
+def broadcast(x):
     sent = jnp.broadcast_to(x[None], (lax.axis_size(AXES),) + x.shape)
-    return jnp.sum(lax.all_to_all(sent, AXES, 0, 0, tiled=True), axis=0)
+    return lax.all_to_all(sent, AXES, 0, 0, tiled=True)
 
 
 AXES = ("tower", "z", "x", "core")
@@ -1007,19 +1038,16 @@
     w_proj_all = w_all[:, -width:]
 
     near_bias, tags = bias_tables(rel_bias, rows // TILE)
-    a1, qkv, norms = project_qkv(x_all, gain1, wqkv)
-
-    room = jnp.maximum(60.0 - jnp.max(jnp.abs(rel_bias)), 0.0)
-    norms = jnp.max(norms, axis=0)
-    small = jnp.all(norms[0] * norms[1] * 1.05 <= room * room).astype(jnp.int32)
+    room = jnp.maximum(60.0 - jnp.max(jnp.abs(rel_bias)), 0.0).reshape(1, 1)
+    a1, qkv, small = project_qkv(room, x_all, gain1, wqkv)
     lens = lengths[0, 0]
     groups = jnp.arange(rows // GROUP, dtype=jnp.int32)
     per_group = jnp.clip(lens[:, 0:1] - GROUP * groups[None], 0, GROUP)
     glen = jnp.where(is_doc, per_group, lens).astype(jnp.int32)
-    flags = jnp.broadcast_to(jnp.stack([is_doc.astype(jnp.int32), small]), (MICRO, 2))
-    info = jnp.concatenate([flags[:, 0:1], lens[:, 0:1], flags[:, 1:2], glen], axis=1)
+    flag = jnp.broadcast_to(is_doc.astype(jnp.int32), (MICRO, 1))
+    info = jnp.concatenate([flag, lens[:, 0:1], glen], axis=1)
     glen = glen.reshape(-1)
-    mixed, probs, linv = attention(info, qkv, tags, near_bias, heads)
+    mixed, probs, linv = attention(info, small, qkv, tags, near_bias, heads)
     x1, a2, act, slope, x2, out, pool = ffn_forward(
         glen, x_all, mixed, w_all, gain2, gain3
     )
@@ -1032,8 +1060,9 @@
     ).reshape(MICRO, slots, width)
     unit_vec, unit_pull = jax.vjp(unit_norm, projected)
     unit_low = unit_vec.astype(BF)
-    sent = jnp.broadcast_to(unit_low[:, 0].reshape(1, -1, TILE), (devices, MICRO * width // TILE, TILE))
-    docs = lax.all_to_all(sent, AXES, 0, 0, tiled=True)[dp_count:].reshape(-1, MICRO, width)
+    sent = jnp.broadcast_to(unit_low[None, :, 0].astype(F32), (devices, MICRO, width))
+    docs = lax.optimization_barrier(lax.all_to_all(sent, AXES, 0, 0, tiled=True))
+    docs = docs[dp_count:].astype(BF)
     logits = (
         jnp.einsum("msd,bmd->msb", unit_low, docs, preferred_element_type=F32) * logit_scale
     )
@@ -1095,18 +1124,21 @@
         dqkvs.append(dqkv)
         bias_sums.append(sums)
     piece, gain_part = qkv_weight_grads(a1, dqkvs, wqkv, 0, 1)
+    if shard % 8 == 0:
+        piece = after(piece, inner)
+        grad_all = lax.psum_scatter(inner, "z", scatter_dimension=0, tiled=True).astype(F32)
     flow = quick_scatter(piece)
     sent = next(flow)
     ggain1 = jnp.sum(gain_part, axis=1) / gain_attn
     bias_part = bias_grad(bias_sums[0] + bias_sums[1], buckets)
-    smalls = jnp.concatenate(
-        [ggain1, ggains[0], ggains[1], bias_part.reshape(-1), loss_part[None]]
-    )
-    pad = -smalls.shape[0] % (8 * TILE)
-    smalls = jnp.pad(smalls, (0, pad)).reshape(-1, TILE)
-    if shard % 8 == 0:
-        sent = after(sent, inner)
-        grad_all = lax.psum_scatter(inner, "z", scatter_dimension=0, tiled=True).astype(F32)
+    row = lax.broadcasted_iota(jnp.int32, (4, width), 0)
+    lane = lax.broadcasted_iota(jnp.int32, (4, width), 1)
+    used = buckets * heads
+    bias_row = jnp.pad(bias_part.reshape(1, -1), ((0, 0), (0, width - used)))
+    smalls = jnp.where(lane == used, loss_part, bias_row)
+    for at, part in enumerate((ggain1[None], ggains[0:1], ggains[1:2])):
+        smalls = jnp.where(row == at, part, smalls)
+    everywhere = broadcast(smalls)
     input_grads = qkv_input_grad(
         hidden[0, 0], gain1, wqkv, dqkvs[:1], after(backs[0][0], sent), 0, None
     )
@@ -1115,9 +1147,8 @@
         hidden[0, 0], gain1, wqkv, dqkvs[1:], after(backs[1][0], sent), 1, input_grads
     )
     flow.send((input_grads,))
-    totals = sum_everywhere(smalls).reshape(-1)
     flow.send(())
-    grad_qkv = flow.send(()).reshape(shard, 3, width)
+    totals = jnp.sum(everywhere, axis=0)
     grad_in = jnp.concatenate(
         [grad_all[:, 2 * c * width : (2 * c + 1) * width] for c in range(chunks)], axis=1
     )
@@ -1128,10 +1159,11 @@
     grad_wo = grad_all[:, 2 * ff : 2 * ff + width]
     grad_proj = grad_all[:, 2 * ff + width :]
 
+    grad_qkv = flow.send((grad_in,)).reshape(shard, 3, width)
     return (
         out.reshape(hidden.shape),
         input_grads[None, None],
-        totals[3 * width + buckets * heads] / (dp_count * slots * MICRO),
+        totals[3, used] / (dp_count * slots * MICRO),
         grad_qkv[:, 0],
         grad_qkv[:, 1],
         grad_qkv[:, 2],
@@ -1139,10 +1171,10 @@
         grad_in,
         grad_out,
         grad_proj,
-        totals[:width],
-        totals[width : 2 * width],
-        totals[2 * width : 3 * width],
-        totals[3 * width : 3 * width + buckets * heads].reshape(buckets, heads),
+        totals[0],
+        totals[1],
+        totals[2],
+        totals[3, :used].reshape(buckets, heads),
     )
 
 

time: 476 us -> 437 us (0.918)
  starting transfers between devices: 63.2 us -> 32.1 us
  local copies, waits for them, and re-layouts: 50.4 us -> 25 us
  waiting for transfers between devices: 78.4 us -> 88.7 us
  Pallas kernels: 233 us -> 241 us
    all_to_all x2, starting transfers between devices: 37.8 us -> 10.7 us  [the longest x1 7.28 us: broadcast(): return lax.all_to_all(sent, AXES, 0, 0, tiled=True)]
    reduce_scatter x1, waiting for transfers between devices: 0.01 us -> 21.7 us  [per_device(): lax.psum_scatter(grads, ('tower', 'x', 'core'), scatter_dimension=0, tile...]
    unnamed x98 -> x59, local copies, waits for them, and re-layouts: 23.5 us -> 4.3 us
    ppermute x3, waiting for transfers between devices: 18 us -> 1.97 us  [quick_scatter(): lax.ppermute(part, 'z', [(j, (j + k) % count) for j in range(count)])]
    all_to_all x2, waiting for transfers between devices: 8.23 us -> 20.8 us  [the longest x1 13 us: broadcast(): return lax.all_to_all(sent, AXES, 0, 0, tiled=True)]
    pallas_call x2, Pallas kernels: 13.5 us -> 19.8 us  [qkv_input_grad(): pl.pallas_call(kernel, grid=(rows // block,), in_specs=in_specs, out_spec...]
    reduce_scatter x1, waiting for transfers between devices: 6.16 us -> 0.01 us  [per_device(): lax.psum_scatter(inner, 'z', scatter_dimension=0, tiled=True).astype(F32)]
    ppermute x11 -> x10, starting transfers between devices: 11.8 us -> 8.73 us  [swap(): return lax.ppermute(x, axis, [(0, 1), (1, 0)])]
  transfers between devices with their start and end apart: 23 -> 22, of which waited for: 16 -> 13; matrix products, arithmetic and copies ran while one was open for 8% -> 7% of each run, Pallas kernels for 25% -> 29%
where the time goes in v3:
time: 437 us; the launch traced here: 432 us
  Pallas kernels  241 us (55%)
  waiting for transfers between devices  88.7 us (20%)
  starting transfers between devices  32.1 us (7%)
  local copies, waits for them, and re-layouts  25 us (6%)
  other arithmetic  20 us (5%)
  between operations  18.2 us (4%)
  matrix products  7.42 us (2%)
    pallas_call x2, Pallas kernels, ffn_backward(): pl.pallas_call(ffn_bwd_kernel(slab, order), grid_spec=pltpu.PrefetchScala...  74.2 us
    pallas_call x2, Pallas kernels, attention_back(): pl.pallas_call(attn_bwd_kernel, grid_spec=pltpu.PrefetchScalarGridSpec(nu...  49.1 us
    pallas_call x1, Pallas kernels, ffn_forward(): pl.pallas_call(ffn_fwd_kernel, grid_spec=pltpu.PrefetchScalarGridSpec(num...  40.2 us
    pallas_call x1, Pallas kernels, attention(): pl.pallas_call(attn_fwd_kernel, grid_spec=pltpu.PrefetchScalarGridSpec(nu...  25.8 us
    reduce_scatter x1, waiting for transfers between devices, per_device(): lax.psum_scatter(grads, ('tower', 'x', 'core'), scatter_dimension=0, tile...  21.7 us
    ppermute x10, waiting for transfers between devices, swap(): return lax.ppermute(x, axis, [(0, 1), (1, 0)])  19.9 us
    pallas_call x2, Pallas kernels, qkv_input_grad(): pl.pallas_call(kernel, grid=(rows // block,), in_specs=in_specs, out_spec...  19.8 us
    pallas_call x1, Pallas kernels, project_qkv(): pl.pallas_call(qkv_kernel, grid=(rows // block,), in_specs=[pl.BlockSpec(...  15.4 us
  transfers between devices with their start and end apart: 22, of which 13 were waited for; matrix products, arithmetic and copies ran while one was open for 7% of the time, Pallas kernels for 29%

profile of v3, /device:TPU:0, one launch (start us, length us, event | category | flops | bytes accessed | tf_op | source)
XLA Modules:
  0.0 432.1 jit_solution(8848451231448689983)
XLA Ops:
  7.3 2.2 reshape.343
  11.9 3.1 collective-permute-start
  15.0 2.6 collective-permute-start.1
  21.0 3.9 collective-permute-done.1
  29.7 3.3 bias_tables.1.t_ref
  36.8 14.1 %collective-permute-done.6 = bf16[2,4,24,1152]{3,2,1,0:T(8,128)(2,1)S(1)} collective-permute-done((bf16[2,4,24,1152]{3,2,1,0:T(8,128)(2,1)S(1)}, bf16[2,4,24,1152]{3,2,1,0:T(8,128)(2,1)S(1)}, u32[]{:S(2)}, u32[]{:S(2)}) %collective-permute-start.6) | collective-permute-done | bytes 442400 | tf_op jit(solution)/shard_map/ppermute | solution.py:897
  56.6 2.1 pad_maximum_fusion
  58.7 15.4 %norm_qkv.1 = (bf16[2048,768]{1,0:T(8,128)(2,1)}, bf16[2048,2304]{1,0:T(8,128)(2,1)}, s32[1,1]{1,0:T(1,128)}) custom-call(f32[1,1]{1,0:T(1,128)} %bitcast.2.room_ref, bf16[2048,768]{1,0:T(8,128)(2,1)} %bitcast.149, f32[1,768]{1,0:T(1,128)} %broadcast_in_dim.181.gain_ref.refs_1_, bf16[768,2304]{1,0:T(8,128)(2,1)} %bitcast.144), custom_call_target="tpu_custom_call" | custom-call | flops 7247757312 | bytes 15728640 | tf_op jit(solution)/shard_map/norm_qkv/pallas_call | solution.py:92
  74.1 25.8 %attention_forward.1 = (bf16[2048,768]{1,0:T(8,128)(2,1)}, bf16[24,1024,1024]{2,1,0:T(8,128)(2,1)}, f32[12,2,1024]{2,1,0:T(2,128)}) custom-call(s32[2,18]{1,0:T(2,128)} %pad_add_fusion.info_ref, s32[1,1]{1,0:T(1,128)} %get-tuple-element.50.small_ref, bf16[2048,2304]{1,0:T(8,128)(2,1)} %get-tuple-element.51.q_ref.k_ref.v_ref, ...), custom_call_target="tpu_custom_call" | custom-call | flops 12884901888 | bytes 50331648 | tf_op jit(solution)/shard_map/attention_forward/pallas_call | solution.py:259
  99.8 10.0 %all-gather.2.cloned.1.call-done.w_ref.refs_9_ = bf16[768,7680]{1,0:T(8,128)(2,1)} async-done(((bf16[24,7680]{1,0:T(8,128)(2,1)}), bf16[768,7680]{1,0:T(8,128)(2,1)}) %all-gather.2.cloned.1.call-update) | async-done | bytes 11796496 | tf_op jit(solution)/shard_map/all_gather | solution.py:1035
  109.9 40.2 %ffn_forward.1 = (f32[2048,768]{1,0:T(8,128)}, bf16[2048,768]{1,0:T(8,128)(2,1)}, bf16[2048,3072]{1,0:T(8,128)(2,1)}, bf16[2048,3072]{1,0:T(8,128)(2,1)}, f32[20...) custom-call(s32[32]{0:T(128)} %broadcast_select_fusion.2.glen_ref.refs_0_, ...), custom_call_target="tpu_custom_call" | custom-call | flops 21743271936 | bytes 62914560 | tf_op jit(solution)/shard_map/ffn_forward/pallas_call | solution.py:524
  154.5 3.4 all-to-all-start
  158.0 7.8 %all-to-all-done = bf16[32,2,768]{2,1,0:T(2,128)(2,1)S(1)} async-done(((bf16[32,2,768]{2,1,0:T(2,128)(2,1)}), bf16[32,2,768]{2,1,0:T(2,128)(2,1)S(1)}, u32[]{:S(2)}, u32[]{:S(2)}) %all-to-all-start) | async-done | bytes 98336 | tf_op jit(solution)/shard_map/all_to_all | solution.py:1064
  167.6 2.6 all-to-all-start.1
  170.2 8.9 %all-to-all-done.1 = f32[32,2,768]{2,1,0:T(2,128)S(1)} async-done(((f32[32,2,768]{2,1,0:T(2,128)}), f32[32,2,768]{2,1,0:T(2,128)S(1)}, u32[]{:S(2)}, u32[]{:S(2)}) %all-to-all-start.1) | async-done | bytes 196640 | tf_op jit(solution)/shard_map/all_to_all | solution.py:1084
  179.5 2.0 convolution_bitcast_fusion.refs_13_
  181.5 1.7 convolution_divide_fusion
  183.9 36.2 %ffn_backward.2 = (f32[768,7680]{1,0:T(8,128)}, f32[1024,768]{1,0:T(8,128)}, bf16[1024,768]{1,0:T(8,128)(2,1)}, f32[2,768]{1,0:T(2,128)}) custom-call(s32[32]{0:T(128)} %broadcast_select_fusion.2.glen_ref.refs_0_, f32[2048,768]{1,0:T(8,128)} %get-tuple-element.54.refs_1_, bf16[2,1024,768]{2,1,0:T(8,128)(2,1)} %bitcast.155, ...), custom_call_target="tpu_custom_call" | custom-call | flops 21743271936 | bytes 47185920 | tf_op jit(solution)/shard_map/ffn_backward/pallas_call | solution.py:711
  220.1 38.1 %ffn_backward.3 = (bf16[768,7680]{1,0:T(8,128)(2,1)}, f32[1024,768]{1,0:T(8,128)}, bf16[1024,768]{1,0:T(8,128)(2,1)}, f32[2,768]{1,0:T(2,128)}) custom-call(s32[32]{0:T(128)} %broadcast_select_fusion.2.glen_ref.refs_0_, f32[2048,768]{1,0:T(8,128)} %get-tuple-element.54.refs_1_, bf16[2,1024,768]{2,1,0:T(8,128)(2,1)} %bitcast.156, ...), custom_call_target="tpu_custom_call" | custom-call | flops 21743271936 | bytes 47185920 | tf_op jit(solution)/shard_map/ffn_backward/pallas_call | solution.py:711
  260.7 25.1 %attention_backward.2 = (bf16[3,1024,768]{2,1,0:T(8,128)(2,1)}, f32[12,8,256]{2,1,0:T(8,128)}) custom-call(s32[2,18]{1,0:T(2,128)} %pad_add_fusion.info_ref, bf16[2048,2304]{1,0:T(8,128)(2,1)} %get-tuple-element.51.q_ref.k_ref.v_ref, bf16[2048,2304]{1,0:T(8,128)(2,1)} %get-tuple-element.51.q_ref.k_ref.v_ref, ...), custom_call_target="tpu_custom_call" | custom-call | flops 12884901888 | bytes 25165824 | tf_op jit(solution)/shard_map/attention_backward/pallas_call | solution.py:427
  285.8 23.9 %attention_backward.3 = (bf16[3,1024,768]{2,1,0:T(8,128)(2,1)}, f32[12,8,256]{2,1,0:T(8,128)}) custom-call(s32[2,18]{1,0:T(2,128)} %pad_add_fusion.info_ref, bf16[2048,2304]{1,0:T(8,128)(2,1)} %get-tuple-element.51.q_ref.k_ref.v_ref, bf16[2048,2304]{1,0:T(8,128)(2,1)} %get-tuple-element.51.q_ref.k_ref.v_ref, ...), custom_call_target="tpu_custom_call" | custom-call | flops 12884901888 | bytes 25165824 | tf_op jit(solution)/shard_map/attention_backward/pallas_call | solution.py:427
  309.7 13.0 %qkv_weight_grads.1 = (bf16[768,2304]{1,0:T(8,128)(2,1)}, f32[768,128]{1,0:T(8,128)}) custom-call(bf16[2048,768]{1,0:T(8,128)(2,1)} %get-tuple-element.62.a1_ref, bf16[3,1024,768]{2,1,0:T(8,128)(2,1)} %get-tuple-element.66.d0_ref.refs_0_, bf16[3,1024,768]{2,1,0:T(8,128)(2,1)} %get-tuple-element.68.d1_ref.refs_4_, bf16[768,2304]{1,0:T(8,128)(2,1)} %bitcast.145), custom_call_target="tpu_custom_call" | custom-call | flops 7247757312 | bytes 15728640 | tf_op jit(solution)/shard_map/qkv_weight_grads/pallas_call | solution.py:768
  322.7 21.7 %reduce-scatter.3.cloned.1.call-done = bf16[96,7680]{1,0:T(8,128)(2,1)} async-done(((bf16[768,7680]{1,0:T(8,128)(2,1)}), bf16[96,7680]{1,0:T(8,128)(2,1)}) %reduce-scatter.3.cloned.1.call-update) | async-done | bytes 1474576 | tf_op jit(solution)/shard_map/reduce_scatter | solution.py:1120
  344.4 2.3 dynamic-slice_bitcast_fusion.1
  352.6 7.3 %all-to-all-start.2 = ((f32[32,4,768]{2,1,0:T(4,128)}), f32[32,4,768]{2,1,0:T(4,128)}, u32[]{:S(2)}, u32[]{:S(2)}) async-start(f32[32,4,768]{2,1,0:T(4,128)} %broadcast_in_dim.216), calls=%async_computation.3 | async-start | bytes 786432 | tf_op jit(solution)/shard_map/all_to_all | solution.py:993
  360.0 13.0 %all-to-all-done.2 = f32[32,4,768]{2,1,0:T(4,128)} async-done(((f32[32,4,768]{2,1,0:T(4,128)}), f32[32,4,768]{2,1,0:T(4,128)}, u32[]{:S(2)}, u32[]{:S(2)}) %all-to-all-start.2) | async-done | bytes 393248 | tf_op jit(solution)/shard_map/all_to_all | solution.py:993
  374.6 10.0 %qkv_input_grad.2.refs_5_ = f32[2,1024,768]{2,1,0:T(8,128)} custom-call(bf16[2,1024,768]{2,1,0:T(8,128)(2,1)} %bitcast.151, f32[1,768]{1,0:T(1,128)} %broadcast_in_dim.181.gain_ref.refs_1_, bf16[768,2304]{1,0:T(8,128)(2,1)} %bitcast.146, f32[1024,768]{1,0:T(8,128)} %get-tuple-element.73.dx1_ref, bf16[3,1024,768]{2,1,0:T(8,128)(2,1)} %get-tuple-element.66.d0_ref.refs_0_), custom_call_target="tpu_custom_call" | custom-call | flops 3623878656 | bytes 12582912 | tf_op jit(solution)/shard_map/qkv_input_grad/pallas_call | solution.py:826
  384.6 1.9 add_convert_fusion
  389.0 9.7 %qkv_input_grad.3 = f32[2,1024,768]{2,1,0:T(8,128)} custom-call(bf16[2,1024,768]{2,1,0:T(8,128)(2,1)} %bitcast.152, f32[1,768]{1,0:T(1,128)} %broadcast_in_dim.181.gain_ref.refs_1_, bf16[768,2304]{1,0:T(8,128)(2,1)} %bitcast.147, f32[1024,768]{1,0:T(8,128)} %get-tuple-element.75.refs_3_, ...), custom_call_target="tpu_custom_call", output_to_operand_aliasing={{}: (5, {})} | custom-call | flops 3623878656 | bytes 12582912 | tf_op jit(solution)/shard_map/qkv_input_grad/pallas_call | solution.py:826
  403.3 1.9 collective-permute-done.10
  415.4 2.6 reshape.350
  418.0 2.0 collective-permute-done.14
  (204 shorter events, 56.4 us)
Async XLA Ops:
  7.2 4.7 %copy-start.12 = (bf16[24,768]{1,0:T(8,128)(2,1)S(1)}, bf16[24,768]{1,0:T(8,128)(2,1)}, u32[]{:S(2)}) copy-start(bf16[24,768]{1,0:T(8,128)(2,1)} %param.21) | copy-start | bytes 110596
  7.2 11.9 %copy-start.15 = (s32[1,1,2,16]{3,2,1,0:T(2,128)S(1)}, s32[1,1,2,16]{3,2,1,0:T(2,128)}, u32[]{:S(2)}) copy-start(s32[1,1,2,16]{3,2,1,0:T(2,128)} %param.16) | copy-start | bytes 388
  7.3 12.0 %copy-start.5 = (f32[32,12]{0,1:T(8,128)S(1)}, f32[32,12]{0,1:T(8,128)}, u32[]{:S(2)}) copy-start(f32[32,12]{0,1:T(8,128)} %param.29) | copy-start | bytes 4612
  7.3 102.6 %all-gather.2.cloned.1.call-start = ((), (), s32[]{:S(2)}) async-start(), calls=%async_computation.5 | async-start | bytes 12165120 | tf_op jit(solution)/shard_map/all_gather | solution.py:1035
  9.5 18.9 %copy-start.13 = (f32[768]{0:T(1024)S(1)}, f32[768]{0:T(1024)}, u32[]{:S(2)}) copy-start(f32[768]{0:T(1024)} %param.26) | copy-start | bytes 9220
  10.9 22.1 %copy-start.17 = (f32[768]{0:T(1024)S(1)}, f32[768]{0:T(1024)}, u32[]{:S(2)}) copy-start(f32[768]{0:T(1024)} %param.27) | copy-start | bytes 9220
  11.0 22.6 %copy-start.18 = (f32[768]{0:T(1024)S(1)}, f32[768]{0:T(1024)}, u32[]{:S(2)}) copy-start(f32[768]{0:T(1024)} %param.28) | copy-start | bytes 9220
  11.9 9.1 %collective-permute-start = (bf16[24,2304]{1,0:T(8,128)(2,1)S(1)}, bf16[24,2304]{1,0:T(8,128)(2,1)S(1)}, u32[]{:S(2)}, u32[]{:S(2)}) collective-permute-start(bf16[24,2304]{1,0:T(8,128)(2,1)S(1)} %constant_dynamic-update-slice_fusion), channel_id=1, source_target_pairs={{0,4},{4,8},{8,12},{12,0},{1,5},{5,9},{9,13},{13,1},{2,6},{6,10},{... | collective-permute-start | bytes 331784 | tf_op jit(solution)/shard_map/ppermute | solution.py:914
  15.0 9.9 %collective-permute-start.1 = (bf16[24,2304]{1,0:T(8,128)(2,1)S(1)}, bf16[24,2304]{1,0:T(8,128)(2,1)S(1)}, u32[]{:S(2)}, u32[]{:S(2)}) collective-permute-start(bf16[24,2304]{1,0:T(8,128)(2,1)S(1)} %constant_dynamic-update-slice_fusion), channel_id=1, source_target_pairs={{0,8},{4,12},{8,0},{12,4},{1,9},{5,13},{9,1},{13,5},{2,10},{6,14},... | collective-permute-start | bytes 331784 | tf_op jit(solution)/shard_map/ppermute | solution.py:914
  17.6 7.3 %collective-permute-start.2 = (bf16[24,2304]{1,0:T(8,128)(2,1)S(1)}, bf16[24,2304]{1,0:T(8,128)(2,1)S(1)}, u32[]{:S(2)}, u32[]{:S(2)}) collective-permute-start(bf16[24,2304]{1,0:T(8,128)(2,1)S(1)} %constant_dynamic-update-slice_fusion), channel_id=1, source_target_pairs={{0,12},{4,0},{8,4},{12,8},{1,13},{5,1},{9,5},{13,9},{2,14},{6,2},{... | collective-permute-start | bytes 331784 | tf_op jit(solution)/shard_map/ppermute | solution.py:914
  25.0 10.4 %collective-permute-start.3 = (bf16[4,24,1152]{2,1,0:T(8,128)(2,1)S(1)}, bf16[4,24,1152]{2,1,0:T(8,128)(2,1)S(1)}, u32[]{:S(2)}, u32[]{:S(2)}) collective-permute-start(bf16[4,24,1152]{2,1,0:T(8,128)(2,1)S(1)} %get-tuple-element.174), channel_id=1, source_target_pairs={{0,2},{2,0},{1,3},{3,1},{4,6},{6,4},{5,7},{7,5},{8,10},{10,8},{9,1... | collective-permute-start | bytes 663560 | tf_op jit(solution)/shard_map/ppermute | solution.py:897
  26.6 8.8 %collective-permute-start.5 = (bf16[4,24,1152]{2,1,0:T(8,128)(2,1)S(1)}, bf16[4,24,1152]{2,1,0:T(8,128)(2,1)S(1)}, u32[]{:S(2)}, u32[]{:S(2)}) collective-permute-start(bf16[4,24,1152]{2,1,0:T(8,128)(2,1)S(1)} %get-tuple-element.175), channel_id=1, source_target_pairs={{0,16},{16,0},{1,17},{17,1},{2,18},{18,2},{3,19},{19,3},{4,20},{20... | collective-permute-start | bytes 663560 | tf_op jit(solution)/shard_map/ppermute | solution.py:897
  35.6 15.3 %collective-permute-start.6 = (bf16[2,4,24,1152]{3,2,1,0:T(8,128)(2,1)S(1)}, bf16[2,4,24,1152]{3,2,1,0:T(8,128)(2,1)S(1)}, u32[]{:S(2)}, u32[]{:S(2)}) collective-permute-start(bf16[2,4,24,1152]{3,2,1,0:T(8,128)(2,1)S(1)} %pad_maximum_fusion.4), channel_id=1, source_target_pairs={{0,2},{2,0},{1,3},{3,1},{4,6},{6,4},{5,7},{7,5},{8,10},{10,8},{9,1... | collective-permute-start | bytes 1327112 | tf_op jit(solution)/shard_map/ppermute | solution.py:897
  36.3 15.7 %collective-permute-start.4 = (bf16[2,4,24,1152]{3,2,1,0:T(8,128)(2,1)S(1)}, bf16[2,4,24,1152]{3,2,1,0:T(8,128)(2,1)S(1)}, u32[]{:S(2)}, u32[]{:S(2)}) collective-permute-start(bf16[2,4,24,1152]{3,2,1,0:T(8,128)(2,1)S(1)} %pad_maximum_fusion.3), channel_id=1, source_target_pairs={{0,16},{16,0},{1,17},{17,1},{2,18},{18,2},{3,19},{19,3},{4,20},{20... | collective-permute-start | bytes 1327112 | tf_op jit(solution)/shard_map/ppermute | solution.py:897
  52.2 3.8 collective-permute-start.7
  109.9 56.1 %copy-start.16 = (s32[2,1,16]{2,1,0:T(1,128)S(1)}, s32[2,1,16]{2,1,0:T(1,128)}, u32[]{:S(2)}) copy-start(s32[2,1,16]{2,1,0:T(1,128)} %param.17) | copy-start | bytes 388
  154.5 11.2 %all-to-all-start = ((bf16[32,2,768]{2,1,0:T(2,128)(2,1)}), bf16[32,2,768]{2,1,0:T(2,128)(2,1)S(1)}, u32[]{:S(2)}, u32[]{:S(2)}) async-start(bf16[32,2,768]{2,1,0:T(2,128)(2,1)} %broadcast_in_dim.201), calls=%async_computation | async-start | bytes 196608 | tf_op jit(solution)/shard_map/all_to_all | solution.py:1064
  167.6 11.5 %all-to-all-start.1 = ((f32[32,2,768]{2,1,0:T(2,128)}), f32[32,2,768]{2,1,0:T(2,128)S(1)}, u32[]{:S(2)}, u32[]{:S(2)}) async-start(f32[32,2,768]{2,1,0:T(2,128)} %concatenate.35.clone), calls=%async_computation.1 | async-start | bytes 393216 | tf_op jit(solution)/shard_map/all_to_all | solution.py:1084
  170.2 174.2 %reduce-scatter.3.cloned.1.call-start = ((), (), s32[]{:S(2)}) async-start(), calls=%async_computation.6 | async-start | bytes 13271040 | tf_op jit(solution)/shard_map/reduce_scatter | solution.py:1120
  344.4 5.8 %copy-start.14 = (f32[768]{0:T(1024)S(1)}, f32[768]{0:T(1024)}, u32[]{:S(2)}) copy-start(f32[768]{0:T(1024)} %param.26) | copy-start | bytes 9220
  346.7 37.9 %collective-permute-start.8 = (bf16[2,4,2,24,2304]{4,3,2,1,0:T(8,128)(2,1)S(1)}, bf16[2,4,2,24,2304]{4,3,2,1,0:T(8,128)(2,1)}, u32[]{:S(2)}, u32[]{:S(2)}) collective-permute-start(bf16[2,4,2,24,2304]{4,3,2,1,0:T(8,128)(2,1)S(1)} %get-tuple-element.154), channel_id=1, source_target_pairs={{0,1},{1,0},{2,3},{3,2},{4,5},{5,4},{6,7},{7,6},{8,9},{9,8},{10,11... | collective-permute-start | bytes 5308424 | tf_op jit(solution)/shard_map/ppermute | solution.py:897
  352.6 20.4 %all-to-all-start.2 = ((f32[32,4,768]{2,1,0:T(4,128)}), f32[32,4,768]{2,1,0:T(4,128)}, u32[]{:S(2)}, u32[]{:S(2)}) async-start(f32[32,4,768]{2,1,0:T(4,128)} %broadcast_in_dim.216), calls=%async_computation.3 | async-start | bytes 786432 | tf_op jit(solution)/shard_map/all_to_all | solution.py:993
  359.9 51.5 %reduce-scatter.5.cloned.1.call-start = ((), (), s32[]{:S(2)}) async-start(), calls=%async_computation.7 | async-start | bytes 1843200 | tf_op jit(solution)/shard_map/reduce_scatter | solution.py:1129
  386.8 12.0 %collective-permute-start.9 = (bf16[4,2,24,1152]{3,2,0,1:T(8,128)(2,1)S(1)}, bf16[4,2,24,1152]{3,2,0,1:T(8,128)(2,1)S(1)}, u32[]{:S(2)}, u32[]{:S(2)}) collective-permute-start(bf16[4,2,24,1152]{3,2,0,1:T(8,128)(2,1)S(1)} %bitcast.159), channel_id=1, source_target_pairs={{0,16},{16,0},{1,17},{17,1},{2,18},{18,2},{3,19},{19,3},{4,20},{20... | collective-permute-start | bytes 1327112 | tf_op jit(solution)/shard_map/ppermute | solution.py:897
  387.9 12.1 %collective-permute-start.11 = (bf16[2,4,24,1152]{3,2,1,0:T(8,128)(2,1)S(1)}, bf16[2,4,24,1152]{3,2,1,0:T(8,128)(2,1)S(1)}, u32[]{:S(2)}, u32[]{:S(2)}) collective-permute-start(bf16[2,4,24,1152]{3,2,1,0:T(8,128)(2,1)S(1)} %dynamic-slice_bitcast_fusion.2), channel_id=1, source_target_pairs={{0,2},{2,0},{1,3},{3,1},{4,6},{6,4},{5,7},{7,5},{8,10},{10,8},{9,1... | collective-permute-start | bytes 1327112 | tf_op jit(solution)/shard_map/ppermute | solution.py:897
  398.9 6.3 %collective-permute-start.10 = (bf16[4,24,1152]{2,1,0:T(8,128)(2,1)S(1)}, bf16[4,24,1152]{2,1,0:T(8,128)(2,1)S(1)}, u32[]{:S(2)}, u32[]{:S(2)}) collective-permute-start(bf16[4,24,1152]{2,1,0:T(8,128)(2,1)S(1)} %dynamic-slice_bitcast_fusion.4), channel_id=1, source_target_pairs={{0,2},{2,0},{1,3},{3,1},{4,6},{6,4},{5,7},{7,5},{8,10},{10,8},{9,1... | collective-permute-start | bytes 663560 | tf_op jit(solution)/shard_map/ppermute | solution.py:897
  400.1 6.6 %collective-permute-start.12 = (bf16[4,24,1152]{2,1,0:T(8,128)(2,1)S(1)}, bf16[4,24,1152]{2,1,0:T(8,128)(2,1)S(1)}, u32[]{:S(2)}, u32[]{:S(2)}) collective-permute-start(bf16[4,24,1152]{2,1,0:T(8,128)(2,1)S(1)} %dynamic-slice_bitcast_fusion.3), channel_id=1, source_target_pairs={{0,16},{16,0},{1,17},{17,1},{2,18},{18,2},{3,19},{19,3},{4,20},{20... | collective-permute-start | bytes 663560 | tf_op jit(solution)/shard_map/ppermute | solution.py:897
  408.3 9.7 %collective-permute-start.15 = (bf16[24,2304]{1,0:T(8,128)(2,1)}, bf16[24,2304]{1,0:T(8,128)(2,1)}, u32[]{:S(2)}, u32[]{:S(2)}) collective-permute-start(bf16[24,2304]{1,0:T(8,128)(2,1)} %get-tuple-element.171), channel_id=1, source_target_pairs={{0,12},{4,0},{8,4},{12,8},{1,13},{5,1},{9,5},{13,9},{2,14},{6,2},{... | collective-permute-start | bytes 331784 | tf_op jit(solution)/shard_map/ppermute | solution.py:984
  409.3 10.7 %collective-permute-start.14 = (bf16[24,2304]{1,0:T(8,128)(2,1)}, bf16[24,2304]{1,0:T(8,128)(2,1)}, u32[]{:S(2)}, u32[]{:S(2)}) collective-permute-start(bf16[24,2304]{1,0:T(8,128)(2,1)} %get-tuple-element.170), channel_id=1, source_target_pairs={{0,8},{4,12},{8,0},{12,4},{1,9},{5,13},{9,1},{13,5},{2,10},{6,14},... | collective-permute-start | bytes 331784 | tf_op jit(solution)/shard_map/ppermute | solution.py:984
  411.0 9.0 %collective-permute-start.13 = (bf16[24,2304]{1,0:T(8,128)(2,1)}, bf16[24,2304]{1,0:T(8,128)(2,1)}, u32[]{:S(2)}, u32[]{:S(2)}) collective-permute-start(bf16[24,2304]{1,0:T(8,128)(2,1)} %get-tuple-element.169), channel_id=1, source_target_pairs={{0,4},{4,8},{8,12},{12,0},{1,5},{5,9},{9,13},{13,1},{2,6},{6,10},{... | collective-permute-start | bytes 331784 | tf_op jit(solution)/shard_map/ppermute | solution.py:984
  415.4 7.8 %copy-start.2 = (f32[24,768]{1,0:T(8,128)S(1)}, f32[24,768]{1,0:T(8,128)}, u32[]{:S(2)}) copy-start(f32[24,768]{1,0:T(8,128)} %get-tuple-element.179) | copy-start | bytes 221188
  415.4 7.8 %copy-start.3 = (f32[24,768]{1,0:T(8,128)S(1)}, f32[24,768]{1,0:T(8,128)}, u32[]{:S(2)}) copy-start(f32[24,768]{1,0:T(8,128)} %get-tuple-element.180) | copy-start | bytes 221188
  (9 other events, 27.0 us)
Sparse Core Ops, SparseCore 0:
  12.0 97.8 all-gather.1
  258.3 86.0 reduce-scatter.2
  374.7 31.6 reduce-scatter.4

commit v4 on v3

--- a/solution.py
+++ b/solution.py
@@ -333,7 +333,9 @@
         masked = jnp.where(mine, q_ref[...], BF(0))
         return scaled, jnp.concatenate([scaled, extra], axis=1), masked
 
-    @pl.when(info_ref[0, 0] == 1)
+    is_doc = info_ref[0, 0] == 1
+
+    @pl.when(is_doc)
     def _():
         block = lax.broadcasted_iota(jnp.int32, (16, rows), 1) // TILE
         place = lax.broadcasted_iota(jnp.int32, (16, rows), 0)
@@ -388,7 +390,7 @@
         dqkv_ref[1] = dk.astype(BF)
         dqkv_ref[2] = dv.astype(BF)
 
-    @pl.when(info_ref[0, 0] == 0)
+    @pl.when(jnp.logical_not(is_doc))
     def _():
         for head in range(2):
             scaled, outer, masked = prepare(head)
@@ -415,32 +417,30 @@
     dqkv_ref[0] = dqt_scr[...].T.astype(BF)
 
 
-def attention_back(info, qkv, mixed, d_mixed, probs, linv, slab, part, parts):
+def attention_back(info, qkv, mixed, d_mixed, probs, linv):
     slabs = info.shape[0]
     rows = qkv.shape[0] // slabs
     width = qkv.shape[1] // 3
     pairs = linv.shape[0] // slabs
     tiles = rows // TILE
-    count = pairs // parts
-    base = part * count
-    heads = 2 * count
+    heads = 2 * pairs
     return pl.pallas_call(
         attn_bwd_kernel,
         grid_spec=pltpu.PrefetchScalarGridSpec(
             num_scalar_prefetch=1,
-            grid=(count,),
+            grid=(slabs, pairs),
             in_specs=[
-                pl.BlockSpec((rows, TILE), lambda i, _: (slab, base + i)),
-                pl.BlockSpec((rows, TILE), lambda i, _: (slab, pairs + base + i)),
-                pl.BlockSpec((rows, TILE), lambda i, _: (slab, 2 * pairs + base + i)),
-                pl.BlockSpec((rows, TILE), lambda i, _: (slab, base + i)),
-                pl.BlockSpec((rows, TILE), lambda i, _: (0, base + i)),
-                pl.BlockSpec((2, rows, rows), lambda i, _: (slab * pairs + base + i, 0, 0)),
-                pl.BlockSpec((1, 2, rows), lambda i, _: (slab * pairs + base + i, 0, 0)),
+                pl.BlockSpec((rows, TILE), lambda s, i, _: (s, i)),
+                pl.BlockSpec((rows, TILE), lambda s, i, _: (s, pairs + i)),
+                pl.BlockSpec((rows, TILE), lambda s, i, _: (s, 2 * pairs + i)),
+                pl.BlockSpec((rows, TILE), lambda s, i, _: (s, i)),
+                pl.BlockSpec((rows, TILE), lambda s, i, _: (s, i)),
+                pl.BlockSpec((2, rows, rows), lambda s, i, _: (s * pairs + i, 0, 0)),
+                pl.BlockSpec((1, 2, rows), lambda s, i, _: (s * pairs + i, 0, 0)),
             ],
             out_specs=[
-                pl.BlockSpec((3, rows, TILE), lambda i, _: (0, 0, i)),
-                pl.BlockSpec((2, 8, 2 * TILE), lambda i, _: (i, 0, 0)),
+                pl.BlockSpec((3, rows, TILE), lambda s, i, _: (0, s, i)),
+                pl.BlockSpec((2, 8, 2 * TILE), lambda s, i, _: (s * pairs + i, 0, 0)),
             ],
             scratch_shapes=[
                 pltpu.VMEM((2, rows, rows), BF),
@@ -449,11 +449,11 @@
             ],
         ),
         out_shape=[
-            jax.ShapeDtypeStruct((3, rows, count * TILE), BF),
-            jax.ShapeDtypeStruct((heads, 8, 2 * TILE), F32),
+            jax.ShapeDtypeStruct((3, slabs * rows, width), BF),
+            jax.ShapeDtypeStruct((slabs * heads, 8, 2 * TILE), F32),
         ],
         compiler_params=params(60),
-        cost_estimate=cost(heads * rows * rows * 1024, heads * rows * rows * 2),
+        cost_estimate=cost(slabs * heads * rows * rows * 1024, slabs * heads * rows * rows * 2),
         name="attention_backward",
     )(info, qkv, qkv, qkv, mixed, d_mixed, probs, linv)
 
@@ -589,7 +589,7 @@
         rest = refs[12:]
         if second:
             before_ref, gproj_ref = rest[:2]
-            rest = rest[2:]
+            rest = rest[4:]
         (
             g_ref,
             dx1_ref,
@@ -705,9 +705,11 @@
         fixed((1, width)),
     ]
     operands = [x2, cot, dpool, x1, a2, mixed, act, slope, w_all, gain2, gain3]
+    aliases = {}
     if second:
-        in_specs += [part, fixed((width, width))]
-        operands += [before, gproj]
+        in_specs += [part, fixed((width, width))] + [pl.BlockSpec(memory_space=pl.ANY)] * 2
+        aliases = {len(operands) + 3: 1, len(operands) + 4: 2}
+        operands += [before[0], gproj, before[1], before[2]]
     return pl.pallas_call(
         ffn_bwd_kernel(slab, order),
         grid_spec=pltpu.PrefetchScalarGridSpec(
@@ -716,8 +718,8 @@
             in_specs=in_specs,
             out_specs=[
                 part,
-                fixed((rows, width)),
-                fixed((rows, width)),
+                mine,
+                mine,
                 fixed((2, width)),
             ],
             scratch_shapes=[
@@ -733,19 +735,20 @@
         ),
         out_shape=[
             jax.ShapeDtypeStruct(w_all.shape, BF if second else F32),
-            jax.ShapeDtypeStruct((rows, width), F32),
-            jax.ShapeDtypeStruct((rows, width), BF),
+            jax.ShapeDtypeStruct(x2.shape, F32),
+            jax.ShapeDtypeStruct(x2.shape, BF),
             jax.ShapeDtypeStruct((2, width), F32),
         ],
+        input_output_aliases=aliases,
         compiler_params=params(60),
         cost_estimate=cost(4 * rows * width * (width + 2 * ff), rows * width * 60),
         name="ffn_backward",
     )(glen, *operands)
 
 
-def qkv_weight_kernel(a1_ref, d0_ref, d1_ref, w_ref, g_ref, gain_ref):
-    rows, cols = d0_ref.shape[1:]
-    total = mm(a1_ref[0:rows, :], d0_ref[0], TN) + mm(a1_ref[rows:, :], d1_ref[0], TN)
+def qkv_weight_kernel(a1_ref, d_ref, w_ref, g_ref, gain_ref):
+    cols = d_ref.shape[2]
+    total = mm(a1_ref[...], d_ref[0], TN)
     g_ref[...] = total.astype(BF)
     prod = total * w_ref[...].astype(F32)
     part = prod[:, 0:TILE]
@@ -761,59 +764,55 @@
         gain_ref[...] = gain_ref[...] + part
 
 
-def qkv_weight_grads(a1, d, w, part, parts):
+def qkv_weight_grads(a1, d, w):
     rows, width = a1.shape
-    cols = width // parts
-    one = pl.BlockSpec((1, rows // 2, cols), lambda i: (i, 0, 0))
+    col = pl.BlockSpec((width, width), lambda i: (0, i))
     return pl.pallas_call(
         qkv_weight_kernel,
         grid=(3,),
         in_specs=[
             fixed((rows, width)),
-            one,
-            one,
-            pl.BlockSpec((width, cols), lambda i: (0, parts * i + part)),
+            pl.BlockSpec((1, rows, width), lambda i: (i, 0, 0)),
+            col,
         ],
-        out_specs=[pl.BlockSpec((width, cols), lambda i: (0, i)), fixed((width, TILE))],
+        out_specs=[col, fixed((width, TILE))],
         out_shape=[
-            jax.ShapeDtypeStruct((width, 3 * cols), BF),
+            jax.ShapeDtypeStruct((width, 3 * width), BF),
             jax.ShapeDtypeStruct((width, TILE), F32),
         ],
         compiler_params=params(60),
-        cost_estimate=cost(6 * rows * width * cols, rows * width * 10),
+        cost_estimate=cost(6 * rows * width * width, rows * width * 10),
         name="qkv_weight_grads",
-    )(a1, *d, w)
-
-
-def qkv_input_kernel(x_ref, gain_ref, w_ref, dx1_ref, *refs):
-    out_ref, parts = refs[-1], refs[:-1]
+    )(a1, d, w)
+
+
+def qkv_input_kernel(x_ref, gain_ref, w_ref, dx1_ref, d_ref, out_ref):
     width = x_ref.shape[1]
-    grad = None
-    for i in range(3):
-        for part, d_ref in enumerate(parts):
-            cols = d_ref.shape[2]
-            at = i * width + part * cols
-            term = mm(d_ref[i], w_ref[:, at : at + cols], NT)
-            grad = term if grad is None else grad + term
+    grad = mm(d_ref[0], w_ref[:, 0:width], NT)
+    for i in (1, 2):
+        grad = grad + mm(d_ref[i], w_ref[:, i * width : (i + 1) * width], NT)
     x = x_ref[...].astype(F32)
     r = lax.rsqrt(jnp.mean(x * x, axis=-1, keepdims=True) + 1e-06)
     hat = x * r
     d_hat = grad * gain_ref[...]
     dx = r * (d_hat - hat * jnp.mean(d_hat * hat, axis=-1, keepdims=True))
-    out_ref[0] = dx + dx1_ref[...]
+    out_ref[...] = dx + dx1_ref[...]
 
 
 def qkv_input_grad(x, gain, w, d, dx1, slab, before):
-    slabs, rows, width = x.shape
+    rows, width = x.shape
     block = 256
-    spec = pl.BlockSpec((block, width), lambda i: (i, 0))
+    steps = rows // MICRO // block
+    first = slab * steps
+    spec = pl.BlockSpec((block, width), lambda i: (first + i, 0))
     in_specs = [
-        pl.BlockSpec((None, block, width), lambda i: (slab, i, 0)),
+        spec,
         fixed((1, width)),
         fixed(w.shape),
         spec,
-    ] + [pl.BlockSpec((3, block, part.shape[2]), lambda i: (0, i, 0)) for part in d]
-    operands = [x, gain, w, dx1, *d]
+        pl.BlockSpec((3, block, width), lambda i: (0, first + i, 0)),
+    ]
+    operands = [x, gain, w, dx1, d]
     kernel, aliases = qkv_input_kernel, {}
     if before is not None:
         aliases = {len(operands): 0}
@@ -825,13 +824,13 @@
 
     return pl.pallas_call(
         kernel,
-        grid=(rows // block,),
+        grid=(steps,),
         in_specs=in_specs,
-        out_specs=pl.BlockSpec((1, block, width), lambda i: (slab, i, 0)),
-        out_shape=jax.ShapeDtypeStruct((slabs, rows, width), F32),
+        out_specs=spec,
+        out_shape=jax.ShapeDtypeStruct((rows, width), F32),
         input_output_aliases=aliases,
         compiler_params=params(60),
-        cost_estimate=cost(6 * rows * width * width, rows * width * 16),
+        cost_estimate=cost(6 * rows * width * width // MICRO, rows * width * 8),
         name="qkv_input_grad",
     )(*operands)
 
@@ -1091,9 +1090,9 @@
     dpool = jnp.where(is_doc, jnp.broadcast_to(dpooled[:, 0:1], dpooled.shape), dpooled)
 
     order = scatter_order(shard)
-    grads, ggains, backs = None, 0.0, []
+    backs, ggains = None, 0.0
     for m in range(MICRO):
-        grads, dx1, d_mixed, ggain = ffn_backward(
+        *backs, ggain = ffn_backward(
             m,
             order,
             glen,
@@ -1108,29 +1107,26 @@
             w_all,
             gain2,
             gain3,
-            grads,
+            backs,
             grad_proj,
         )
-        backs.append((dx1, d_mixed))
         ggains = ggains + ggain
+    grads, dx1, d_mixed = backs
 
     if shard % 8:
         grad_all = lax.psum_scatter(grads, AXES, scatter_dimension=0, tiled=True).astype(F32)
     else:
         inner = lax.psum_scatter(grads, ("tower", "x", "core"), scatter_dimension=0, tiled=True)
-    dqkvs, bias_sums = [], []
-    for m in range(MICRO):
-        dqkv, sums = attention_back(info, qkv, mixed, backs[m][1], probs, linv, m, 0, 1)
-        dqkvs.append(dqkv)
-        bias_sums.append(sums)
-    piece, gain_part = qkv_weight_grads(a1, dqkvs, wqkv, 0, 1)
+    dqkv, bias_sums = attention_back(info, qkv, mixed, d_mixed, probs, linv)
+    bias_sums = jnp.sum(bias_sums.reshape((MICRO, heads) + bias_sums.shape[1:]), axis=0)
+    bias_part = bias_grad(bias_sums, buckets)
+    piece, gain_part = qkv_weight_grads(a1, after(dqkv, bias_part), wqkv)
     if shard % 8 == 0:
         piece = after(piece, inner)
         grad_all = lax.psum_scatter(inner, "z", scatter_dimension=0, tiled=True).astype(F32)
     flow = quick_scatter(piece)
     sent = next(flow)
     ggain1 = jnp.sum(gain_part, axis=1) / gain_attn
-    bias_part = bias_grad(bias_sums[0] + bias_sums[1], buckets)
     row = lax.broadcasted_iota(jnp.int32, (4, width), 0)
     lane = lax.broadcasted_iota(jnp.int32, (4, width), 1)
     used = buckets * heads
@@ -1139,16 +1135,12 @@
     for at, part in enumerate((ggain1[None], ggains[0:1], ggains[1:2])):
         smalls = jnp.where(row == at, part, smalls)
     everywhere = broadcast(smalls)
-    input_grads = qkv_input_grad(
-        hidden[0, 0], gain1, wqkv, dqkvs[:1], after(backs[0][0], sent), 0, None
-    )
+    totals = jnp.sum(everywhere, axis=0)
+    sent = flow.send((totals,))
+    input_grads = qkv_input_grad(x_all, gain1, wqkv, dqkv, after(dx1, sent), 0, None)
     sent = flow.send((input_grads,))
-    input_grads = qkv_input_grad(
-        hidden[0, 0], gain1, wqkv, dqkvs[1:], after(backs[1][0], sent), 1, input_grads
-    )
+    input_grads = qkv_input_grad(x_all, gain1, wqkv, dqkv, after(dx1, *sent), 1, input_grads)
     flow.send((input_grads,))
-    flow.send(())
-    totals = jnp.sum(everywhere, axis=0)
     grad_in = jnp.concatenate(
         [grad_all[:, 2 * c * width : (2 * c + 1) * width] for c in range(chunks)], axis=1
     )
@@ -1162,7 +1154,7 @@
     grad_qkv = flow.send((grad_in,)).reshape(shard, 3, width)
     return (
         out.reshape(hidden.shape),
-        input_grads[None, None],
+        input_grads.reshape(hidden.shape),
         totals[3, used] / (dp_count * slots * MICRO),
         grad_qkv[:, 0],
         grad_qkv[:, 1],

time: 437 us -> 444 us (1.016)
  waiting for transfers between devices: 88.7 us -> 98.2 us
    reduce_scatter x1, waiting for transfers between devices: 0.01 us -> 10.8 us  [per_device(): lax.psum_scatter(inner, 'z', scatter_dimension=0, tiled=True).astype(F32)]
    pallas_call x2 -> x1, Pallas kernels: 49.1 us -> 45.7 us  [attention_back(): pl.pallas_call(attn_bwd_kernel, grid_spec=pltpu.PrefetchScalarGridSpec(nu...]
  transfers between devices with their start and end apart: 22 -> 22, of which waited for: 13 -> 12; matrix products, arithmetic and copies ran while one was open for 7% -> 7% of each run, Pallas kernels for 29% -> 28%
where the time goes in v4:
time: 444 us; the launch traced here: 439 us
  Pallas kernels  237 us (53%)
  waiting for transfers between devices  98.2 us (22%)
  starting transfers between devices  29.3 us (7%)
  local copies, waits for them, and re-layouts  27.7 us (6%)
  other arithmetic  21.7 us (5%)
  between operations  18 us (4%)
  matrix products  7.06 us (2%)
    pallas_call x2, Pallas kernels, ffn_backward(): pl.pallas_call(ffn_bwd_kernel(slab, order), grid_spec=pltpu.PrefetchScala...  74.1 us
    pallas_call x1, Pallas kernels, attention_back(): pl.pallas_call(attn_bwd_kernel, grid_spec=pltpu.PrefetchScalarGridSpec(nu...  45.7 us
    pallas_call x1, Pallas kernels, ffn_forward(): pl.pallas_call(ffn_fwd_kernel, grid_spec=pltpu.PrefetchScalarGridSpec(num...  40.2 us
    pallas_call x1, Pallas kernels, attention(): pl.pallas_call(attn_fwd_kernel, grid_spec=pltpu.PrefetchScalarGridSpec(nu...  25.8 us
    reduce_scatter x1, waiting for transfers between devices, per_device(): lax.psum_scatter(grads, ('tower', 'x', 'core'), scatter_dimension=0, tile...  25.6 us
    pallas_call x2, Pallas kernels, qkv_input_grad(): pl.pallas_call(kernel, grid=(steps,), in_specs=in_specs, out_specs=spec,...  19.7 us
    ppermute x10, waiting for transfers between devices, swap(): return lax.ppermute(x, axis, [(0, 1), (1, 0)])  16.6 us
    pallas_call x1, Pallas kernels, project_qkv(): pl.pallas_call(qkv_kernel, grid=(rows // block,), in_specs=[pl.BlockSpec(...  15.3 us
  transfers between devices with their start and end apart: 22, of which 12 were waited for; matrix products, arithmetic and copies ran while one was open for 7% of the time, Pallas kernels for 28%

profile of v4, /device:TPU:0, one launch (start us, length us, event | category | flops | bytes accessed | tf_op | source)
XLA Modules:
  0.0 438.7 jit_solution(14407084937632281059)
XLA Ops:
  7.3 2.2 reshape.351
  11.9 3.1 collective-permute-start
  15.0 2.6 collective-permute-start.1
  21.0 3.9 collective-permute-done.1
  29.7 3.3 bias_tables.1.t_ref
  36.8 14.1 %collective-permute-done.6 = bf16[2,4,24,1152]{3,2,1,0:T(8,128)(2,1)S(1)} collective-permute-done((bf16[2,4,24,1152]{3,2,1,0:T(8,128)(2,1)S(1)}, bf16[2,4,24,1152]{3,2,1,0:T(8,128)(2,1)S(1)}, u32[]{:S(2)}, u32[]{:S(2)}) %collective-permute-start.6) | collective-permute-done | bytes 442400 | tf_op jit(solution)/shard_map/ppermute | solution.py:896
  56.6 2.2 pad_maximum_fusion
  58.8 15.3 %norm_qkv.1 = (bf16[2048,768]{1,0:T(8,128)(2,1)}, bf16[2048,2304]{1,0:T(8,128)(2,1)}, s32[1,1]{1,0:T(1,128)}) custom-call(f32[1,1]{1,0:T(1,128)} %bitcast.2.room_ref, bf16[2048,768]{1,0:T(8,128)(2,1)} %bitcast.147, f32[1,768]{1,0:T(1,128)} %broadcast_in_dim.178.gain_ref.refs_1_, bf16[768,2304]{1,0:T(8,128)(2,1)} %bitcast.142), custom_call_target="tpu_custom_call" | custom-call | flops 7247757312 | bytes 15728640 | tf_op jit(solution)/shard_map/norm_qkv/pallas_call | solution.py:92
  74.1 25.8 %attention_forward.1 = (bf16[2048,768]{1,0:T(8,128)(2,1)}, bf16[24,1024,1024]{2,1,0:T(8,128)(2,1)}, f32[12,2,1024]{2,1,0:T(2,128)}) custom-call(s32[2,18]{1,0:T(2,128)} %pad_add_fusion.info_ref, s32[1,1]{1,0:T(1,128)} %get-tuple-element.51.small_ref, bf16[2048,2304]{1,0:T(8,128)(2,1)} %get-tuple-element.52.q_ref.k_ref.v_ref, ...), custom_call_target="tpu_custom_call" | custom-call | flops 12884901888 | bytes 50331648 | tf_op jit(solution)/shard_map/attention_forward/pallas_call | solution.py:259
  99.8 10.0 %all-gather.2.cloned.1.call-done.w_ref.refs_9_ = bf16[768,7680]{1,0:T(8,128)(2,1)} async-done(((bf16[24,7680]{1,0:T(8,128)(2,1)}), bf16[768,7680]{1,0:T(8,128)(2,1)}) %all-gather.2.cloned.1.call-update) | async-done | bytes 11796496 | tf_op jit(solution)/shard_map/all_gather | solution.py:1034
  109.8 40.2 %ffn_forward.1 = (f32[2048,768]{1,0:T(8,128)}, bf16[2048,768]{1,0:T(8,128)(2,1)}, bf16[2048,3072]{1,0:T(8,128)(2,1)}, bf16[2048,3072]{1,0:T(8,128)(2,1)}, f32[20...) custom-call(s32[32]{0:T(128)} %broadcast_select_fusion.2.glen_ref.refs_0_, ...), custom_call_target="tpu_custom_call" | custom-call | flops 21743271936 | bytes 62914560 | tf_op jit(solution)/shard_map/ffn_forward/pallas_call | solution.py:524
  152.0 1.7 multiply_reduce_fusion.1
  154.5 3.5 all-to-all-start
  158.0 7.8 %all-to-all-done = bf16[32,2,768]{2,1,0:T(2,128)(2,1)S(1)} async-done(((bf16[32,2,768]{2,1,0:T(2,128)(2,1)}), bf16[32,2,768]{2,1,0:T(2,128)(2,1)S(1)}, u32[]{:S(2)}, u32[]{:S(2)}) %all-to-all-start) | async-done | bytes 98336 | tf_op jit(solution)/shard_map/all_to_all | solution.py:1063
  167.6 2.6 all-to-all-start.1
  170.2 8.9 %all-to-all-done.1 = f32[32,2,768]{2,1,0:T(2,128)S(1)} async-done(((f32[32,2,768]{2,1,0:T(2,128)}), f32[32,2,768]{2,1,0:T(2,128)S(1)}, u32[]{:S(2)}, u32[]{:S(2)}) %all-to-all-start.1) | async-done | bytes 196640 | tf_op jit(solution)/shard_map/all_to_all | solution.py:1083
  179.5 1.9 convolution_bitcast_fusion.refs_13_
  181.4 1.7 convolution_divide_fusion
  183.8 36.1 %ffn_backward.2 = (f32[768,7680]{1,0:T(8,128)}, f32[2048,768]{1,0:T(8,128)}, bf16[2048,768]{1,0:T(8,128)(2,1)}, f32[2,768]{1,0:T(2,128)}) custom-call(s32[32]{0:T(128)} %broadcast_select_fusion.2.glen_ref.refs_0_, f32[2048,768]{1,0:T(8,128)} %get-tuple-element.55.refs_1_, bf16[2,1024,768]{2,1,0:T(8,128)(2,1)} %bitcast.153, ...), custom_call_target="tpu_custom_call" | custom-call | flops 21743271936 | bytes 47185920 | tf_op jit(solution)/shard_map/ffn_backward/pallas_call | solution.py:713
  219.9 38.0 %ffn_backward.3 = (bf16[768,7680]{1,0:T(8,128)(2,1)}, f32[2048,768]{1,0:T(8,128)}, bf16[2048,768]{1,0:T(8,128)(2,1)}, f32[2,768]{1,0:T(2,128)}) custom-call(s32[32]{0:T(128)} %broadcast_select_fusion.2.glen_ref.refs_0_, f32[2048,768]{1,0:T(8,128)} %get-tuple-element.55.refs_1_, ...), custom_call_target="tpu_custom_call", output_to_operand_aliasing={{1}: (14, {}), {2}: (15, {})} | custom-call | flops 21743271936 | bytes 47185920 | tf_op jit(solution)/shard_map/ffn_backward/pallas_call | solution.py:713
  258.2 45.7 %attention_backward.1 = (bf16[3,2048,768]{2,1,0:T(8,128)(2,1)}, f32[24,8,256]{2,1,0:T(8,128)}) custom-call(s32[2,18]{1,0:T(2,128)} %pad_add_fusion.info_ref, bf16[2048,2304]{1,0:T(8,128)(2,1)} %get-tuple-element.52.q_ref.k_ref.v_ref, bf16[2048,2304]{1,0:T(8,128)(2,1)} %get-tuple-element.52.q_ref.k_ref.v_ref, ...), custom_call_target="tpu_custom_call" | custom-call | flops 25769803776 | bytes 50331648 | tf_op jit(solution)/shard_map/attention_backward/pallas_call | solution.py:427
  306.0 12.6 %qkv_weight_grads.1 = (bf16[768,2304]{1,0:T(8,128)(2,1)}, f32[768,128]{1,0:T(8,128)}) custom-call(bf16[2048,768]{1,0:T(8,128)(2,1)} %get-tuple-element.65.a1_ref, bf16[3,2048,768]{2,1,0:T(8,128)(2,1)} %get-tuple-element.71.d_ref.refs_4_, bf16[768,2304]{1,0:T(8,128)(2,1)} %bitcast.143), custom_call_target="tpu_custom_call" | custom-call | flops 7247757312 | bytes 15728640 | tf_op jit(solution)/shard_map/qkv_weight_grads/pallas_call | solution.py:770
  318.6 25.6 %reduce-scatter.3.cloned.1.call-done = bf16[96,7680]{1,0:T(8,128)(2,1)} async-done(((bf16[768,7680]{1,0:T(8,128)(2,1)}), bf16[96,7680]{1,0:T(8,128)(2,1)}) %reduce-scatter.3.cloned.1.call-update) | async-done | bytes 1474576 | tf_op jit(solution)/shard_map/reduce_scatter | solution.py:1119
  344.2 2.3 constant_dynamic-slice_fusion.1
  355.3 4.8 %all-to-all-start.2 = ((f32[32,4,768]{2,1,0:T(4,128)}), f32[32,4,768]{2,1,0:T(4,128)}, u32[]{:S(2)}, u32[]{:S(2)}) async-start(f32[32,4,768]{2,1,0:T(4,128)} %broadcast_in_dim.212), calls=%async_computation.3 | async-start | bytes 786432 | tf_op jit(solution)/shard_map/all_to_all | solution.py:992
  360.2 13.0 %all-to-all-done.2 = f32[32,4,768]{2,1,0:T(4,128)} async-done(((f32[32,4,768]{2,1,0:T(4,128)}), f32[32,4,768]{2,1,0:T(4,128)}, u32[]{:S(2)}, u32[]{:S(2)}) %all-to-all-start.2) | async-done | bytes 393248 | tf_op jit(solution)/shard_map/all_to_all | solution.py:992
  377.6 1.9 fusion
  382.6 10.0 %qkv_input_grad.2.refs_5_ = f32[2048,768]{1,0:T(8,128)} custom-call(bf16[2048,768]{1,0:T(8,128)(2,1)} %bitcast.149, f32[1,768]{1,0:T(1,128)} %broadcast_in_dim.178.gain_ref.refs_1_, bf16[768,2304]{1,0:T(8,128)(2,1)} %bitcast.144, f32[2048,768]{1,0:T(8,128)} %get-tuple-element.82.dx1_ref.refs_3_, bf16[3,2048,768]{2,1,0:T(8,128)(2,1)} %get-tuple-element.71.d_ref.refs_4_), custom_call_target="tpu_custom_call" | custom-call | flops 3623878656 | bytes 12582912 | tf_op jit(solution)/shard_map/qkv_input_grad/pallas_call | solution.py:825
  395.1 9.8 %qkv_input_grad.3 = f32[2048,768]{1,0:T(8,128)} custom-call(bf16[2048,768]{1,0:T(8,128)(2,1)} %bitcast.150, f32[1,768]{1,0:T(1,128)} %broadcast_in_dim.178.gain_ref.refs_1_, bf16[768,2304]{1,0:T(8,128)(2,1)} %bitcast.145, f32[2048,768]{1,0:T(8,128)} %get-tuple-element.82.dx1_ref.refs_3_, ...), custom_call_target="tpu_custom_call", output_to_operand_aliasing={{}: (5, {})} | custom-call | flops 3623878656 | bytes 12582912 | tf_op jit(solution)/shard_map/qkv_input_grad/pallas_call | solution.py:825
  406.4 2.1 collective-permute-start.15
  409.2 10.8 %reduce-scatter.5.cloned.1.call-done = bf16[24,7680]{1,0:T(8,128)(2,1)} async-done(((bf16[96,7680]{1,0:T(8,128)(2,1)}), bf16[24,7680]{1,0:T(8,128)(2,1)}) %reduce-scatter.5.cloned.1.call-update) | async-done | bytes 368656 | tf_op jit(solution)/shard_map/reduce_scatter | solution.py:1126
  424.2 2.6 reshape.360
  (202 shorter events, 54.9 us)
Async XLA Ops:
  7.2 4.7 %copy-start.11 = (bf16[24,768]{1,0:T(8,128)(2,1)S(1)}, bf16[24,768]{1,0:T(8,128)(2,1)}, u32[]{:S(2)}) copy-start(bf16[24,768]{1,0:T(8,128)(2,1)} %param.20) | copy-start | bytes 110596
  7.2 4.7 %copy-start.12 = (bf16[24,768]{1,0:T(8,128)(2,1)S(1)}, bf16[24,768]{1,0:T(8,128)(2,1)}, u32[]{:S(2)}) copy-start(bf16[24,768]{1,0:T(8,128)(2,1)} %param.21) | copy-start | bytes 110596
  7.2 11.9 %copy-start.14 = (s32[1,1,2,16]{3,2,1,0:T(2,128)S(1)}, s32[1,1,2,16]{3,2,1,0:T(2,128)}, u32[]{:S(2)}) copy-start(s32[1,1,2,16]{3,2,1,0:T(2,128)} %param.16) | copy-start | bytes 388
  7.3 12.0 %copy-start.5 = (f32[32,12]{0,1:T(8,128)S(1)}, f32[32,12]{0,1:T(8,128)}, u32[]{:S(2)}) copy-start(f32[32,12]{0,1:T(8,128)} %param.29) | copy-start | bytes 4612
  7.3 102.6 %all-gather.2.cloned.1.call-start = ((), (), s32[]{:S(2)}) async-start(), calls=%async_computation.5 | async-start | bytes 12165120 | tf_op jit(solution)/shard_map/all_gather | solution.py:1034
  9.5 18.9 %copy-start.13 = (f32[768]{0:T(1024)S(1)}, f32[768]{0:T(1024)}, u32[]{:S(2)}) copy-start(f32[768]{0:T(1024)} %param.26) | copy-start | bytes 9220
  10.9 22.0 %copy-start.16 = (f32[768]{0:T(1024)S(1)}, f32[768]{0:T(1024)}, u32[]{:S(2)}) copy-start(f32[768]{0:T(1024)} %param.27) | copy-start | bytes 9220
  11.0 22.6 %copy-start.17 = (f32[768]{0:T(1024)S(1)}, f32[768]{0:T(1024)}, u32[]{:S(2)}) copy-start(f32[768]{0:T(1024)} %param.28) | copy-start | bytes 9220
  11.9 9.1 %collective-permute-start = (bf16[24,2304]{1,0:T(8,128)(2,1)S(1)}, bf16[24,2304]{1,0:T(8,128)(2,1)S(1)}, u32[]{:S(2)}, u32[]{:S(2)}) collective-permute-start(bf16[24,2304]{1,0:T(8,128)(2,1)S(1)} %constant_dynamic-update-slice_fusion), channel_id=1, source_target_pairs={{0,4},{4,8},{8,12},{12,0},{1,5},{5,9},{9,13},{13,1},{2,6},{6,10},{... | collective-permute-start | bytes 331784 | tf_op jit(solution)/shard_map/ppermute | solution.py:913
  15.0 9.9 %collective-permute-start.1 = (bf16[24,2304]{1,0:T(8,128)(2,1)S(1)}, bf16[24,2304]{1,0:T(8,128)(2,1)S(1)}, u32[]{:S(2)}, u32[]{:S(2)}) collective-permute-start(bf16[24,2304]{1,0:T(8,128)(2,1)S(1)} %constant_dynamic-update-slice_fusion), channel_id=1, source_target_pairs={{0,8},{4,12},{8,0},{12,4},{1,9},{5,13},{9,1},{13,5},{2,10},{6,14},... | collective-permute-start | bytes 331784 | tf_op jit(solution)/shard_map/ppermute | solution.py:913
  17.6 7.3 %collective-permute-start.2 = (bf16[24,2304]{1,0:T(8,128)(2,1)S(1)}, bf16[24,2304]{1,0:T(8,128)(2,1)S(1)}, u32[]{:S(2)}, u32[]{:S(2)}) collective-permute-start(bf16[24,2304]{1,0:T(8,128)(2,1)S(1)} %constant_dynamic-update-slice_fusion), channel_id=1, source_target_pairs={{0,12},{4,0},{8,4},{12,8},{1,13},{5,1},{9,5},{13,9},{2,14},{6,2},{... | collective-permute-start | bytes 331784 | tf_op jit(solution)/shard_map/ppermute | solution.py:913
  25.0 10.4 %collective-permute-start.3 = (bf16[4,24,1152]{2,1,0:T(8,128)(2,1)S(1)}, bf16[4,24,1152]{2,1,0:T(8,128)(2,1)S(1)}, u32[]{:S(2)}, u32[]{:S(2)}) collective-permute-start(bf16[4,24,1152]{2,1,0:T(8,128)(2,1)S(1)} %get-tuple-element.174), channel_id=1, source_target_pairs={{0,2},{2,0},{1,3},{3,1},{4,6},{6,4},{5,7},{7,5},{8,10},{10,8},{9,1... | collective-permute-start | bytes 663560 | tf_op jit(solution)/shard_map/ppermute | solution.py:896
  26.6 8.8 %collective-permute-start.5 = (bf16[4,24,1152]{2,1,0:T(8,128)(2,1)S(1)}, bf16[4,24,1152]{2,1,0:T(8,128)(2,1)S(1)}, u32[]{:S(2)}, u32[]{:S(2)}) collective-permute-start(bf16[4,24,1152]{2,1,0:T(8,128)(2,1)S(1)} %get-tuple-element.175), channel_id=1, source_target_pairs={{0,16},{16,0},{1,17},{17,1},{2,18},{18,2},{3,19},{19,3},{4,20},{20... | collective-permute-start | bytes 663560 | tf_op jit(solution)/shard_map/ppermute | solution.py:896
  35.6 15.3 %collective-permute-start.6 = (bf16[2,4,24,1152]{3,2,1,0:T(8,128)(2,1)S(1)}, bf16[2,4,24,1152]{3,2,1,0:T(8,128)(2,1)S(1)}, u32[]{:S(2)}, u32[]{:S(2)}) collective-permute-start(bf16[2,4,24,1152]{3,2,1,0:T(8,128)(2,1)S(1)} %pad_maximum_fusion.4), channel_id=1, source_target_pairs={{0,2},{2,0},{1,3},{3,1},{4,6},{6,4},{5,7},{7,5},{8,10},{10,8},{9,1... | collective-permute-start | bytes 1327112 | tf_op jit(solution)/shard_map/ppermute | solution.py:896
  36.2 15.7 %collective-permute-start.4 = (bf16[2,4,24,1152]{3,2,1,0:T(8,128)(2,1)S(1)}, bf16[2,4,24,1152]{3,2,1,0:T(8,128)(2,1)S(1)}, u32[]{:S(2)}, u32[]{:S(2)}) collective-permute-start(bf16[2,4,24,1152]{3,2,1,0:T(8,128)(2,1)S(1)} %pad_maximum_fusion.3), channel_id=1, source_target_pairs={{0,16},{16,0},{1,17},{17,1},{2,18},{18,2},{3,19},{19,3},{4,20},{20... | collective-permute-start | bytes 1327112 | tf_op jit(solution)/shard_map/ppermute | solution.py:896
  52.2 3.8 collective-permute-start.7
  109.8 56.1 %copy-start.15 = (s32[2,1,16]{2,1,0:T(1,128)S(1)}, s32[2,1,16]{2,1,0:T(1,128)}, u32[]{:S(2)}) copy-start(s32[2,1,16]{2,1,0:T(1,128)} %param.17) | copy-start | bytes 388
  154.5 11.3 %all-to-all-start = ((bf16[32,2,768]{2,1,0:T(2,128)(2,1)}), bf16[32,2,768]{2,1,0:T(2,128)(2,1)S(1)}, u32[]{:S(2)}, u32[]{:S(2)}) async-start(bf16[32,2,768]{2,1,0:T(2,128)(2,1)} %broadcast_in_dim.198), calls=%async_computation | async-start | bytes 196608 | tf_op jit(solution)/shard_map/all_to_all | solution.py:1063
  167.6 11.5 %all-to-all-start.1 = ((f32[32,2,768]{2,1,0:T(2,128)}), f32[32,2,768]{2,1,0:T(2,128)S(1)}, u32[]{:S(2)}, u32[]{:S(2)}) async-start(f32[32,2,768]{2,1,0:T(2,128)} %concatenate.35.clone), calls=%async_computation.1 | async-start | bytes 393216 | tf_op jit(solution)/shard_map/all_to_all | solution.py:1083
  170.1 174.1 %reduce-scatter.3.cloned.1.call-start = ((), (), s32[]{:S(2)}) async-start(), calls=%async_computation.6 | async-start | bytes 13271040 | tf_op jit(solution)/shard_map/reduce_scatter | solution.py:1119
  346.6 31.0 %collective-permute-start.8 = (bf16[2,4,2,24,2304]{4,3,1,0,2:T(8,128)(2,1)S(1)}, bf16[2,4,2,24,2304]{4,3,1,0,2:T(8,128)(2,1)}, u32[]{:S(2)}, u32[]{:S(2)}) collective-permute-start(bf16[2,4,2,24,2304]{4,3,1,0,2:T(8,128)(2,1)S(1)} %bitcast.156), channel_id=1, source_target_pairs={{0,1},{1,0},{2,3},{3,2},{4,5},{5,4},{6,7},{7,6},{8,9},{9,8},{10,11... | collective-permute-start | bytes 5308424 | tf_op jit(solution)/shard_map/ppermute | solution.py:896
  355.3 17.9 %all-to-all-start.2 = ((f32[32,4,768]{2,1,0:T(4,128)}), f32[32,4,768]{2,1,0:T(4,128)}, u32[]{:S(2)}, u32[]{:S(2)}) async-start(f32[32,4,768]{2,1,0:T(4,128)} %broadcast_in_dim.212), calls=%async_computation.3 | async-start | bytes 786432 | tf_op jit(solution)/shard_map/all_to_all | solution.py:992
  360.1 59.9 %reduce-scatter.5.cloned.1.call-start = ((), (), s32[]{:S(2)}) async-start(), calls=%async_computation.7 | async-start | bytes 1843200 | tf_op jit(solution)/shard_map/reduce_scatter | solution.py:1126
  379.7 12.8 %collective-permute-start.9 = (bf16[4,2,24,1152]{3,2,0,1:T(8,128)(2,1)S(1)}, bf16[4,2,24,1152]{3,2,0,1:T(8,128)(2,1)S(1)}, u32[]{:S(2)}, u32[]{:S(2)}) collective-permute-start(bf16[4,2,24,1152]{3,2,0,1:T(8,128)(2,1)S(1)} %dynamic-slice_bitcast_fusion.1), channel_id=1, source_target_pairs={{0,16},{16,0},{1,17},{17,1},{2,18},{18,2},{3,19},{19,3},{4,20},{20... | collective-permute-start | bytes 1327112 | tf_op jit(solution)/shard_map/ppermute | solution.py:896
  380.8 12.0 %collective-permute-start.10 = (bf16[2,4,24,1152]{3,2,1,0:T(8,128)(2,1)S(1)}, bf16[2,4,24,1152]{3,2,1,0:T(8,128)(2,1)S(1)}, u32[]{:S(2)}, u32[]{:S(2)}) collective-permute-start(bf16[2,4,24,1152]{3,2,1,0:T(8,128)(2,1)S(1)} %dynamic-slice_bitcast_fusion), channel_id=1, source_target_pairs={{0,2},{2,0},{1,3},{3,1},{4,6},{6,4},{5,7},{7,5},{8,10},{10,8},{9,1... | collective-permute-start | bytes 1327112 | tf_op jit(solution)/shard_map/ppermute | solution.py:896
  393.1 11.8 %collective-permute-start.11 = (bf16[4,24,1152]{2,1,0:T(8,128)(2,1)S(1)}, bf16[4,24,1152]{2,1,0:T(8,128)(2,1)S(1)}, u32[]{:S(2)}, u32[]{:S(2)}) collective-permute-start(bf16[4,24,1152]{2,1,0:T(8,128)(2,1)S(1)} %dynamic-slice_bitcast_fusion.3), channel_id=1, source_target_pairs={{0,2},{2,0},{1,3},{3,1},{4,6},{6,4},{5,7},{7,5},{8,10},{10,8},{9,1... | collective-permute-start | bytes 663560 | tf_op jit(solution)/shard_map/ppermute | solution.py:896
  394.0 10.8 %collective-permute-start.12 = (bf16[4,24,1152]{2,1,0:T(8,128)(2,1)S(1)}, bf16[4,24,1152]{2,1,0:T(8,128)(2,1)S(1)}, u32[]{:S(2)}, u32[]{:S(2)}) collective-permute-start(bf16[4,24,1152]{2,1,0:T(8,128)(2,1)S(1)} %dynamic-slice_bitcast_fusion.2), channel_id=1, source_target_pairs={{0,16},{16,0},{1,17},{17,1},{2,18},{18,2},{3,19},{19,3},{4,20},{20... | collective-permute-start | bytes 663560 | tf_op jit(solution)/shard_map/ppermute | solution.py:896
  406.4 20.3 %collective-permute-start.15 = (bf16[24,2304]{1,0:T(8,128)(2,1)}, bf16[24,2304]{1,0:T(8,128)(2,1)}, u32[]{:S(2)}, u32[]{:S(2)}) collective-permute-start(bf16[24,2304]{1,0:T(8,128)(2,1)} %get-tuple-element.171), channel_id=1, source_target_pairs={{0,12},{4,0},{8,4},{12,8},{1,13},{5,1},{9,5},{13,9},{2,14},{6,2},{... | collective-permute-start | bytes 331784 | tf_op jit(solution)/shard_map/ppermute | solution.py:983
  408.5 18.3 %collective-permute-start.14 = (bf16[24,2304]{1,0:T(8,128)(2,1)}, bf16[24,2304]{1,0:T(8,128)(2,1)}, u32[]{:S(2)}, u32[]{:S(2)}) collective-permute-start(bf16[24,2304]{1,0:T(8,128)(2,1)} %get-tuple-element.170), channel_id=1, source_target_pairs={{0,8},{4,12},{8,0},{12,4},{1,9},{5,13},{9,1},{13,5},{2,10},{6,14},... | collective-permute-start | bytes 331784 | tf_op jit(solution)/shard_map/ppermute | solution.py:983
  408.8 17.9 %collective-permute-start.13 = (bf16[24,2304]{1,0:T(8,128)(2,1)}, bf16[24,2304]{1,0:T(8,128)(2,1)}, u32[]{:S(2)}, u32[]{:S(2)}) collective-permute-start(bf16[24,2304]{1,0:T(8,128)(2,1)} %get-tuple-element.169), channel_id=1, source_target_pairs={{0,4},{4,8},{8,12},{12,0},{1,5},{5,9},{9,13},{13,1},{2,6},{6,10},{... | collective-permute-start | bytes 331784 | tf_op jit(solution)/shard_map/ppermute | solution.py:983
  424.1 5.9 %copy-start.2 = (f32[24,768]{1,0:T(8,128)S(1)}, f32[24,768]{1,0:T(8,128)}, u32[]{:S(2)}) copy-start(f32[24,768]{1,0:T(8,128)} %get-tuple-element.179) | copy-start | bytes 221188
  424.2 5.9 %copy-start.3 = (f32[24,768]{1,0:T(8,128)S(1)}, f32[24,768]{1,0:T(8,128)}, u32[]{:S(2)}) copy-start(f32[24,768]{1,0:T(8,128)} %get-tuple-element.180) | copy-start | bytes 221188
  (8 other events, 20.6 us)
Sparse Core Ops, SparseCore 0:
  12.0 97.7 all-gather.1
  258.1 86.0 reduce-scatter.2
  382.7 37.3 reduce-scatter.4
